TPU v7x, 256 devices: a whole 4x4x8 slice. The times are simulated.
256 devices in a mesh: tile: 64 (over y, x_hi, z), day: 4 (over x_lo, core).
Axes of the slice: x: 4 (x_hi: 2, x_lo: 2; x = x_hi * 2 + x_lo), y: 4, z: 8, core: 2. Of those that a mesh axis runs over, the one named last changes fastest.
Arguments:
- source_spectra: bfloat16 [16, 64, 2, 1024], P('day', 'tile'), may hold values from -6 to 6
- receiver_spectra: bfloat16 [16, 1024, 2, 1024], P('day', 'tile'), may hold values from -6 to 6
- valid_pairs: int32 [16, 64, 1024], P('day', None, 'tile'), may hold values 0 or 1
Outputs:
- mean_day_stack: float32 [64, 1024, 401], P(None, 'tile')
- phase_weighted: float32 [64, 1024, 401], P(None, 'tile')
All inputs are finite; a program needn't handle non-finite values. No bound on the sum of `valid_pairs` on one device may be relied on, other than what follows from the above.
Results may differ from a plain program's by a relative error of at most 0.0055.
Values may be sent and summed in bfloat16 or wider, within the bound.
No kernel may reach another device: no remote copies, remote signals or barrier semaphores. Data moves between devices by JAX's collectives and lax.ppermute only.
A program may use at most 128 MiB of HBM per device.

v0:
```python
import math

import jax
import jax.numpy as jnp
from jax import lax
from jax.sharding import PartitionSpec as P

MAXLAG = 200


def lag_basis_table(frequency_count, max_lag):
    samples = 2 * frequency_count
    freq_index = jnp.arange(frequency_count, dtype=jnp.int32)
    lag_index = jnp.arange(2 * max_lag + 1, dtype=jnp.int32) - max_lag
    phase_turns = jnp.mod(freq_index[:, None] * lag_index[None, :], samples).astype(jnp.float32)
    angles = phase_turns * (2.0 * math.pi / samples)
    weight = jnp.where(freq_index == 0, 0.5, 1.0).astype(jnp.float32)[
        :, None
    ] * frequency_count ** (-0.5)
    cosine = weight * jnp.cos(angles)
    sine = weight * jnp.sin(angles)
    upper_half = jnp.concatenate([cosine, sine], axis=1)
    negative_lag_half = jnp.concatenate([-sine, cosine], axis=1)
    return jnp.concatenate([upper_half, negative_lag_half], axis=0).astype(jnp.bfloat16)


def pair_stacks(sources, receivers, weights, lag_fourier_matrix):
    source_real = sources[:, :, 0].astype(jnp.float32)[:, :, None, :]
    source_imag = sources[:, :, 1].astype(jnp.float32)[:, :, None, :]
    receiver_real = receivers[:, :, 0].astype(jnp.float32)[:, None, :, :]
    receiver_imag = receivers[:, :, 1].astype(jnp.float32)[:, None, :, :]
    cross_real = source_real * receiver_real + source_imag * receiver_imag
    cross_imag = source_real * receiver_imag - source_imag * receiver_real
    cross_spectrum = jnp.concatenate([cross_real, cross_imag], axis=-1).astype(jnp.bfloat16)
    analytic_signal = jnp.einsum(
        "dkrf,fl->dkrl", cross_spectrum, lag_fourier_matrix, preferred_element_type=jnp.float32
    )
    lag_count = lag_fourier_matrix.shape[1] // 2
    real_part = analytic_signal[..., :lag_count]
    imag_part = analytic_signal[..., lag_count:]
    inverse_norm = lax.rsqrt(real_part * real_part + imag_part * imag_part + 0.0625)
    mask_lags = weights[:, :, :, None]
    linear = jnp.sum(mask_lags * real_part, axis=0)
    phase_real = jnp.sum(mask_lags * real_part * inverse_norm, axis=0)
    phase_imag = jnp.sum(mask_lags * imag_part * inverse_norm, axis=0)
    return jnp.stack([linear, phase_real, phase_imag], axis=1)


def finish_stacks(running_totals, counts):
    divisor = jnp.maximum(counts, 1.0)[:, :, None]
    linear = running_totals[:, 0] / divisor
    coherence = (
        running_totals[:, 1] * running_totals[:, 1] + running_totals[:, 2] * running_totals[:, 2]
    ) / (divisor * divisor)
    return (linear, linear * coherence)


def on_device(source_spectra, receiver_spectra, valid_pairs):
    lag_fourier_matrix = lag_basis_table(source_spectra.shape[3], MAXLAG)
    mask_float = valid_pairs.astype(jnp.float32)
    day_terms = pair_stacks(
        lax.all_gather(source_spectra, "tile", axis=1, tiled=True),
        receiver_spectra,
        mask_float,
        lag_fourier_matrix,
    )
    counts = jnp.sum(mask_float, axis=0)
    running_totals, all_counts = lax.psum((day_terms, counts), "day")
    linear, weighted = finish_stacks(running_totals, all_counts)
    return (linear, weighted)


def solution(mesh):
    in_specs = (P("day", "tile", None, None), P("day", "tile", None, None), P("day", None, "tile"))
    out_specs = (P(None, "tile", None), P(None, "tile", None))
    return jax.shard_map(
        on_device, mesh=mesh, in_specs=in_specs, out_specs=out_specs, check_vma=False
    )
```

profile of v0, /device:TPU:1, one launch (start us, length us, event | category | flops | bytes accessed | tf_op | source)
XLA Modules:
  0.0 315.0 jit_solution(17966853545975398731)
XLA Ops:
  7.2 0.0 all-gather.2.cloned.1.call-start
  7.2 1.3 copy.11
  8.5 0.0 all-gather.2.cloned.1.call-update
  8.6 0.0 all-reduce.2.cloned.1.call-start
  8.6 0.8 convert_element_type.38
  9.4 0.1 copy.10
  9.5 1.5 fusion.31
  11.0 0.1 fusion.25
  11.1 7.9 %fusion.22 = (bf16[1024,401]{0,1:T(8,128)(2,1)S(1)}, bf16[1024,401]{0,1:T(8,128)(2,1)}, bf16[1024,401]{0,1:T(8,128)(2,1)}) fusion(s32[401]{0:T(512)S(1)} %iota_add_fusion, f32[1024]{0:T(1024)S(1)} %select_multiply_fusion), kind=kLoop, calls=%fused_computation.39 | loop fusion | flops 8212480 | bytes 2469444 | tf_op jit(solution)/shard_map/convert.9
  19.0 106.3 %all-gather.2.cloned.1.call-done = bf16[4,64,2,1024]{3,0,2,1:T(4,128)(2,1)} async-done(((bf16[4,1,2,1024]{3,0,2,1:T(4,128)(2,1)}), bf16[4,64,2,1024]{3,0,2,1:T(4,128)(2,1)}) %all-gather.2.cloned.1.call-update) | async-done | bytes 1048592 | tf_op jit(solution)/shard_map/all_gather | solution.py:62
  125.3 1.6 fusion.30
  126.9 0.4 fusion.23
  127.3 7.0 %add_convert_fusion = (bf16[4,64,16,1024]{3,2,1,0:T(8,128)(2,1)S(1)}, bf16[4,64,16,1024]{3,2,1,0:T(8,128)(2,1)}) fusion(f32[4,16,1024]{2,1,0:T(8,128)S(1)} %get-tuple-element.18, f32[4,64,1024]{2,1,0:T(8,128)S(1)} %get-tuple-element.20, f32[4,16,1024]{2,1,0:T(8,128)S(1)} %get-tuple-element.19, f32[4,64,1024]{2,1,0:T(8,128)S(1)} %get-tuple-element.21), kind=kLoop, calls=%fused_computation.5 | loop fusion | flops 33554432 | bytes 19398656 | tf_op jit(solution)/shard_map/convert.10
  134.2 25.0 %fusion = f32[4,64,16,802]{3,2,1,0:T(8,128)} fusion(bf16[4,64,16,1024]{3,2,1,0:T(8,128)(2,1)} %get-tuple-element.8, bf16[4,64,16,1024]{3,2,1,0:T(8,128)(2,1)S(1)} %get-tuple-element.7, bf16[1024,401]{0,1:T(8,128)(2,1)} %get-tuple-element.17, bf16[1024,401]{0,1:T(8,128)(2,1)} %get-tuple-element.16, bf16[1024,401]{0,1:T(8,128)(2,1)S(1)} %get-tuple-element.15), kind=kOutput, calls=%fused_computation | convolution fusion | flops 13502021632 | bytes 32380928 | tf_op jit(solution)/shard_map/dkrf,fl->dkrl/dot_general | solution.py:35
  159.3 8.6 %fusion.4 = (f32[64,16,401]{2,1,0:T(8,128)S(1)}, f32[64,16,401]{2,1,0:T(8,128)S(1)}, f32[64,16,401]{2,1,0:T(8,128)S(1)}) fusion(f32[4,64,16,802]{3,2,1,0:T(8,128)} %fusion, f32[4,64,16]{2,1,0:T(8,128)S(1)} %copy.10), kind=kLoop, calls=%fused_computation.10 | loop fusion | flops 16835584 | bytes 18083840 | tf_op jit(solution)/shard_map/reduce_sum | solution.py:43
  167.9 3.5 %pad_maximum_fusion = f32[64,3,16,401]{3,2,0,1:T(8,128)} fusion(f32[64,1,16,401]{3,2,0,1:T(8,128)S(1)} %bitcast.40, f32[64,1,16,401]{3,2,0,1:T(8,128)S(1)} %bitcast.41, f32[64,1,16,401]{3,2,0,1:T(8,128)S(1)} %bitcast.39), kind=kLoop, calls=%fused_computation.11 | loop fusion | flops 2463744 | bytes 9854976 | tf_op jit(solution)/shard_map/stack | solution.py:46
  171.3 0.0 copy-start
  171.3 0.0 all-reduce.2.cloned.1.call-update
  171.4 0.7 copy-done
  172.1 10.1 %psum.15 = f32[64,16]{0,1:T(8,128)S(1)} all-reduce(f32[64,16]{0,1:T(8,128)S(1)} %convert_reduce_fusion), channel_id=1, replica_groups=mesh['tile'=64,'day'=4] {'day'}, use_global_device_ids=true, to_apply=%region_5.6 | all-reduce | flops 1024 | bytes 8192 | tf_op jit(solution)/shard_map/psum | solution.py:68
  182.2 0.1 copy.16
  182.3 0.1 copy.17
  182.4 121.4 %all-reduce.2.cloned.1.call-done = f32[64,3,16,401]{3,2,0,1:T(8,128)} async-done(((f32[64,3,16,401]{3,2,0,1:T(8,128)}), f32[64,3,16,401]{3,2,0,1:T(8,128)}) %all-reduce.2.cloned.1.call-update) | async-done | bytes 4927504 | tf_op jit(solution)/shard_map/psum | solution.py:68
  303.8 4.4 %fusion.14 = (f32[64,16,401]{2,1,0:T(8,128)}, f32[64,16,401]{2,1,0:T(8,128)}) fusion(f32[64,3,16,401]{3,2,0,1:T(8,128)} %all-reduce.2.cloned.1.call-done, f32[64,16]{1,0:T(8,128)S(1)} %copy.17, f32[64,16]{1,0:T(8,128)S(1)} %copy.16), kind=kLoop, calls=%fused_computation.26 | loop fusion | flops 2463744 | bytes 8220672 | tf_op jit(solution)/shard_map/mul | solution.py:55
  (4 shorter events, 0.0 us)
Async XLA Ops:
  7.2 118.2 %all-gather.2.cloned.1.call-start = ((), (), s32[]{:S(2)}) async-start(), calls=%async_computation | async-start | bytes 1064960 | tf_op jit(solution)/shard_map/all_gather | solution.py:62
  8.6 295.2 %all-reduce.2.cloned.1.call-start = ((), (), s32[]{:S(2)}) async-start(), calls=%async_computation.1 | async-start | bytes 12582912 | tf_op jit(solution)/shard_map/psum | solution.py:68
  171.3 0.8 copy-start
Sparse Core Ops, SparseCore 0:
  11.6 113.6 all-gather.1
  171.5 132.2 all-reduce.1
where the time goes:
time: 315 us
  waiting for transfers between devices  228 us (72%)
  other arithmetic  32.6 us (10%)
  matrix products  25 us (8%)
  between operations  14.1 us (4%)
  blocking collectives  10.1 us (3%)
  local copies, waits for them, and re-layouts  5.37 us (2%)
    psum x1, waiting for transfers between devices, on_device(): running_totals, all_counts = lax.psum((day_terms, counts), 'day')  121 us
    all_gather x1, waiting for transfers between devices, on_device(): lax.all_gather(source_spectra, 'tile', axis=1, tiled=True)  106 us
    dot_general x1, matrix products, pair_stacks(): jnp.einsum('dkrf,fl->dkrl', cross_spectrum, lag_fourier_matrix, preferred...  25 us
    another operation x2, other arithmetic  14.9 us
    psum x1, blocking collectives, on_device(): running_totals, all_counts = lax.psum((day_terms, counts), 'day')  10.1 us
    reduce_sum x1, other arithmetic, pair_stacks(): linear = jnp.sum(mask_lags * real_part, axis=0)  8.59 us
  transfers between devices with their start and end apart: 2, of which 2 were waited for; matrix products, arithmetic and copies ran while one was open for 3% of the time, Pallas kernels for 0%

commit v1 on v0

v1 whole, which is shorter than its diff:
```python
import math

import jax
import jax.numpy as jnp
import numpy as np
from jax import lax
from jax.experimental import pallas as pl
from jax.experimental.pallas import tpu as pltpu
from jax.sharding import PartitionSpec as P

MAXLAG = 200
HALF = 256
TILES, DAYS = 64, 4
PER = 4


def half_basis(frequency_count):
    samples = 2 * frequency_count
    freq = np.arange(frequency_count)[:, None]
    lag = np.arange(MAXLAG + 1)[None, :]
    angles = ((freq * lag) % samples) * (2.0 * math.pi / samples)
    weight = np.where(freq == 0, 0.5, 1.0) * frequency_count ** (-0.5)
    table = np.zeros((frequency_count, 2 * HALF))
    table[:, : MAXLAG + 1] = weight * np.cos(angles)
    table[:, HALF : HALF + MAXLAG + 1] = weight * np.sin(angles)
    return jnp.asarray(table, jnp.bfloat16)


def lag_order():
    table = np.zeros((2 * HALF, 2 * HALF))
    lag = np.arange(MAXLAG + 1)
    table[lag, MAXLAG + lag] = 1.0
    table[HALF + lag[1:], MAXLAG - lag[1:]] = 1.0
    return jnp.asarray(table, jnp.bfloat16)


def stack_kernel(shift_ref, src_ref, rec0, rec1, rec2, rec3, mask_ref, basis_ref, out_ref,
                 rec_f32, src_f32, lhs_r, lhs_i, res_r, res_i, done):
    shift = shift_ref[0]
    for j, rec in enumerate((rec0, rec1, rec2, rec3)):
        rec_f32[pl.ds((j ^ shift) * PER, PER)] = rec[...].astype(jnp.float32)
    for s in range(PER):
        src_f32[s] = src_ref[s].astype(jnp.float32)
    width = basis_ref.shape[0]
    for s in range(PER):
        p = s % 2
        for d in range(4 * PER):
            rows = slice(d * 16, d * 16 + 16)
            for lane in range(0, width, 256):
                cols = slice(lane, lane + 256)
                a = src_f32[s, 2 * d : 2 * d + 1, cols]
                b = src_f32[s, 2 * d + 1 : 2 * d + 2, cols]
                c = rec_f32[d, 0, :, cols]
                e = rec_f32[d, 1, :, cols]
                lhs_r[p, rows, cols] = (a * c + b * e).astype(jnp.bfloat16)
                lhs_i[p, rows, cols] = (a * e - b * c).astype(jnp.bfloat16)
        res_r[p] = jnp.dot(lhs_r[p], basis_ref[...], preferred_element_type=jnp.float32)
        res_i[p] = jnp.dot(lhs_i[p], basis_ref[...], preferred_element_type=jnp.float32)
        for h in range(0, 16, 8):
            zero = jnp.zeros((8, 128), jnp.float32)
            sums = [[zero] * 6 for _ in range(2)]
            count = zero
            for d in range(4 * PER):
                rows = slice(d * 16 + h, d * 16 + h + 8)
                col = s * 4 * PER + d
                m = jnp.broadcast_to(mask_ref[h : h + 8, col : col + 1], (8, 128))
                count = count + m
                for i in range(2):
                    lo = slice(i * 128, i * 128 + 128)
                    hi = slice(HALF + i * 128, HALF + i * 128 + 128)
                    rc, rs = res_r[p, rows, lo], res_r[p, rows, hi]
                    ic, is_ = res_i[p, rows, lo], res_i[p, rows, hi]
                    for sign, (u, v) in enumerate(((rc - is_, ic + rs), (rc + is_, ic - rs))):
                        w = m * lax.rsqrt(u * u + v * v + 0.0625)
                        acc = sums[i]
                        acc[3 * sign] = acc[3 * sign] + m * u
                        acc[3 * sign + 1] = acc[3 * sign + 1] + w * u
                        acc[3 * sign + 2] = acc[3 * sign + 2] + w * v
            inverse = 1.0 / jnp.maximum(count, 1.0)
            for i in range(2):
                for sign in range(2):
                    linear, real, imag = sums[i][3 * sign : 3 * sign + 3]
                    mean = linear * inverse
                    cols = slice(sign * HALF + i * 128, sign * HALF + i * 128 + 128)
                    done[0, h : h + 8, cols] = mean
                    done[1, h : h + 8, cols] = mean * ((real * real + imag * imag) * (inverse * inverse))
        out_ref[0, s] = done[0].astype(jnp.bfloat16)
        out_ref[1, s] = done[1].astype(jnp.bfloat16)


def stack_group(shift, sources, receivers, mask, basis):
    width = sources.shape[-1]
    whole = pl.BlockSpec(memory_space=pltpu.VMEM)
    rows = 4 * PER * 16
    return pl.pallas_call(
        stack_kernel,
        out_shape=jax.ShapeDtypeStruct((2, PER, 16, 2 * HALF), jnp.bfloat16),
        in_specs=[pl.BlockSpec(memory_space=pltpu.SMEM)] + [whole] * 7,
        out_specs=whole,
        scratch_shapes=[
            pltpu.VMEM((4 * PER, 2, 16, width), jnp.float32),
            pltpu.VMEM((PER, 8 * PER, width), jnp.float32),
            pltpu.VMEM((2, rows, width), jnp.bfloat16),
            pltpu.VMEM((2, rows, width), jnp.bfloat16),
            pltpu.VMEM((2, rows, 2 * HALF), jnp.float32),
            pltpu.VMEM((2, rows, 2 * HALF), jnp.float32),
            pltpu.VMEM((2, 16, 2 * HALF), jnp.float32),
        ],
        compiler_params=pltpu.CompilerParams(vmem_limit_bytes=32 * 2**20),
        cost_estimate=pl.CostEstimate(
            flops=2 * 2 * PER * rows * width * 2 * HALF, bytes_accessed=3 * 2**20, transcendentals=0
        ),
        name="stack_group",
    )(shift, sources, *receivers, mask, basis)


def order_kernel(where_ref, order_ref, *refs):
    parts, (mean_ref, weighted_ref) = refs[:16], refs[16:]
    y, xh, z0, day = (where_ref[i] for i in range(4))
    for k3 in range(4):
        for j in range(4):
            part = parts[4 * k3 + j][...].reshape(2 * PER * 16, 2 * HALF)
            full = jnp.dot(part, order_ref[...], preferred_element_type=jnp.float32)
            for k2 in range(PER):
                source = ((y ^ k3) << 4) | ((xh ^ (k2 >> 1)) << 3) | ((day ^ j) << 1) | (z0 ^ (k2 & 1))
                mean_ref[source] = full[k2 * 16 : k2 * 16 + 16, : 2 * MAXLAG + 1]
                low = (PER + k2) * 16
                weighted_ref[source] = full[low : low + 16, : 2 * MAXLAG + 1]


def order_outputs(where, parts):
    whole = pl.BlockSpec(memory_space=pltpu.VMEM)
    shape = jax.ShapeDtypeStruct((TILES, 16, 2 * MAXLAG + 1), jnp.float32)
    return pl.pallas_call(
        order_kernel,
        out_shape=(shape, shape),
        in_specs=[pl.BlockSpec(memory_space=pltpu.SMEM)] + [whole] * 17,
        out_specs=(whole, whole),
        compiler_params=pltpu.CompilerParams(vmem_limit_bytes=32 * 2**20),
        name="order_outputs",
    )(where, lag_order(), *parts)


def flip_bits(x, axis, amount, bits):
    shape = x.shape
    for bit in range(bits):
        step = 1 << bit
        view = x.reshape(shape[:axis] + (shape[axis] // (2 * step), 2, step) + shape[axis + 1 :])
        view = jnp.where((amount >> bit) & 1 == 1, jnp.flip(view, axis + 1), view)
        x = view.reshape(shape)
    return x


def day_swap(x, k):
    return lax.ppermute(x, "day", [(i, i ^ k) for i in range(DAYS)])


def tile_swap(x, k):
    return lax.ppermute(x, "tile", [(i, i ^ k) for i in range(TILES)])


def turn(x, k):
    pairs = []
    for t in range(TILES):
        for d in range(DAYS):
            to = (t & ~6) | ((d ^ k) << 1)
            pairs.append((t * DAYS + d, to * DAYS + ((t >> 1) & 3)))
    return lax.ppermute(x, ("tile", "day"), pairs)


def on_device(source_spectra, receiver_spectra, valid_pairs):
    width = source_spectra.shape[3]
    tile, day = lax.axis_index("tile"), lax.axis_index("day")
    y, xh, low, z0 = tile >> 4, (tile >> 3) & 1, (tile >> 1) & 3, tile & 1
    shift = low ^ day

    own = source_spectra.reshape(8, width)
    first = jnp.concatenate([turn(own, k) for k in range(4)], axis=0)

    rec0 = jnp.transpose(receiver_spectra, (0, 2, 1, 3))
    rec2 = day_swap(rec0, 2)
    rec1 = day_swap(rec0, 1)
    rec3 = day_swap(rec2, 1)

    m0 = valid_pairs.astype(jnp.bfloat16).reshape(32, 128)
    m2 = day_swap(m0, 2)
    m1 = day_swap(m0, 1)
    m3 = day_swap(m2, 1)
    masks = jnp.stack([m0, m1, m2, m3]).reshape(4, 4, 4, 2, 4, 2, 16)
    masks = lax.dynamic_index_in_dim(masks, day, axis=4, keepdims=False)
    masks = flip_bits(masks, 0, shift, 2)
    masks = flip_bits(masks, 2, y, 2)
    masks = flip_bits(masks, 3, xh, 1)
    masks = flip_bits(masks, 4, z0, 1)
    masks = jnp.transpose(masks, (2, 5, 3, 4, 0, 1)).reshape(4, 16, 64).astype(jnp.float32)
    masks = jnp.pad(masks, ((0, 0), (0, 0), (0, 64)))

    second = jnp.stack([first] + [tile_swap(first, k) for k in (1, 8, 9)])
    groups = [second] + [tile_swap(second, 16 * k) for k in (1, 2, 3)]

    basis = half_basis(width)
    shift_arg = shift.reshape(1).astype(jnp.int32)
    parts = []
    for k3 in range(4):
        mine = stack_group(shift_arg, groups[k3], (rec0, rec1, rec2, rec3), masks[k3], basis)
        across = day_swap(mine, 2)
        parts += [mine, day_swap(mine, 1), across, day_swap(across, 1)]
    where = jnp.stack([y, xh, z0, day]).astype(jnp.int32)
    return order_outputs(where, parts)


def solution(mesh):
    in_specs = (P("day", "tile", None, None), P("day", "tile", None, None), P("day", None, "tile"))
    out_specs = (P(None, "tile", None), P(None, "tile", None))
    return jax.shard_map(
        on_device, mesh=mesh, in_specs=in_specs, out_specs=out_specs, check_vma=False
    )
```

time: 315 us -> 71.9 us (0.23)
  waiting for transfers between devices: 228 us -> 9.01 us
  starting transfers between devices: 0.08 us -> 39.7 us
  other arithmetic: 32.6 us -> 0.58 us
  matrix products: 25 us -> 0 us
  Pallas kernels: 0 us -> 18 us
  between operations: 14.1 us -> 0.9 us
  blocking collectives: 10.1 us -> 0 us
    psum x1 -> x0, waiting for transfers between devices: 121 us -> none  [on_device(): running_totals, all_counts = lax.psum((day_terms, counts), 'day')]
    all_gather x1 -> x0, waiting for transfers between devices: 106 us -> none  [on_device(): lax.all_gather(source_spectra, 'tile', axis=1, tiled=True)]
    ppermute x0 -> x28, starting transfers between devices: none -> 39.7 us  [the longest x18 22.8 us: day_swap(): return lax.ppermute(x, 'day', [(i, i ^ k) for i in range(DAYS)])]
    dot_general x1 -> x0, matrix products: 25 us -> none  [pair_stacks(): jnp.einsum('dkrf,fl->dkrl', cross_spectrum, lag_fourier_matrix, preferred...]
    another operation x3 -> x6, other arithmetic: 18.4 us -> 0.41 us  [the longest x3 0.16 us: flip_bits(): x.reshape(shape[:axis] + (shape[axis] // (2 * step), 2, step) + shape[axi...]
    pallas_call x0 -> x5, Pallas kernels: none -> 18 us  [the longest x4 14.2 us: stack_group(): pl.pallas_call(stack_kernel, out_shape=jax.ShapeDtypeStruct((2, PER, 16,...]
    psum x1 -> x0, blocking collectives: 10.1 us -> none  [on_device(): running_totals, all_counts = lax.psum((day_terms, counts), 'day')]
    ppermute x0 -> x28, waiting for transfers between devices: none -> 9.01 us  [the longest x6 5.72 us: tile_swap(): return lax.ppermute(x, 'tile', [(i, i ^ k) for i in range(TILES)])]
  transfers between devices with their start and end apart: 2 -> 28, of which waited for: 2 -> 4; matrix products, arithmetic and copies ran while one was open for 3% -> 4% of each run, Pallas kernels for 0% -> 20%
where the time goes in v1:
time: 71.9 us; the launch traced here: 71.3 us
  starting transfers between devices  39.7 us (55%)
  Pallas kernels  18 us (25%)
  waiting for transfers between devices  9.01 us (13%)
  local copies, waits for them, and re-layouts  3.19 us (4%)
  between operations  0.9 us (1%)
    ppermute x18, starting transfers between devices, day_swap(): return lax.ppermute(x, 'day', [(i, i ^ k) for i in range(DAYS)])  22.8 us
    pallas_call x4, Pallas kernels, stack_group(): pl.pallas_call(stack_kernel, out_shape=jax.ShapeDtypeStruct((2, PER, 16,...  14.2 us
    ppermute x4, starting transfers between devices, turn(): return lax.ppermute(x, ('tile', 'day'), pairs)  9.13 us
    ppermute x6, starting transfers between devices, tile_swap(): return lax.ppermute(x, 'tile', [(i, i ^ k) for i in range(TILES)])  7.75 us
    ppermute x6, waiting for transfers between devices, tile_swap(): return lax.ppermute(x, 'tile', [(i, i ^ k) for i in range(TILES)])  5.72 us
    pallas_call x1, Pallas kernels, order_outputs(): pl.pallas_call(order_kernel, out_shape=(shape, shape), in_specs=[pl.Block...  3.8 us
    ppermute x18, waiting for transfers between devices, day_swap(): return lax.ppermute(x, 'day', [(i, i ^ k) for i in range(DAYS)])  3.27 us
    unnamed x9, local copies, waits for them, and re-layouts  1.86 us
  transfers between devices with their start and end apart: 28, of which 4 were waited for; matrix products, arithmetic and copies ran while one was open for 4% of the time, Pallas kernels for 20%

profile of v1, /device:TPU:1, one launch (start us, length us, event | category | flops | bytes accessed | tf_op | source)
XLA Modules:
  0.0 71.3 jit_solution(11988659199861318772)
XLA Ops:
  0.6 0.0 copy-start.1
  0.6 0.8 %reshape.33 = bf16[8,1024]{1,0:T(8,128)(2,1)S(1)} reshape(bf16[4,1,2,1024]{3,2,1,0:T(2,128)(2,1)} %param.5) | data formatting | bytes 32768 | tf_op jit(solution)/shard_map/reshape | solution.py:177
  1.5 6.3 %collective-permute-start = (bf16[8,1024]{1,0:T(8,128)(2,1)S(1)}, bf16[8,1024]{1,0:T(8,128)(2,1)S(1)}, u32[]{:S(2)}, u32[]{:S(2)}) collective-permute-start(bf16[8,1024]{1,0:T(8,128)(2,1)S(1)} %reshape.33), channel_id=1, source_target_pairs={{0,0},{1,8},{2,16},{3,24},{4,4},{5,12},{6,20},{7,28},{8,1},{9,9},{... | collective-permute-start | bytes 49160 | tf_op jit(solution)/shard_map/ppermute | solution.py:168
  7.8 0.8 %copy.9 = s32[4,64,16]{2,1,0:T(8,128)S(1)} copy(s32[4,64,16]{1,2,0:T(8,128)} %param.7) | data formatting | bytes 32768 | tf_op args[2]
  8.6 0.1 reshape.34
  8.7 0.1 collective-permute-start.10
  8.8 5.5 %collective-permute-start.11 = (bf16[32,128]{1,0:T(8,128)(2,1)S(1)}, bf16[32,128]{1,0:T(8,128)(2,1)S(1)}, u32[]{:S(2)}, u32[]{:S(2)}) collective-permute-start(bf16[32,128]{1,0:T(8,128)(2,1)S(1)} %reshape.34), channel_id=1, source_target_pairs={{0,2},{1,3},{2,0},{3,1},{4,6},{5,7},{6,4},{7,5},{8,10},{9,11},{10,... | collective-permute-start | bytes 24584 | tf_op jit(solution)/shard_map/ppermute | solution.py:155
  14.3 1.5 %collective-permute-start.3 = (bf16[8,1024]{1,0:T(8,128)(2,1)S(1)}, bf16[8,1024]{1,0:T(8,128)(2,1)S(1)}, u32[]{:S(2)}, u32[]{:S(2)}) collective-permute-start(bf16[8,1024]{1,0:T(8,128)(2,1)S(1)} %reshape.33), channel_id=1, source_target_pairs={{0,24},{1,16},{2,8},{3,0},{4,28},{5,20},{6,12},{7,4},{8,25},{9,17}... | collective-permute-start | bytes 49160 | tf_op jit(solution)/shard_map/ppermute | solution.py:168
  15.8 0.0 collective-permute-start.2
  15.8 1.0 %copy.13 = bf16[4,16,2,1024]{3,1,2,0:T(8,128)(2,1)S(1)} copy(bf16[4,16,2,1024]{3,2,1,0:T(2,128)(2,1)} %param.6) | data formatting | bytes 524288 | tf_op args[1]
  16.8 0.0 collective-permute-done.10
  16.8 1.4 %collective-permute-start.1 = (bf16[8,1024]{1,0:T(8,128)(2,1)S(1)}, bf16[8,1024]{1,0:T(8,128)(2,1)S(1)}, u32[]{:S(2)}, u32[]{:S(2)}) collective-permute-start(bf16[8,1024]{1,0:T(8,128)(2,1)S(1)} %reshape.33), channel_id=1, source_target_pairs={{0,8},{1,0},{2,24},{3,16},{4,12},{5,4},{6,28},{7,20},{8,9},{9,1},{... | collective-permute-start | bytes 49160 | tf_op jit(solution)/shard_map/ppermute | solution.py:168
  18.2 0.1 stack.55
  18.3 0.0 collective-permute-done.11
  18.3 3.0 %collective-permute-start.8 = (bf16[4,2,16,1024]{3,2,1,0:T(8,128)(2,1)S(1)}, bf16[4,2,16,1024]{3,2,1,0:T(8,128)(2,1)S(1)}, u32[]{:S(2)}, u32[]{:S(2)}) collective-permute-start(bf16[4,2,16,1024]{3,2,1,0:T(8,128)(2,1)S(1)} %bitcast.35), channel_id=1, source_target_pairs={{0,2},{1,3},{2,0},{3,1},{4,6},{5,7},{6,4},{7,5},{8,10},{9,11},{10,... | collective-permute-start | bytes 786440 | tf_op jit(solution)/shard_map/ppermute | solution.py:155
  21.3 0.1 stack.56
  21.4 0.0 collective-permute-done
  21.4 2.0 %collective-permute-start.7 = (bf16[4,2,16,1024]{3,2,1,0:T(8,128)(2,1)S(1)}, bf16[4,2,16,1024]{3,2,1,0:T(8,128)(2,1)S(1)}, u32[]{:S(2)}, u32[]{:S(2)}) collective-permute-start(bf16[4,2,16,1024]{3,2,1,0:T(8,128)(2,1)S(1)} %bitcast.36), channel_id=1, source_target_pairs={{0,1},{1,0},{2,3},{3,2},{4,5},{5,4},{6,7},{7,6},{8,9},{9,8},{10,11... | collective-permute-start | bytes 786440 | tf_op jit(solution)/shard_map/ppermute | solution.py:155
  23.4 0.0 collective-permute-done.1
  23.4 0.1 collective-permute-start.12
  23.5 0.0 collective-permute-done.2
  23.6 3.3 %collective-permute-start.6 = (bf16[32,1024]{1,0:T(8,128)(2,1)S(1)}, bf16[32,1024]{1,0:T(8,128)(2,1)S(1)}, u32[]{:S(2)}, u32[]{:S(2)}) collective-permute-start(bf16[32,1024]{1,0:T(8,128)(2,1)S(1)} %constant_dynamic-update-slice_fusion), channel_id=1, source_target_pairs={{0,36},{4,32},{8,44},{12,40},{16,52},{20,48},{24,60},{28,56},{32,4... | collective-permute-start | bytes 196616 | tf_op jit(solution)/shard_map/ppermute | solution.py:159
  26.9 0.2 collective-permute-start.5
  27.1 0.7 %collective-permute-start.4 = (bf16[32,1024]{1,0:T(8,128)(2,1)S(1)}, bf16[32,1024]{1,0:T(8,128)(2,1)S(1)}, u32[]{:S(2)}, u32[]{:S(2)}) collective-permute-start(bf16[32,1024]{1,0:T(8,128)(2,1)S(1)} %constant_dynamic-update-slice_fusion), channel_id=1, source_target_pairs={{0,4},{4,0},{8,12},{12,8},{16,20},{20,16},{24,28},{28,24},{32,36},... | collective-permute-start | bytes 196616 | tf_op jit(solution)/shard_map/ppermute | solution.py:159
  27.8 0.1 stack.57
  27.9 0.1 fusion.2
  28.1 0.1 fusion.5
  28.1 0.1 broadcast_select_fusion.1
  28.2 0.1 fusion.4
  28.3 0.1 broadcast_select_fusion.3
  28.4 0.1 copy.11
  28.5 0.0 collective-permute-done.8.rec2
  28.6 1.3 %collective-permute-start.9 = (bf16[4,2,16,1024]{3,2,1,0:T(8,128)(2,1)S(1)}, bf16[4,2,16,1024]{3,2,1,0:T(8,128)(2,1)S(1)}, u32[]{:S(2)}, u32[]{:S(2)}) collective-permute-start(bf16[4,2,16,1024]{3,2,1,0:T(8,128)(2,1)S(1)} %collective-permute-done.8.rec2), channel_id=1, source_target_pairs={{0,1},{1,0},{2,3},{3,2},{4,5},{5,4},{6,7},{7,6},{8,9},{9,8},{10,11... | collective-permute-start | bytes 786440 | tf_op jit(solution)/shard_map/ppermute | solution.py:155
  29.9 2.4 %collective-permute-done.5 = bf16[32,1024]{1,0:T(8,128)(2,1)S(1)} collective-permute-done((bf16[32,1024]{1,0:T(8,128)(2,1)S(1)}, bf16[32,1024]{1,0:T(8,128)(2,1)S(1)}, u32[]{:S(2)}, u32[]{:S(2)}) %collective-permute-start.5) | collective-permute-done | bytes 65568 | tf_op jit(solution)/shard_map/ppermute | solution.py:159
  32.2 0.0 collective-permute-done.4
  32.3 2.8 %collective-permute-start.24 = (bf16[4,32,1024]{2,1,0:T(8,128)(2,1)S(1)}, bf16[4,32,1024]{2,1,0:T(8,128)(2,1)S(1)}, u32[]{:S(2)}, u32[]{:S(2)}) collective-permute-start(bf16[4,32,1024]{2,1,0:T(8,128)(2,1)S(1)} %pad_maximum_fusion.src_ref), channel_id=1, source_target_pairs={{0,192},{4,196},{8,200},{12,204},{16,208},{20,212},{24,216},{28,22... | collective-permute-start | bytes 786440 | tf_op jit(solution)/shard_map/ppermute | solution.py:159
  35.1 0.3 collective-permute-start.20
  35.5 0.3 collective-permute-start.16
  35.8 0.0 collective-permute-done.7.rec1
  35.8 0.0 collective-permute-done.9.rec3
  35.8 3.5 %stack_group.4.refs_0_ = bf16[2,4,16,512]{3,2,1,0:T(8,128)(2,1)S(1)} custom-call(s32[1]{0:T(128)} %bitcast.4.shift_ref, bf16[4,32,1024]{2,1,0:T(8,128)(2,1)S(1)} %pad_maximum_fusion.src_ref, bf16[4,2,16,1024]{3,2,1,0:T(8,128)(2,1)S(1)} %bitcast.37, bf16[4,2,16,1024]{3,2,1,0:T(8,128)(2,1)S(1)} %collective-permute-done.7.rec1, ...), custom_call_target="tpu_custom_call" | custom-call | flops 2147483648 | bytes 3145728 | tf_op jit(solution)/shard_map/stack_group/pallas_call | solution.py:95
  39.4 1.2 %collective-permute-start.14 = (bf16[2,4,16,512]{3,2,1,0:T(8,128)(2,1)S(1)}, bf16[2,4,16,512]{3,2,1,0:T(8,128)(2,1)S(1)}, u32[]{:S(2)}, u32[]{:S(2)}) collective-permute-start(bf16[2,4,16,512]{3,2,1,0:T(8,128)(2,1)S(1)} %stack_group.4.refs_0_), channel_id=1, source_target_pairs={{0,2},{1,3},{2,0},{3,1},{4,6},{5,7},{6,4},{7,5},{8,10},{9,11},{10,... | collective-permute-start | bytes 393224 | tf_op jit(solution)/shard_map/ppermute | solution.py:155
  40.5 2.4 %collective-permute-start.13 = (bf16[2,4,16,512]{3,2,1,0:T(8,128)(2,1)S(1)}, bf16[2,4,16,512]{3,2,1,0:T(8,128)(2,1)S(1)}, u32[]{:S(2)}, u32[]{:S(2)}) collective-permute-start(bf16[2,4,16,512]{3,2,1,0:T(8,128)(2,1)S(1)} %stack_group.4.refs_0_), channel_id=1, source_target_pairs={{0,1},{1,0},{2,3},{3,2},{4,5},{5,4},{6,7},{7,6},{8,9},{9,8},{10,11... | collective-permute-start | bytes 393224 | tf_op jit(solution)/shard_map/ppermute | solution.py:155
  42.9 3.4 %collective-permute-done.24.src_ref = bf16[4,32,1024]{2,1,0:T(8,128)(2,1)S(1)} collective-permute-done((bf16[4,32,1024]{2,1,0:T(8,128)(2,1)S(1)}, bf16[4,32,1024]{2,1,0:T(8,128)(2,1)S(1)}, u32[]{:S(2)}, u32[]{:S(2)}) %collective-permute-start.24) | collective-permute-done | bytes 262176 | tf_op jit(solution)/shard_map/ppermute | solution.py:159
  46.3 3.5 %stack_group.7.refs_12_ = bf16[2,4,16,512]{3,2,1,0:T(8,128)(2,1)S(1)} custom-call(s32[1]{0:T(128)} %bitcast.4.shift_ref, bf16[4,32,1024]{2,1,0:T(8,128)(2,1)S(1)} %collective-permute-done.24.src_ref, bf16[4,2,16,1024]{3,2,1,0:T(8,128)(2,1)S(1)} %bitcast.38, bf16[4,2,16,1024]{3,2,1,0:T(8,128)(2,1)S(1)} %collective-permute-done.7.rec1, ...), custom_call_target="tpu_custom_call" | custom-call | flops 2147483648 | bytes 3145728 | tf_op jit(solution)/shard_map/stack_group/pallas_call | solution.py:95
  49.8 1.2 %collective-permute-start.26 = (bf16[2,4,16,512]{3,2,1,0:T(8,128)(2,1)S(1)}, bf16[2,4,16,512]{3,2,1,0:T(8,128)(2,1)S(1)}, u32[]{:S(2)}, u32[]{:S(2)}) collective-permute-start(bf16[2,4,16,512]{3,2,1,0:T(8,128)(2,1)S(1)} %stack_group.7.refs_12_), channel_id=1, source_target_pairs={{0,2},{1,3},{2,0},{3,1},{4,6},{5,7},{6,4},{7,5},{8,10},{9,11},{10,... | collective-permute-start | bytes 393224 | tf_op jit(solution)/shard_map/ppermute | solution.py:155
  51.0 0.0 collective-permute-done.20.src_ref
  51.0 2.0 %collective-permute-start.25 = (bf16[2,4,16,512]{3,2,1,0:T(8,128)(2,1)S(1)}, bf16[2,4,16,512]{3,2,1,0:T(8,128)(2,1)S(1)}, u32[]{:S(2)}, u32[]{:S(2)}) collective-permute-start(bf16[2,4,16,512]{3,2,1,0:T(8,128)(2,1)S(1)} %stack_group.7.refs_12_), channel_id=1, source_target_pairs={{0,1},{1,0},{2,3},{3,2},{4,5},{5,4},{6,7},{7,6},{8,9},{9,8},{10,11... | collective-permute-start | bytes 393224 | tf_op jit(solution)/shard_map/ppermute | solution.py:155
  53.0 3.5 %stack_group.6.refs_8_ = bf16[2,4,16,512]{3,2,1,0:T(8,128)(2,1)S(1)} custom-call(s32[1]{0:T(128)} %bitcast.4.shift_ref, bf16[4,32,1024]{2,1,0:T(8,128)(2,1)S(1)} %collective-permute-done.20.src_ref, bf16[4,2,16,1024]{3,2,1,0:T(8,128)(2,1)S(1)} %bitcast.39, bf16[4,2,16,1024]{3,2,1,0:T(8,128)(2,1)S(1)} %collective-permute-done.7.rec1, ...), custom_call_target="tpu_custom_call" | custom-call | flops 2147483648 | bytes 3145728 | tf_op jit(solution)/shard_map/stack_group/pallas_call | solution.py:95
  56.5 0.0 collective-permute-done.16.src_ref
  56.5 0.1 collective-permute-start.22
  56.7 3.5 %stack_group.5.refs_4_ = bf16[2,4,16,512]{3,2,1,0:T(8,128)(2,1)S(1)} custom-call(s32[1]{0:T(128)} %bitcast.4.shift_ref, bf16[4,32,1024]{2,1,0:T(8,128)(2,1)S(1)} %collective-permute-done.16.src_ref, bf16[4,2,16,1024]{3,2,1,0:T(8,128)(2,1)S(1)} %bitcast.40, bf16[4,2,16,1024]{3,2,1,0:T(8,128)(2,1)S(1)} %collective-permute-done.7.rec1, ...), custom_call_target="tpu_custom_call" | custom-call | flops 2147483648 | bytes 3145728 | tf_op jit(solution)/shard_map/stack_group/pallas_call | solution.py:95
  60.2 0.4 collective-permute-start.21
  60.6 1.4 %collective-permute-start.18 = (bf16[2,4,16,512]{3,2,1,0:T(8,128)(2,1)S(1)}, bf16[2,4,16,512]{3,2,1,0:T(8,128)(2,1)S(1)}, u32[]{:S(2)}, u32[]{:S(2)}) collective-permute-start(bf16[2,4,16,512]{3,2,1,0:T(8,128)(2,1)S(1)} %stack_group.5.refs_4_), channel_id=1, source_target_pairs={{0,2},{1,3},{2,0},{3,1},{4,6},{5,7},{6,4},{7,5},{8,10},{9,11},{10,... | collective-permute-start | bytes 393224 | tf_op jit(solution)/shard_map/ppermute | solution.py:155
  62.1 0.5 collective-permute-start.17
  62.6 0.1 collective-permute-start.15
  62.7 0.4 collective-permute-start.27
  63.1 0.1 collective-permute-start.23
  63.2 2.3 %collective-permute-done.18.refs_6_ = bf16[2,4,16,512]{3,2,1,0:T(8,128)(2,1)S(1)} collective-permute-done((bf16[2,4,16,512]{3,2,1,0:T(8,128)(2,1)S(1)}, bf16[2,4,16,512]{3,2,1,0:T(8,128)(2,1)S(1)}, u32[]{:S(2)}, u32[]{:S(2)}) %collective-permute-start.18) | collective-permute-done | bytes 131104 | tf_op jit(solution)/shard_map/ppermute | solution.py:155
  65.5 1.0 %collective-permute-start.19 = (bf16[2,4,16,512]{3,2,1,0:T(8,128)(2,1)S(1)}, bf16[2,4,16,512]{3,2,1,0:T(8,128)(2,1)S(1)}, u32[]{:S(2)}, u32[]{:S(2)}) collective-permute-start(bf16[2,4,16,512]{3,2,1,0:T(8,128)(2,1)S(1)} %collective-permute-done.18.refs_6_), channel_id=1, source_target_pairs={{0,1},{1,0},{2,3},{3,2},{4,5},{5,4},{6,7},{7,6},{8,9},{9,8},{10,11... | collective-permute-start | bytes 393224 | tf_op jit(solution)/shard_map/ppermute | solution.py:155
  66.5 0.1 pad_add_fusion.where_ref
  66.6 0.0 collective-permute-done.23.refs_11_
  66.6 0.9 %collective-permute-done.19.refs_7_ = bf16[2,4,16,512]{3,2,1,0:T(8,128)(2,1)S(1)} collective-permute-done((bf16[2,4,16,512]{3,2,1,0:T(8,128)(2,1)S(1)}, bf16[2,4,16,512]{3,2,1,0:T(8,128)(2,1)S(1)}, u32[]{:S(2)}, u32[]{:S(2)}) %collective-permute-start.19) | collective-permute-done | bytes 131104 | tf_op jit(solution)/shard_map/ppermute | solution.py:155
  67.5 3.8 %order_outputs.1 = (f32[64,16,401]{2,1,0:T(8,128)}, f32[64,16,401]{2,1,0:T(8,128)}) custom-call(s32[4]{0:T(128)S(1)} %pad_add_fusion.where_ref, bf16[512,512]{1,0:T(8,128)(2,1)S(1)} %copy-done, bf16[2,4,16,512]{3,2,1,0:T(8,128)(2,1)S(1)} %stack_group.4.refs_0_, bf16[2,4,16,512]{3,2,1,0:T(8,128)(2,1)S(1)} %collective-permute-done.13.refs_1_, ...), custom_call_target="tpu_custom_call" | custom-call | tf_op jit(solution)/shard_map/order_outputs/pallas_call | solution.py:134
  (26 shorter events, 0.2 us)
Async XLA Ops:
  0.6 35.2 %copy-start.1 = (bf16[1024,512]{1,0:T(8,128)(2,1)S(1)}, bf16[1024,512]{1,0:T(8,128)(2,1)}, u32[]{:S(2)}) copy-start(bf16[1024,512]{1,0:T(8,128)(2,1)} %constant.28.clone.basis_ref) | copy-start | bytes 3145732
  1.5 19.9 %collective-permute-start = (bf16[8,1024]{1,0:T(8,128)(2,1)S(1)}, bf16[8,1024]{1,0:T(8,128)(2,1)S(1)}, u32[]{:S(2)}, u32[]{:S(2)}) collective-permute-start(bf16[8,1024]{1,0:T(8,128)(2,1)S(1)} %reshape.33), channel_id=1, source_target_pairs={{0,0},{1,8},{2,16},{3,24},{4,4},{5,12},{6,20},{7,28},{8,1},{9,9},{... | collective-permute-start | bytes 49160 | tf_op jit(solution)/shard_map/ppermute | solution.py:168
  8.7 8.1 %collective-permute-start.10 = (bf16[32,128]{1,0:T(8,128)(2,1)S(1)}, bf16[32,128]{1,0:T(8,128)(2,1)S(1)}, u32[]{:S(2)}, u32[]{:S(2)}) collective-permute-start(bf16[32,128]{1,0:T(8,128)(2,1)S(1)} %reshape.34), channel_id=1, source_target_pairs={{0,1},{1,0},{2,3},{3,2},{4,5},{5,4},{6,7},{7,6},{8,9},{9,8},{10,11... | collective-permute-start | bytes 24584 | tf_op jit(solution)/shard_map/ppermute | solution.py:155
  8.8 9.5 %collective-permute-start.11 = (bf16[32,128]{1,0:T(8,128)(2,1)S(1)}, bf16[32,128]{1,0:T(8,128)(2,1)S(1)}, u32[]{:S(2)}, u32[]{:S(2)}) collective-permute-start(bf16[32,128]{1,0:T(8,128)(2,1)S(1)} %reshape.34), channel_id=1, source_target_pairs={{0,2},{1,3},{2,0},{3,1},{4,6},{5,7},{6,4},{7,5},{8,10},{9,11},{10,... | collective-permute-start | bytes 24584 | tf_op jit(solution)/shard_map/ppermute | solution.py:155
  14.3 9.2 %collective-permute-start.3 = (bf16[8,1024]{1,0:T(8,128)(2,1)S(1)}, bf16[8,1024]{1,0:T(8,128)(2,1)S(1)}, u32[]{:S(2)}, u32[]{:S(2)}) collective-permute-start(bf16[8,1024]{1,0:T(8,128)(2,1)S(1)} %reshape.33), channel_id=1, source_target_pairs={{0,24},{1,16},{2,8},{3,0},{4,28},{5,20},{6,12},{7,4},{8,25},{9,17}... | collective-permute-start | bytes 49160 | tf_op jit(solution)/shard_map/ppermute | solution.py:168
  15.8 7.7 %collective-permute-start.2 = (bf16[8,1024]{1,0:T(8,128)(2,1)S(1)}, bf16[8,1024]{1,0:T(8,128)(2,1)S(1)}, u32[]{:S(2)}, u32[]{:S(2)}) collective-permute-start(bf16[8,1024]{1,0:T(8,128)(2,1)S(1)} %reshape.33), channel_id=1, source_target_pairs={{0,16},{1,24},{2,0},{3,8},{4,20},{5,28},{6,4},{7,12},{8,17},{9,25}... | collective-permute-start | bytes 49160 | tf_op jit(solution)/shard_map/ppermute | solution.py:168
  16.8 6.6 %collective-permute-start.1 = (bf16[8,1024]{1,0:T(8,128)(2,1)S(1)}, bf16[8,1024]{1,0:T(8,128)(2,1)S(1)}, u32[]{:S(2)}, u32[]{:S(2)}) collective-permute-start(bf16[8,1024]{1,0:T(8,128)(2,1)S(1)} %reshape.33), channel_id=1, source_target_pairs={{0,8},{1,0},{2,24},{3,16},{4,12},{5,4},{6,28},{7,20},{8,9},{9,1},{... | collective-permute-start | bytes 49160 | tf_op jit(solution)/shard_map/ppermute | solution.py:168
  18.3 10.2 %collective-permute-start.8 = (bf16[4,2,16,1024]{3,2,1,0:T(8,128)(2,1)S(1)}, bf16[4,2,16,1024]{3,2,1,0:T(8,128)(2,1)S(1)}, u32[]{:S(2)}, u32[]{:S(2)}) collective-permute-start(bf16[4,2,16,1024]{3,2,1,0:T(8,128)(2,1)S(1)} %bitcast.35), channel_id=1, source_target_pairs={{0,2},{1,3},{2,0},{3,1},{4,6},{5,7},{6,4},{7,5},{8,10},{9,11},{10,... | collective-permute-start | bytes 786440 | tf_op jit(solution)/shard_map/ppermute | solution.py:155
  21.4 14.4 %collective-permute-start.7 = (bf16[4,2,16,1024]{3,2,1,0:T(8,128)(2,1)S(1)}, bf16[4,2,16,1024]{3,2,1,0:T(8,128)(2,1)S(1)}, u32[]{:S(2)}, u32[]{:S(2)}) collective-permute-start(bf16[4,2,16,1024]{3,2,1,0:T(8,128)(2,1)S(1)} %bitcast.36), channel_id=1, source_target_pairs={{0,1},{1,0},{2,3},{3,2},{4,5},{5,4},{6,7},{7,6},{8,9},{9,8},{10,11... | collective-permute-start | bytes 786440 | tf_op jit(solution)/shard_map/ppermute | solution.py:155
  23.4 3.7 %collective-permute-start.12 = (bf16[32,128]{1,0:T(8,128)(2,1)S(1)}, bf16[32,128]{1,0:T(8,128)(2,1)S(1)}, u32[]{:S(2)}, u32[]{:S(2)}) collective-permute-start(bf16[32,128]{1,0:T(8,128)(2,1)S(1)} %collective-permute-done.11), channel_id=1, source_target_pairs={{0,1},{1,0},{2,3},{3,2},{4,5},{5,4},{6,7},{7,6},{8,9},{9,8},{10,11... | collective-permute-start | bytes 24584 | tf_op jit(solution)/shard_map/ppermute | solution.py:155
  23.6 6.3 %collective-permute-start.6 = (bf16[32,1024]{1,0:T(8,128)(2,1)S(1)}, bf16[32,1024]{1,0:T(8,128)(2,1)S(1)}, u32[]{:S(2)}, u32[]{:S(2)}) collective-permute-start(bf16[32,1024]{1,0:T(8,128)(2,1)S(1)} %constant_dynamic-update-slice_fusion), channel_id=1, source_target_pairs={{0,36},{4,32},{8,44},{12,40},{16,52},{20,48},{24,60},{28,56},{32,4... | collective-permute-start | bytes 196616 | tf_op jit(solution)/shard_map/ppermute | solution.py:159
  26.9 5.4 %collective-permute-start.5 = (bf16[32,1024]{1,0:T(8,128)(2,1)S(1)}, bf16[32,1024]{1,0:T(8,128)(2,1)S(1)}, u32[]{:S(2)}, u32[]{:S(2)}) collective-permute-start(bf16[32,1024]{1,0:T(8,128)(2,1)S(1)} %constant_dynamic-update-slice_fusion), channel_id=1, source_target_pairs={{0,32},{4,36},{8,40},{12,44},{16,48},{20,52},{24,56},{28,60},{32,0... | collective-permute-start | bytes 196616 | tf_op jit(solution)/shard_map/ppermute | solution.py:159
  27.1 5.2 %collective-permute-start.4 = (bf16[32,1024]{1,0:T(8,128)(2,1)S(1)}, bf16[32,1024]{1,0:T(8,128)(2,1)S(1)}, u32[]{:S(2)}, u32[]{:S(2)}) collective-permute-start(bf16[32,1024]{1,0:T(8,128)(2,1)S(1)} %constant_dynamic-update-slice_fusion), channel_id=1, source_target_pairs={{0,4},{4,0},{8,12},{12,8},{16,20},{20,16},{24,28},{28,24},{32,36},... | collective-permute-start | bytes 196616 | tf_op jit(solution)/shard_map/ppermute | solution.py:159
  28.6 7.2 %collective-permute-start.9 = (bf16[4,2,16,1024]{3,2,1,0:T(8,128)(2,1)S(1)}, bf16[4,2,16,1024]{3,2,1,0:T(8,128)(2,1)S(1)}, u32[]{:S(2)}, u32[]{:S(2)}) collective-permute-start(bf16[4,2,16,1024]{3,2,1,0:T(8,128)(2,1)S(1)} %collective-permute-done.8.rec2), channel_id=1, source_target_pairs={{0,1},{1,0},{2,3},{3,2},{4,5},{5,4},{6,7},{7,6},{8,9},{9,8},{10,11... | collective-permute-start | bytes 786440 | tf_op jit(solution)/shard_map/ppermute | solution.py:155
  32.3 14.0 %collective-permute-start.24 = (bf16[4,32,1024]{2,1,0:T(8,128)(2,1)S(1)}, bf16[4,32,1024]{2,1,0:T(8,128)(2,1)S(1)}, u32[]{:S(2)}, u32[]{:S(2)}) collective-permute-start(bf16[4,32,1024]{2,1,0:T(8,128)(2,1)S(1)} %pad_maximum_fusion.src_ref), channel_id=1, source_target_pairs={{0,192},{4,196},{8,200},{12,204},{16,208},{20,212},{24,216},{28,22... | collective-permute-start | bytes 786440 | tf_op jit(solution)/shard_map/ppermute | solution.py:159
  35.1 15.9 %collective-permute-start.20 = (bf16[4,32,1024]{2,1,0:T(8,128)(2,1)S(1)}, bf16[4,32,1024]{2,1,0:T(8,128)(2,1)S(1)}, u32[]{:S(2)}, u32[]{:S(2)}) collective-permute-start(bf16[4,32,1024]{2,1,0:T(8,128)(2,1)S(1)} %pad_maximum_fusion.src_ref), channel_id=1, source_target_pairs={{0,128},{4,132},{8,136},{12,140},{16,144},{20,148},{24,152},{28,15... | collective-permute-start | bytes 786440 | tf_op jit(solution)/shard_map/ppermute | solution.py:159
  35.5 21.1 %collective-permute-start.16 = (bf16[4,32,1024]{2,1,0:T(8,128)(2,1)S(1)}, bf16[4,32,1024]{2,1,0:T(8,128)(2,1)S(1)}, u32[]{:S(2)}, u32[]{:S(2)}) collective-permute-start(bf16[4,32,1024]{2,1,0:T(8,128)(2,1)S(1)} %pad_maximum_fusion.src_ref), channel_id=1, source_target_pairs={{0,64},{4,68},{8,72},{12,76},{16,80},{20,84},{24,88},{28,92},{32,9... | collective-permute-start | bytes 786440 | tf_op jit(solution)/shard_map/ppermute | solution.py:159
  39.4 20.9 %collective-permute-start.14 = (bf16[2,4,16,512]{3,2,1,0:T(8,128)(2,1)S(1)}, bf16[2,4,16,512]{3,2,1,0:T(8,128)(2,1)S(1)}, u32[]{:S(2)}, u32[]{:S(2)}) collective-permute-start(bf16[2,4,16,512]{3,2,1,0:T(8,128)(2,1)S(1)} %stack_group.4.refs_0_), channel_id=1, source_target_pairs={{0,2},{1,3},{2,0},{3,1},{4,6},{5,7},{6,4},{7,5},{8,10},{9,11},{10,... | collective-permute-start | bytes 393224 | tf_op jit(solution)/shard_map/ppermute | solution.py:155
  40.5 20.1 %collective-permute-start.13 = (bf16[2,4,16,512]{3,2,1,0:T(8,128)(2,1)S(1)}, bf16[2,4,16,512]{3,2,1,0:T(8,128)(2,1)S(1)}, u32[]{:S(2)}, u32[]{:S(2)}) collective-permute-start(bf16[2,4,16,512]{3,2,1,0:T(8,128)(2,1)S(1)} %stack_group.4.refs_0_), channel_id=1, source_target_pairs={{0,1},{1,0},{2,3},{3,2},{4,5},{5,4},{6,7},{7,6},{8,9},{9,8},{10,11... | collective-permute-start | bytes 393224 | tf_op jit(solution)/shard_map/ppermute | solution.py:155
  49.8 12.2 %collective-permute-start.26 = (bf16[2,4,16,512]{3,2,1,0:T(8,128)(2,1)S(1)}, bf16[2,4,16,512]{3,2,1,0:T(8,128)(2,1)S(1)}, u32[]{:S(2)}, u32[]{:S(2)}) collective-permute-start(bf16[2,4,16,512]{3,2,1,0:T(8,128)(2,1)S(1)} %stack_group.7.refs_12_), channel_id=1, source_target_pairs={{0,2},{1,3},{2,0},{3,1},{4,6},{5,7},{6,4},{7,5},{8,10},{9,11},{10,... | collective-permute-start | bytes 393224 | tf_op jit(solution)/shard_map/ppermute | solution.py:155
  51.0 11.5 %collective-permute-start.25 = (bf16[2,4,16,512]{3,2,1,0:T(8,128)(2,1)S(1)}, bf16[2,4,16,512]{3,2,1,0:T(8,128)(2,1)S(1)}, u32[]{:S(2)}, u32[]{:S(2)}) collective-permute-start(bf16[2,4,16,512]{3,2,1,0:T(8,128)(2,1)S(1)} %stack_group.7.refs_12_), channel_id=1, source_target_pairs={{0,1},{1,0},{2,3},{3,2},{4,5},{5,4},{6,7},{7,6},{8,9},{9,8},{10,11... | collective-permute-start | bytes 393224 | tf_op jit(solution)/shard_map/ppermute | solution.py:155
  56.5 6.1 %collective-permute-start.22 = (bf16[2,4,16,512]{3,2,1,0:T(8,128)(2,1)S(1)}, bf16[2,4,16,512]{3,2,1,0:T(8,128)(2,1)S(1)}, u32[]{:S(2)}, u32[]{:S(2)}) collective-permute-start(bf16[2,4,16,512]{3,2,1,0:T(8,128)(2,1)S(1)} %stack_group.6.refs_8_), channel_id=1, source_target_pairs={{0,2},{1,3},{2,0},{3,1},{4,6},{5,7},{6,4},{7,5},{8,10},{9,11},{10,... | collective-permute-start | bytes 393224 | tf_op jit(solution)/shard_map/ppermute | solution.py:155
  56.7 10.8 %copy-start = (bf16[512,512]{1,0:T(8,128)(2,1)S(1)}, bf16[512,512]{1,0:T(8,128)(2,1)}, u32[]{:S(2)}) copy-start(bf16[512,512]{1,0:T(8,128)(2,1)} %constant.29.clone.order_ref) | copy-start | bytes 1572868
  60.2 2.8 %collective-permute-start.21 = (bf16[2,4,16,512]{3,2,1,0:T(8,128)(2,1)S(1)}, bf16[2,4,16,512]{3,2,1,0:T(8,128)(2,1)S(1)}, u32[]{:S(2)}, u32[]{:S(2)}) collective-permute-start(bf16[2,4,16,512]{3,2,1,0:T(8,128)(2,1)S(1)} %stack_group.6.refs_8_), channel_id=1, source_target_pairs={{0,1},{1,0},{2,3},{3,2},{4,5},{5,4},{6,7},{7,6},{8,9},{9,8},{10,11... | collective-permute-start | bytes 393224 | tf_op jit(solution)/shard_map/ppermute | solution.py:155
  60.6 4.9 %collective-permute-start.18 = (bf16[2,4,16,512]{3,2,1,0:T(8,128)(2,1)S(1)}, bf16[2,4,16,512]{3,2,1,0:T(8,128)(2,1)S(1)}, u32[]{:S(2)}, u32[]{:S(2)}) collective-permute-start(bf16[2,4,16,512]{3,2,1,0:T(8,128)(2,1)S(1)} %stack_group.5.refs_4_), channel_id=1, source_target_pairs={{0,2},{1,3},{2,0},{3,1},{4,6},{5,7},{6,4},{7,5},{8,10},{9,11},{10,... | collective-permute-start | bytes 393224 | tf_op jit(solution)/shard_map/ppermute | solution.py:155
  62.1 4.6 %collective-permute-start.17 = (bf16[2,4,16,512]{3,2,1,0:T(8,128)(2,1)S(1)}, bf16[2,4,16,512]{3,2,1,0:T(8,128)(2,1)S(1)}, u32[]{:S(2)}, u32[]{:S(2)}) collective-permute-start(bf16[2,4,16,512]{3,2,1,0:T(8,128)(2,1)S(1)} %stack_group.5.refs_4_), channel_id=1, source_target_pairs={{0,1},{1,0},{2,3},{3,2},{4,5},{5,4},{6,7},{7,6},{8,9},{9,8},{10,11... | collective-permute-start | bytes 393224 | tf_op jit(solution)/shard_map/ppermute | solution.py:155
  62.6 4.1 %collective-permute-start.15 = (bf16[2,4,16,512]{3,2,1,0:T(8,128)(2,1)S(1)}, bf16[2,4,16,512]{3,2,1,0:T(8,128)(2,1)S(1)}, u32[]{:S(2)}, u32[]{:S(2)}) collective-permute-start(bf16[2,4,16,512]{3,2,1,0:T(8,128)(2,1)S(1)} %collective-permute-done.14.refs_2_), channel_id=1, source_target_pairs={{0,1},{1,0},{2,3},{3,2},{4,5},{5,4},{6,7},{7,6},{8,9},{9,8},{10,11... | collective-permute-start | bytes 393224 | tf_op jit(solution)/shard_map/ppermute | solution.py:155
  62.7 4.0 %collective-permute-start.27 = (bf16[2,4,16,512]{3,2,1,0:T(8,128)(2,1)S(1)}, bf16[2,4,16,512]{3,2,1,0:T(8,128)(2,1)S(1)}, u32[]{:S(2)}, u32[]{:S(2)}) collective-permute-start(bf16[2,4,16,512]{3,2,1,0:T(8,128)(2,1)S(1)} %collective-permute-done.26.refs_14_), channel_id=1, source_target_pairs={{0,1},{1,0},{2,3},{3,2},{4,5},{5,4},{6,7},{7,6},{8,9},{9,8},{10,11... | collective-permute-start | bytes 393224 | tf_op jit(solution)/shard_map/ppermute | solution.py:155
  63.1 3.6 %collective-permute-start.23 = (bf16[2,4,16,512]{3,2,1,0:T(8,128)(2,1)S(1)}, bf16[2,4,16,512]{3,2,1,0:T(8,128)(2,1)S(1)}, u32[]{:S(2)}, u32[]{:S(2)}) collective-permute-start(bf16[2,4,16,512]{3,2,1,0:T(8,128)(2,1)S(1)} %collective-permute-done.22.refs_10_), channel_id=1, source_target_pairs={{0,1},{1,0},{2,3},{3,2},{4,5},{5,4},{6,7},{7,6},{8,9},{9,8},{10,11... | collective-permute-start | bytes 393224 | tf_op jit(solution)/shard_map/ppermute | solution.py:155
  65.5 2.0 %collective-permute-start.19 = (bf16[2,4,16,512]{3,2,1,0:T(8,128)(2,1)S(1)}, bf16[2,4,16,512]{3,2,1,0:T(8,128)(2,1)S(1)}, u32[]{:S(2)}, u32[]{:S(2)}) collective-permute-start(bf16[2,4,16,512]{3,2,1,0:T(8,128)(2,1)S(1)} %collective-permute-done.18.refs_6_), channel_id=1, source_target_pairs={{0,1},{1,0},{2,3},{3,2},{4,5},{5,4},{6,7},{7,6},{8,9},{9,8},{10,11... | collective-permute-start | bytes 393224 | tf_op jit(solution)/shard_map/ppermute | solution.py:155

commit v2 on v1

v2 whole, which is shorter than its diff:
```python
import math

import jax
import jax.numpy as jnp
import numpy as np
from jax import lax
from jax.experimental import pallas as pl
from jax.experimental.pallas import tpu as pltpu
from jax.sharding import PartitionSpec as P

MAXLAG = 200
HALF = 256
TILES, DAYS = 64, 4

PER = 4


def half_basis(frequency_count):
    samples = 2 * frequency_count
    freq = np.arange(frequency_count)[:, None]
    lag = np.arange(MAXLAG + 1)[None, :]
    angles = ((freq * lag) % samples) * (2.0 * math.pi / samples)
    weight = np.where(freq == 0, 0.5, 1.0) * frequency_count ** (-0.5)
    table = np.zeros((frequency_count, 2 * HALF))
    table[:, : MAXLAG + 1] = weight * np.cos(angles)
    table[:, HALF : HALF + MAXLAG + 1] = weight * np.sin(angles)
    return jnp.asarray(table, jnp.bfloat16)


def lag_order():
    table = np.zeros((2 * HALF, 2 * HALF))
    lag = np.arange(MAXLAG + 1)
    table[lag, MAXLAG + lag] = 1.0
    table[HALF + lag[1:], MAXLAG - lag[1:]] = 1.0
    return jnp.asarray(table, jnp.bfloat16)


def widen_kernel(where_ref, rec0, rec1, rec2, rec3, out_ref, mask_ref, rows_ref):
    y, middle, day, shift = (where_ref[i] for i in range(4))
    width = out_ref.shape[-1]
    for j, rec in enumerate((rec0, rec1, rec2, rec3)):
        k = j ^ shift
        wide = rec[: 32 * PER].astype(jnp.float32)
        out_ref[pl.ds(k * PER, PER)] = wide.reshape(PER, 2, 16, width)
        rows_ref[k] = rec[32 * PER :]
    rows = rows_ref[...].reshape(64, width)
    gap = lax.broadcasted_iota(jnp.int32, (16, width), 1) - lax.broadcasted_iota(jnp.int32, (16, width), 0)
    for k3 in range(4):
        picks = []
        for k2 in range(PER):
            source = source_index(y ^ k3, day, middle ^ k2)
            picks.append(jnp.where(gap == source * 16, 1.0, 0.0).astype(jnp.bfloat16))
        chosen = lax.dot_general(
            jnp.concatenate(picks, axis=0), rows, (((1,), (1,)), ((), ())),
            preferred_element_type=jnp.float32,
        )
        mask_ref[k3, :, :, :64] = chosen.reshape(PER, 16, 64)


def source_index(y, day, middle):
    return (y << 4) | ((day >> 1) << 3) | (middle << 1) | (day & 1)


def widen_receivers(where, receivers):
    whole = pl.BlockSpec(memory_space=pltpu.VMEM)
    width = receivers[0].shape[-1]
    return pl.pallas_call(
        widen_kernel,
        out_shape=(
            jax.ShapeDtypeStruct((4 * PER, 2, 16, width), jnp.float32),
            jax.ShapeDtypeStruct((4, PER, 16, 128), jnp.float32),
        ),
        in_specs=[pl.BlockSpec(memory_space=pltpu.SMEM)] + [whole] * 4,
        out_specs=(whole, whole),
        scratch_shapes=[pltpu.VMEM((4, 16, width), jnp.bfloat16)],
        compiler_params=pltpu.CompilerParams(vmem_limit_bytes=16 * 2**20),
        name="widen_receivers",
    )(where, *receivers)


def stack_kernel(src_ref, rec_ref, mask_ref, basis_ref, *refs):
    out_ref, src_f32, lhs, res, done = refs[-5:]
    days, half = 4 * PER, lhs.shape[1] // 2
    width = basis_ref.shape[0]
    src_f32[...] = src_ref[...].astype(jnp.float32)
    for s in range(PER):
        p = s % 2
        for d in range(days):
            rows = slice(d * 16, d * 16 + 16)
            low = slice(half + d * 16, half + d * 16 + 16)
            row = (d // PER * PER + s) * 2 * PER + d % PER * 2
            for lane in range(0, width, 256):
                cols = slice(lane, lane + 256)
                a = src_f32[row : row + 1, cols]
                b = src_f32[row + 1 : row + 2, cols]
                c = rec_ref[d, 0, :, cols]
                e = rec_ref[d, 1, :, cols]
                lhs[p, rows, cols] = (a * c + b * e).astype(jnp.bfloat16)
                lhs[p, low, cols] = (a * e - b * c).astype(jnp.bfloat16)
        res[p] = jnp.dot(lhs[p], basis_ref[...], preferred_element_type=jnp.float32)
        for h in range(0, 16, 8):
            zero = jnp.zeros((8, 128), jnp.float32)
            sums = [[zero] * 6 for _ in range(2)]
            count = zero
            for d in range(days):
                rows = slice(d * 16 + h, d * 16 + h + 8)
                low = slice(half + d * 16 + h, half + d * 16 + h + 8)
                col = (d // PER) * 16 + d % PER
                m = jnp.broadcast_to(mask_ref[s, h : h + 8, col : col + 1], (8, 128))
                count = count + m
                for i in range(2):
                    cos = slice(i * 128, i * 128 + 128)
                    sin = slice(HALF + i * 128, HALF + i * 128 + 128)
                    rc, rs = res[p, rows, cos], res[p, rows, sin]
                    ic, is_ = res[p, low, cos], res[p, low, sin]
                    for sign, (u, v) in enumerate(((rc - is_, ic + rs), (rc + is_, ic - rs))):
                        w = m * lax.rsqrt(u * u + v * v + 0.0625)
                        acc = sums[i]
                        acc[3 * sign] = acc[3 * sign] + m * u
                        acc[3 * sign + 1] = acc[3 * sign + 1] + w * u
                        acc[3 * sign + 2] = acc[3 * sign + 2] + w * v
            inverse = 1.0 / jnp.maximum(count, 1.0)
            for i in range(2):
                for sign in range(2):
                    linear, real, imag = sums[i][3 * sign : 3 * sign + 3]
                    mean = linear * inverse
                    cols = slice(sign * HALF + i * 128, sign * HALF + i * 128 + 128)
                    done[0, h : h + 8, cols] = mean
                    done[1, h : h + 8, cols] = mean * ((real * real + imag * imag) * (inverse * inverse))
        out_ref[0, s] = done[0].astype(jnp.bfloat16)
        out_ref[1, s] = done[1].astype(jnp.bfloat16)


def stack_group(sources, receivers, mask, basis, earlier):
    width = sources.shape[-1]
    whole = pl.BlockSpec(memory_space=pltpu.VMEM)
    rows = 2 * 4 * PER * 16
    return pl.pallas_call(
        stack_kernel,
        out_shape=jax.ShapeDtypeStruct((2, PER, 16, 2 * HALF), jnp.bfloat16),
        in_specs=[whole] * 4 + [pl.BlockSpec(memory_space=pl.ANY)] * len(earlier),
        out_specs=whole,
        scratch_shapes=[
            pltpu.VMEM(sources.shape, jnp.float32),
            pltpu.VMEM((2, rows, width), jnp.bfloat16),
            pltpu.VMEM((2, rows, 2 * HALF), jnp.float32),
            pltpu.VMEM((2, 16, 2 * HALF), jnp.float32),
        ],
        compiler_params=pltpu.CompilerParams(vmem_limit_bytes=24 * 2**20),
        cost_estimate=pl.CostEstimate(
            flops=2 * PER * rows * width * 2 * HALF, bytes_accessed=3 * 2**20, transcendentals=0
        ),
        name="stack_group",
    )(sources, receivers, mask, basis, *earlier)


def order_kernel(place_ref, order_ref, *refs):
    mean_ref, weighted_ref = refs[-2:]
    middle, day = place_ref[0], place_ref[1]
    size = 2 * PER * 16

    def one(group):
        parts = [part[...].reshape(size, 2 * HALF) for part in group]
        full = jnp.dot(
            jnp.concatenate(parts, axis=0), order_ref[...], preferred_element_type=jnp.float32
        )
        for j in range(4):
            for k2 in range(PER):
                place = (0, (day ^ j) >> 1, middle ^ k2, (day ^ j) & 1)
                top = j * size + k2 * 16
                mean_ref[place] = full[top : top + 16, : 2 * MAXLAG + 1]
                top = top + PER * 16
                weighted_ref[place] = full[top : top + 16, : 2 * MAXLAG + 1]

    count = (len(refs) - 2) // 4
    for i in range(count):
        pl.when(pl.program_id(0) == i)(lambda i=i: one(refs[4 * i : 4 * i + 4]))


def order_groups(places, order, parts, outputs):
    whole = pl.BlockSpec(memory_space=pltpu.VMEM)
    count = len(parts) // 4
    shape = jax.ShapeDtypeStruct((4, 2, 4, 2, 16, 2 * MAXLAG + 1), jnp.float32)
    block = pl.BlockSpec(
        (1, 2, 4, 2, 16, 2 * MAXLAG + 1), lambda i, place: (place[2 + i], 0, 0, 0, 0, 0)
    )
    return pl.pallas_call(
        order_kernel,
        out_shape=(shape, shape),
        grid_spec=pltpu.PrefetchScalarGridSpec(
            num_scalar_prefetch=1,
            grid=(count,),
            in_specs=[whole] * (1 + len(parts)) + [pl.BlockSpec(memory_space=pl.ANY)] * len(outputs),
            out_specs=(block, block),
        ),
        input_output_aliases={2 + len(parts) + i: i for i in range(len(outputs))},
        compiler_params=pltpu.CompilerParams(vmem_limit_bytes=24 * 2**20),
        cost_estimate=pl.CostEstimate(flops=2**28, bytes_accessed=2**26, transcendentals=0),
        name="order_groups",
    )(places, order, *parts, *outputs)


def day_swap(x, k):
    return lax.ppermute(x, "day", [(i, i ^ k) for i in range(DAYS)])


def tile_swap(x, k):
    return lax.ppermute(x, "tile", [(i, i ^ k) for i in range(TILES)])


def turn(x, k):
    pairs = []
    for t in range(TILES):
        for xl in range(2):
            for core in range(2):
                to = (t & ~9) | ((xl ^ k) << 3) | core
                pairs.append((t * DAYS + 2 * xl + core, to * DAYS + 2 * ((t >> 3) & 1) + (t & 1)))
    return lax.ppermute(x, ("tile", "day"), pairs)


def on_device(source_spectra, receiver_spectra, valid_pairs):
    width = source_spectra.shape[3]
    tile, day = lax.axis_index("tile"), lax.axis_index("day")
    y, middle = tile >> 4, (tile >> 1) & 3
    shift = (((tile >> 3) & 1) * 2 + (tile & 1)) ^ day
    where = jnp.stack([y, middle, day, shift]).astype(jnp.int32)

    rec0 = jnp.transpose(receiver_spectra, (0, 2, 1, 3)).reshape(32 * PER, width)
    m0 = valid_pairs.reshape(PER, width).astype(jnp.bfloat16)
    rec0 = jnp.concatenate([rec0, jnp.pad(m0, ((0, 16 - PER), (0, 0)))], axis=0)
    rec2 = day_swap(rec0, 2)
    rec1 = day_swap(rec0, 1)
    rec3 = day_swap(rec2, 1)

    own = source_spectra.reshape(2 * PER, width)
    line = jnp.concatenate([own] + [tile_swap(own, 2 * k) for k in (1, 2, 3)], axis=0)
    pair = jnp.concatenate([line, day_swap(line, 1)], axis=0)
    second = jnp.concatenate([turn(pair, k) for k in range(2)], axis=0)
    groups = [second] + [tile_swap(second, 16 * k) for k in (1, 2, 3)]

    basis, order = half_basis(width), lag_order()
    receivers, masks = widen_receivers(where, (rec0, rec1, rec2, rec3))
    parts, earlier = {}, ()
    for k3 in (0, 1, 3, 2):
        mine = stack_group(groups[k3], receivers, masks[k3], basis, earlier)
        other = day_swap(mine, 2)
        far = day_swap(mine, 3) if k3 == 2 else day_swap(other, 1)
        parts[k3] = [mine, day_swap(mine, 1), other, far]
        earlier = (parts[0][0],)
    outputs = ()
    for k3 in (0, 1, 3, 2):
        places = jnp.stack([middle, day, y ^ k3]).astype(jnp.int32)
        outputs = order_groups(places, order, parts[k3], tuple(outputs))
    return tuple(out.reshape(TILES, 16, 2 * MAXLAG + 1) for out in outputs)


def solution(mesh):
    in_specs = (P("day", "tile", None, None), P("day", "tile", None, None), P("day", None, "tile"))
    out_specs = (P(None, "tile", None), P(None, "tile", None))
    return jax.shard_map(
        on_device, mesh=mesh, in_specs=in_specs, out_specs=out_specs, check_vma=False
    )
```

time: 71.9 us -> 63.8 us (0.89)
  starting transfers between devices: 39.7 us -> 33.6 us
  waiting for transfers between devices: 9.01 us -> 4.24 us
  Pallas kernels: 18 us -> 21.8 us
  local copies, waits for them, and re-layouts: 3.19 us -> 2.13 us
    ppermute x18 -> x16, starting transfers between devices: 22.8 us -> 14.4 us  [day_swap(): return lax.ppermute(x, 'day', [(i, i ^ k) for i in range(DAYS)])]
    ppermute x6, waiting for transfers between devices: 5.72 us -> 0.02 us  [tile_swap(): return lax.ppermute(x, 'tile', [(i, i ^ k) for i in range(TILES)])]
    ppermute x6, starting transfers between devices: 7.75 us -> 13.1 us  [tile_swap(): return lax.ppermute(x, 'tile', [(i, i ^ k) for i in range(TILES)])]
    pallas_call x1 -> x5, Pallas kernels: 3.8 us -> 8.64 us  [the longest x4 7.71 us: order_groups(): pl.pallas_call(order_kernel, out_shape=(shape, shape), grid_spec=pltpu.Pr...]
    ppermute x4 -> x2, waiting for transfers between devices: 0.01 us -> 3.29 us  [turn(): return lax.ppermute(x, ('tile', 'day'), pairs)]
    ppermute x4 -> x2, starting transfers between devices: 9.13 us -> 6.1 us  [turn(): return lax.ppermute(x, ('tile', 'day'), pairs)]
    ppermute x18 -> x16, waiting for transfers between devices: 3.27 us -> 0.93 us  [day_swap(): return lax.ppermute(x, 'day', [(i, i ^ k) for i in range(DAYS)])]
    unnamed x9, local copies, waits for them, and re-layouts: 1.86 us -> 0.03 us
  transfers between devices with their start and end apart: 28 -> 24, of which waited for: 4 -> 3; matrix products, arithmetic and copies ran while one was open for 4% -> 4% of each run, Pallas kernels for 20% -> 31%
where the time goes in v2:
time: 63.8 us; the launch traced here: 63.6 us
  starting transfers between devices  33.6 us (53%)
  Pallas kernels  21.8 us (34%)
  waiting for transfers between devices  4.24 us (7%)
  local copies, waits for them, and re-layouts  2.13 us (3%)
  other arithmetic  1.02 us (2%)
  between operations  0.77 us (1%)
    ppermute x16, starting transfers between devices, day_swap(): return lax.ppermute(x, 'day', [(i, i ^ k) for i in range(DAYS)])  14.4 us
    pallas_call x4, Pallas kernels, stack_group(): pl.pallas_call(stack_kernel, out_shape=jax.ShapeDtypeStruct((2, PER, 16,...  13.1 us
    ppermute x6, starting transfers between devices, tile_swap(): return lax.ppermute(x, 'tile', [(i, i ^ k) for i in range(TILES)])  13.1 us
    pallas_call x4, Pallas kernels, order_groups(): pl.pallas_call(order_kernel, out_shape=(shape, shape), grid_spec=pltpu.Pr...  7.71 us
    ppermute x2, starting transfers between devices, turn(): return lax.ppermute(x, ('tile', 'day'), pairs)  6.1 us
    ppermute x2, waiting for transfers between devices, turn(): return lax.ppermute(x, ('tile', 'day'), pairs)  3.29 us
  transfers between devices with their start and end apart: 24, of which 3 were waited for; matrix products, arithmetic and copies ran while one was open for 4% of the time, Pallas kernels for 31%

profile of v2, /device:TPU:1, one launch (start us, length us, event | category | flops | bytes accessed | tf_op | source)
XLA Modules:
  0.0 63.6 jit_solution(10449695786084854747)
XLA Ops:
  0.6 0.0 copy-start.1
  0.6 0.8 %reshape.18 = bf16[8,1024]{1,0:T(8,128)(2,1)S(1)} reshape(bf16[4,1,2,1024]{3,2,1,0:T(2,128)(2,1)} %param.5) | data formatting | bytes 32768 | tf_op jit(solution)/shard_map/reshape | solution.py:235
  1.5 6.9 %collective-permute-start.2 = (bf16[8,1024]{1,0:T(8,128)(2,1)S(1)}, bf16[8,1024]{1,0:T(8,128)(2,1)S(1)}, u32[]{:S(2)}, u32[]{:S(2)}) collective-permute-start(bf16[8,1024]{1,0:T(8,128)(2,1)S(1)} %reshape.18), channel_id=1, source_target_pairs={{0,24},{4,28},{8,16},{12,20},{16,8},{20,12},{24,0},{28,4},{32,56},... | collective-permute-start | bytes 49160 | tf_op jit(solution)/shard_map/ppermute | solution.py:208
  8.4 1.0 %collective-permute-start.1 = (bf16[8,1024]{1,0:T(8,128)(2,1)S(1)}, bf16[8,1024]{1,0:T(8,128)(2,1)S(1)}, u32[]{:S(2)}, u32[]{:S(2)}) collective-permute-start(bf16[8,1024]{1,0:T(8,128)(2,1)S(1)} %reshape.18), channel_id=1, source_target_pairs={{0,16},{4,20},{8,24},{12,28},{16,0},{20,4},{24,8},{28,12},{32,48},... | collective-permute-start | bytes 49160 | tf_op jit(solution)/shard_map/ppermute | solution.py:208
  9.4 1.2 %collective-permute-start = (bf16[8,1024]{1,0:T(8,128)(2,1)S(1)}, bf16[8,1024]{1,0:T(8,128)(2,1)S(1)}, u32[]{:S(2)}, u32[]{:S(2)}) collective-permute-start(bf16[8,1024]{1,0:T(8,128)(2,1)S(1)} %reshape.18), channel_id=1, source_target_pairs={{0,8},{4,12},{8,0},{12,4},{16,24},{20,28},{24,16},{28,20},{32,40},... | collective-permute-start | bytes 49160 | tf_op jit(solution)/shard_map/ppermute | solution.py:208
  10.6 0.8 %convert_element_type.8 = bf16[4,64,16]{1,2,0:T(8,128)(2,1)S(1)} convert(s32[4,64,16]{1,2,0:T(8,128)} %param.7) | non-fusion elementwise | flops 4096 | bytes 24576 | tf_op jit(solution)/shard_map/convert_element_type | solution.py:229
  11.3 0.1 copy.16
  11.4 0.1 convert_element_type.9
  11.6 1.0 %copy.15 = bf16[4,2,16,1024]{3,2,1,0:T(8,128)(2,1)S(1)} copy(bf16[4,2,16,1024]{3,1,2,0:T(2,128)(2,1)} %bitcast.22) | data formatting | bytes 524288 | tf_op jit(solution)/shard_map/transpose | solution.py:228
  12.6 1.3 %collective-permute-start.8 = (bf16[144,1024]{1,0:T(8,128)(2,1)S(1)}, bf16[144,1024]{1,0:T(8,128)(2,1)S(1)}, u32[]{:S(2)}, u32[]{:S(2)}) collective-permute-start(bf16[144,1024]{1,0:T(8,128)(2,1)S(1)} %fusion.1.rec0), channel_id=1, source_target_pairs={{0,2},{1,3},{2,0},{3,1},{4,6},{5,7},{6,4},{7,5},{8,10},{9,11},{10,... | collective-permute-start | bytes 884744 | tf_op jit(solution)/shard_map/ppermute | solution.py:204
  13.9 1.5 %collective-permute-start.7 = (bf16[144,1024]{1,0:T(8,128)(2,1)S(1)}, bf16[144,1024]{1,0:T(8,128)(2,1)S(1)}, u32[]{:S(2)}, u32[]{:S(2)}) collective-permute-start(bf16[144,1024]{1,0:T(8,128)(2,1)S(1)} %fusion.1.rec0), channel_id=1, source_target_pairs={{0,1},{1,0},{2,3},{3,2},{4,5},{5,4},{6,7},{7,6},{8,9},{9,8},{10,11... | collective-permute-start | bytes 884744 | tf_op jit(solution)/shard_map/ppermute | solution.py:204
  15.4 0.0 collective-permute-done.2
  15.4 0.0 collective-permute-done.1
  15.4 0.0 collective-permute-done
  15.5 1.6 %collective-permute-start.3 = (bf16[32,1024]{1,0:T(8,128)(2,1)S(1)}, bf16[32,1024]{1,0:T(8,128)(2,1)S(1)}, u32[]{:S(2)}, u32[]{:S(2)}) collective-permute-start(bf16[32,1024]{1,0:T(8,128)(2,1)S(1)} %pad_maximum_fusion), channel_id=1, source_target_pairs={{0,1},{1,0},{2,3},{3,2},{4,5},{5,4},{6,7},{7,6},{8,9},{9,8},{10,11... | collective-permute-start | bytes 196616 | tf_op jit(solution)/shard_map/ppermute | solution.py:204
  17.1 0.9 %collective-permute-done.3 = bf16[32,1024]{1,0:T(8,128)(2,1)S(1)} collective-permute-done((bf16[32,1024]{1,0:T(8,128)(2,1)S(1)}, bf16[32,1024]{1,0:T(8,128)(2,1)S(1)}, u32[]{:S(2)}, u32[]{:S(2)}) %collective-permute-start.3) | collective-permute-done | bytes 65568 | tf_op jit(solution)/shard_map/ppermute | solution.py:204
  18.0 2.9 %collective-permute-start.4 = (bf16[64,1024]{1,0:T(8,128)(2,1)S(1)}, bf16[64,1024]{1,0:T(8,128)(2,1)S(1)}, u32[]{:S(2)}, u32[]{:S(2)}) collective-permute-start(bf16[64,1024]{1,0:T(8,128)(2,1)S(1)} %constant_dynamic-update-slice_fusion), channel_id=1, source_target_pairs={{0,0},{1,4},{2,32},{3,36},{4,1},{5,5},{6,33},{7,37},{8,8},{9,12},{... | collective-permute-start | bytes 393224 | tf_op jit(solution)/shard_map/ppermute | solution.py:218
  20.9 0.1 pad_add_fusion.5
  21.0 3.2 %collective-permute-start.5 = (bf16[64,1024]{1,0:T(8,128)(2,1)S(1)}, bf16[64,1024]{1,0:T(8,128)(2,1)S(1)}, u32[]{:S(2)}, u32[]{:S(2)}) collective-permute-start(bf16[64,1024]{1,0:T(8,128)(2,1)S(1)} %constant_dynamic-update-slice_fusion), channel_id=1, source_target_pairs={{0,32},{1,36},{2,0},{3,4},{4,33},{5,37},{6,1},{7,5},{8,40},{9,44},... | collective-permute-start | bytes 393224 | tf_op jit(solution)/shard_map/ppermute | solution.py:218
  24.2 0.0 collective-permute-done.8.rec2
  24.2 0.0 collective-permute-start.9
  24.2 0.1 pad_add_fusion.2.where_ref
  24.3 0.3 collective-permute-done.4
  24.6 3.0 %collective-permute-done.5 = bf16[64,1024]{1,0:T(8,128)(2,1)S(1)} collective-permute-done((bf16[64,1024]{1,0:T(8,128)(2,1)S(1)}, bf16[64,1024]{1,0:T(8,128)(2,1)S(1)}, u32[]{:S(2)}, u32[]{:S(2)}) %collective-permute-start.5) | collective-permute-done | bytes 131104 | tf_op jit(solution)/shard_map/ppermute | solution.py:218
  27.6 1.4 %collective-permute-start.17 = (bf16[128,1024]{1,0:T(8,128)(2,1)S(1)}, bf16[128,1024]{1,0:T(8,128)(2,1)S(1)}, u32[]{:S(2)}, u32[]{:S(2)}) collective-permute-start(bf16[128,1024]{1,0:T(8,128)(2,1)S(1)} %constant_dynamic-update-slice_fusion.5.src_ref), channel_id=1, source_target_pairs={{0,64},{4,68},{8,72},{12,76},{16,80},{20,84},{24,88},{28,92},{32,9... | collective-permute-start | bytes 786440 | tf_op jit(solution)/shard_map/ppermute | solution.py:208
  29.0 1.9 %collective-permute-start.13 = (bf16[128,1024]{1,0:T(8,128)(2,1)S(1)}, bf16[128,1024]{1,0:T(8,128)(2,1)S(1)}, u32[]{:S(2)}, u32[]{:S(2)}) collective-permute-start(bf16[128,1024]{1,0:T(8,128)(2,1)S(1)} %constant_dynamic-update-slice_fusion.5.src_ref), channel_id=1, source_target_pairs={{0,192},{4,196},{8,200},{12,204},{16,208},{20,212},{24,216},{28,22... | collective-permute-start | bytes 786440 | tf_op jit(solution)/shard_map/ppermute | solution.py:208
  30.9 0.7 %collective-permute-start.6 = (bf16[128,1024]{1,0:T(8,128)(2,1)S(1)}, bf16[128,1024]{1,0:T(8,128)(2,1)S(1)}, u32[]{:S(2)}, u32[]{:S(2)}) collective-permute-start(bf16[128,1024]{1,0:T(8,128)(2,1)S(1)} %constant_dynamic-update-slice_fusion.5.src_ref), channel_id=1, source_target_pairs={{0,128},{4,132},{8,136},{12,140},{16,144},{20,148},{24,152},{28,15... | collective-permute-start | bytes 786440 | tf_op jit(solution)/shard_map/ppermute | solution.py:208
  31.6 0.0 collective-permute-done.7.rec1
  31.6 0.0 collective-permute-done.9.rec3
  31.6 0.9 %widen_receivers.1 = (f32[16,2,16,1024]{3,2,1,0:T(8,128)S(1)}, f32[4,4,16,128]{3,2,1,0:T(8,128)S(1)}) custom-call(s32[4]{0:T(128)S(1)} %pad_add_fusion.2.where_ref, bf16[144,1024]{1,0:T(8,128)(2,1)S(1)} %fusion.1.rec0, bf16[144,1024]{1,0:T(8,128)(2,1)S(1)} %collective-permute-done.7.rec1, bf16[144,1024]{1,0:T(8,128)(2,1)S(1)} %collective-permute-done.8.rec2, ...), custom_call_target="tpu_custom_call" | custom-call | tf_op jit(solution)/shard_map/widen_receivers/pallas_call | solution.py:67
  32.6 3.3 %stack_group.4.refs_0_ = bf16[2,4,16,512]{3,2,1,0:T(8,128)(2,1)S(1)} custom-call(bf16[128,1024]{1,0:T(8,128)(2,1)S(1)} %constant_dynamic-update-slice_fusion.5.src_ref, f32[16,2,16,1024]{3,2,1,0:T(8,128)S(1)} %get-tuple-element.12.rec_ref, f32[4,16,128]{2,1,0:T(8,128)S(1)} %get-tuple-element.26.mask_ref, bf16[1024,512]{1,0:T(8,128)(2,1)S(1)} %copy-done.1), custom_call_target="tpu_custom_call" | custom-call | flops 2147483648 | bytes 3145728 | tf_op jit(solution)/shard_map/stack_group/pallas_call | solution.py:138
  35.9 0.0 collective-permute-done.17.src_ref
  35.9 3.3 %stack_group.7.refs_0_ = bf16[2,4,16,512]{3,2,1,0:T(8,128)(2,1)S(1)} custom-call(bf16[128,1024]{1,0:T(8,128)(2,1)S(1)} %collective-permute-done.17.src_ref, f32[16,2,16,1024]{3,2,1,0:T(8,128)S(1)} %get-tuple-element.12.rec_ref, f32[4,16,128]{2,1,0:T(8,128)S(1)} %get-tuple-element.24.mask_ref, bf16[1024,512]{1,0:T(8,128)(2,1)S(1)} %copy-done.1, ...), custom_call_target="tpu_custom_call" | custom-call | flops 2147483648 | bytes 3145728 | tf_op jit(solution)/shard_map/stack_group/pallas_call | solution.py:138
  39.2 2.5 %collective-permute-start.19 = (bf16[2,4,16,512]{3,2,1,0:T(8,128)(2,1)S(1)}, bf16[2,4,16,512]{3,2,1,0:T(8,128)(2,1)S(1)}, u32[]{:S(2)}, u32[]{:S(2)}) collective-permute-start(bf16[2,4,16,512]{3,2,1,0:T(8,128)(2,1)S(1)} %stack_group.7.refs_0_), channel_id=1, source_target_pairs={{0,2},{1,3},{2,0},{3,1},{4,6},{5,7},{6,4},{7,5},{8,10},{9,11},{10,... | collective-permute-start | bytes 393224 | tf_op jit(solution)/shard_map/ppermute | solution.py:204
  41.7 2.2 %collective-permute-start.18 = (bf16[2,4,16,512]{3,2,1,0:T(8,128)(2,1)S(1)}, bf16[2,4,16,512]{3,2,1,0:T(8,128)(2,1)S(1)}, u32[]{:S(2)}, u32[]{:S(2)}) collective-permute-start(bf16[2,4,16,512]{3,2,1,0:T(8,128)(2,1)S(1)} %stack_group.7.refs_0_), channel_id=1, source_target_pairs={{0,1},{1,0},{2,3},{3,2},{4,5},{5,4},{6,7},{7,6},{8,9},{9,8},{10,11... | collective-permute-start | bytes 393224 | tf_op jit(solution)/shard_map/ppermute | solution.py:204
  43.9 0.0 collective-permute-start.22
  43.9 0.0 collective-permute-done.13.src_ref
  43.9 0.3 collective-permute-start.21
  44.3 3.3 %stack_group.6.refs_0_ = bf16[2,4,16,512]{3,2,1,0:T(8,128)(2,1)S(1)} custom-call(bf16[128,1024]{1,0:T(8,128)(2,1)S(1)} %collective-permute-done.13.src_ref, f32[16,2,16,1024]{3,2,1,0:T(8,128)S(1)} %get-tuple-element.12.rec_ref, f32[4,16,128]{2,1,0:T(8,128)S(1)} %get-tuple-element.25.mask_ref, bf16[1024,512]{1,0:T(8,128)(2,1)S(1)} %copy-done.1, ...), custom_call_target="tpu_custom_call" | custom-call | flops 2147483648 | bytes 3145728 | tf_op jit(solution)/shard_map/stack_group/pallas_call | solution.py:138
  47.5 0.0 collective-permute-done.6.src_ref
  47.6 1.5 %collective-permute-start.15 = (bf16[2,4,16,512]{3,2,1,0:T(8,128)(2,1)S(1)}, bf16[2,4,16,512]{3,2,1,0:T(8,128)(2,1)S(1)}, u32[]{:S(2)}, u32[]{:S(2)}) collective-permute-start(bf16[2,4,16,512]{3,2,1,0:T(8,128)(2,1)S(1)} %stack_group.6.refs_0_), channel_id=1, source_target_pairs={{0,2},{1,3},{2,0},{3,1},{4,6},{5,7},{6,4},{7,5},{8,10},{9,11},{10,... | collective-permute-start | bytes 393224 | tf_op jit(solution)/shard_map/ppermute | solution.py:204
  49.1 0.0 collective-permute-done.19.refs_2_
  49.1 0.5 collective-permute-start.20
  49.6 0.0 collective-permute-done.22.refs_2_
  49.6 0.3 collective-permute-start.23
  49.9 3.3 %stack_group.5.refs_0_ = bf16[2,4,16,512]{3,2,1,0:T(8,128)(2,1)S(1)} custom-call(bf16[128,1024]{1,0:T(8,128)(2,1)S(1)} %collective-permute-done.6.src_ref, f32[16,2,16,1024]{3,2,1,0:T(8,128)S(1)} %get-tuple-element.12.rec_ref, f32[4,16,128]{2,1,0:T(8,128)S(1)} %get-tuple-element.27.mask_ref, bf16[1024,512]{1,0:T(8,128)(2,1)S(1)} %copy-done.1, ...), custom_call_target="tpu_custom_call" | custom-call | flops 2147483648 | bytes 3145728 | tf_op jit(solution)/shard_map/stack_group/pallas_call | solution.py:138
  53.1 0.0 collective-permute-done.18.refs_1_
  53.1 0.3 collective-permute-start.14
  53.5 0.0 collective-permute-done.15.refs_2_
  53.5 1.5 %collective-permute-start.12 = (bf16[2,4,16,512]{3,2,1,0:T(8,128)(2,1)S(1)}, bf16[2,4,16,512]{3,2,1,0:T(8,128)(2,1)S(1)}, u32[]{:S(2)}, u32[]{:S(2)}) collective-permute-start(bf16[2,4,16,512]{3,2,1,0:T(8,128)(2,1)S(1)} %stack_group.5.refs_0_), channel_id=1, source_target_pairs={{0,3},{1,2},{2,1},{3,0},{4,7},{5,6},{6,5},{7,4},{8,11},{9,10},{10,... | collective-permute-start | bytes 393224 | tf_op jit(solution)/shard_map/ppermute | solution.py:204
  55.0 0.0 collective-permute-done.21.refs_1_
  55.0 0.1 collective-permute-start.11
  55.1 0.0 collective-permute-done.20.refs_3_
  55.1 0.5 collective-permute-start.10
  55.6 0.0 collective-permute-done.23.refs_3_
  55.7 0.1 collective-permute-start.16
  55.7 0.1 pad_add_fusion.4
  55.8 1.9 %order_groups.4 = (f32[4,2,4,2,16,401]{5,4,3,2,1,0:T(8,128)}, f32[4,2,4,2,16,401]{5,4,3,2,1,0:T(8,128)}) custom-call(s32[3]{0:T(128)S(1)} %get-tuple-element.22.place_ref, bf16[512,512]{1,0:T(8,128)(2,1)S(1)} %copy-done, bf16[2,4,16,512]{3,2,1,0:T(8,128)(2,1)S(1)} %stack_group.4.refs_0_, bf16[2,4,16,512]{3,2,1,0:T(8,128)(2,1)S(1)} %collective-permute-done.21.refs_1_, ...), custom_call_target="tpu_custom_call" | custom-call | flops 268435456 | bytes 67108864 | tf_op jit(solution)/shard_map/order_groups/pallas_call | solution.py:187
  57.7 1.9 %order_groups.5 = (f32[4,2,4,2,16,401]{5,4,3,2,1,0:T(8,128)}, f32[4,2,4,2,16,401]{5,4,3,2,1,0:T(8,128)}) custom-call(s32[3]{0:T(128)S(1)} %get-tuple-element.28.place_ref, bf16[512,512]{1,0:T(8,128)(2,1)S(1)} %copy-done, bf16[2,4,16,512]{3,2,1,0:T(8,128)(2,1)S(1)} %stack_group.7.refs_0_, ...), custom_call_target="tpu_custom_call", output_to_operand_aliasing={{0}: (6, {}), {1}: (7, {})} | custom-call | flops 268435456 | bytes 67108864 | tf_op jit(solution)/shard_map/order_groups/pallas_call | solution.py:187
  59.7 0.0 collective-permute-done.14.refs_1_
  59.7 0.0 collective-permute-done.16.refs_3_
  59.7 1.9 %order_groups.6 = (f32[4,2,4,2,16,401]{5,4,3,2,1,0:T(8,128)}, f32[4,2,4,2,16,401]{5,4,3,2,1,0:T(8,128)}) custom-call(s32[3]{0:T(128)S(1)} %get-tuple-element.29.place_ref, bf16[512,512]{1,0:T(8,128)(2,1)S(1)} %copy-done, bf16[2,4,16,512]{3,2,1,0:T(8,128)(2,1)S(1)} %stack_group.6.refs_0_, ...), custom_call_target="tpu_custom_call", output_to_operand_aliasing={{0}: (6, {}), {1}: (7, {})} | custom-call | flops 268435456 | bytes 67108864 | tf_op jit(solution)/shard_map/order_groups/pallas_call | solution.py:187
  61.6 0.0 collective-permute-done.12.refs_3_
  61.6 1.9 %order_groups.7 = (f32[4,2,4,2,16,401]{5,4,3,2,1,0:T(8,128)}, f32[4,2,4,2,16,401]{5,4,3,2,1,0:T(8,128)}) custom-call(s32[3]{0:T(128)S(1)} %get-tuple-element.30.place_ref, bf16[512,512]{1,0:T(8,128)(2,1)S(1)} %copy-done, bf16[2,4,16,512]{3,2,1,0:T(8,128)(2,1)S(1)} %stack_group.5.refs_0_, ...), custom_call_target="tpu_custom_call", output_to_operand_aliasing={{0}: (6, {}), {1}: (7, {})} | custom-call | flops 268435456 | bytes 67108864 | tf_op jit(solution)/shard_map/order_groups/pallas_call | solution.py:187
  (15 shorter events, 0.1 us)
Async XLA Ops:
  0.6 32.0 %copy-start.1 = (bf16[1024,512]{1,0:T(8,128)(2,1)S(1)}, bf16[1024,512]{1,0:T(8,128)(2,1)}, u32[]{:S(2)}) copy-start(bf16[1024,512]{1,0:T(8,128)(2,1)} %constant.24.clone.basis_ref) | copy-start | bytes 3145732
  1.5 14.0 %collective-permute-start.2 = (bf16[8,1024]{1,0:T(8,128)(2,1)S(1)}, bf16[8,1024]{1,0:T(8,128)(2,1)S(1)}, u32[]{:S(2)}, u32[]{:S(2)}) collective-permute-start(bf16[8,1024]{1,0:T(8,128)(2,1)S(1)} %reshape.18), channel_id=1, source_target_pairs={{0,24},{4,28},{8,16},{12,20},{16,8},{20,12},{24,0},{28,4},{32,56},... | collective-permute-start | bytes 49160 | tf_op jit(solution)/shard_map/ppermute | solution.py:208
  8.4 7.0 %collective-permute-start.1 = (bf16[8,1024]{1,0:T(8,128)(2,1)S(1)}, bf16[8,1024]{1,0:T(8,128)(2,1)S(1)}, u32[]{:S(2)}, u32[]{:S(2)}) collective-permute-start(bf16[8,1024]{1,0:T(8,128)(2,1)S(1)} %reshape.18), channel_id=1, source_target_pairs={{0,16},{4,20},{8,24},{12,28},{16,0},{20,4},{24,8},{28,12},{32,48},... | collective-permute-start | bytes 49160 | tf_op jit(solution)/shard_map/ppermute | solution.py:208
  9.4 6.1 %collective-permute-start = (bf16[8,1024]{1,0:T(8,128)(2,1)S(1)}, bf16[8,1024]{1,0:T(8,128)(2,1)S(1)}, u32[]{:S(2)}, u32[]{:S(2)}) collective-permute-start(bf16[8,1024]{1,0:T(8,128)(2,1)S(1)} %reshape.18), channel_id=1, source_target_pairs={{0,8},{4,12},{8,0},{12,4},{16,24},{20,28},{24,16},{28,20},{32,40},... | collective-permute-start | bytes 49160 | tf_op jit(solution)/shard_map/ppermute | solution.py:208
  12.6 11.6 %collective-permute-start.8 = (bf16[144,1024]{1,0:T(8,128)(2,1)S(1)}, bf16[144,1024]{1,0:T(8,128)(2,1)S(1)}, u32[]{:S(2)}, u32[]{:S(2)}) collective-permute-start(bf16[144,1024]{1,0:T(8,128)(2,1)S(1)} %fusion.1.rec0), channel_id=1, source_target_pairs={{0,2},{1,3},{2,0},{3,1},{4,6},{5,7},{6,4},{7,5},{8,10},{9,11},{10,... | collective-permute-start | bytes 884744 | tf_op jit(solution)/shard_map/ppermute | solution.py:204
  13.9 17.7 %collective-permute-start.7 = (bf16[144,1024]{1,0:T(8,128)(2,1)S(1)}, bf16[144,1024]{1,0:T(8,128)(2,1)S(1)}, u32[]{:S(2)}, u32[]{:S(2)}) collective-permute-start(bf16[144,1024]{1,0:T(8,128)(2,1)S(1)} %fusion.1.rec0), channel_id=1, source_target_pairs={{0,1},{1,0},{2,3},{3,2},{4,5},{5,4},{6,7},{7,6},{8,9},{9,8},{10,11... | collective-permute-start | bytes 884744 | tf_op jit(solution)/shard_map/ppermute | solution.py:204
  15.5 2.5 %collective-permute-start.3 = (bf16[32,1024]{1,0:T(8,128)(2,1)S(1)}, bf16[32,1024]{1,0:T(8,128)(2,1)S(1)}, u32[]{:S(2)}, u32[]{:S(2)}) collective-permute-start(bf16[32,1024]{1,0:T(8,128)(2,1)S(1)} %pad_maximum_fusion), channel_id=1, source_target_pairs={{0,1},{1,0},{2,3},{3,2},{4,5},{5,4},{6,7},{7,6},{8,9},{9,8},{10,11... | collective-permute-start | bytes 196616 | tf_op jit(solution)/shard_map/ppermute | solution.py:204
  18.0 6.6 %collective-permute-start.4 = (bf16[64,1024]{1,0:T(8,128)(2,1)S(1)}, bf16[64,1024]{1,0:T(8,128)(2,1)S(1)}, u32[]{:S(2)}, u32[]{:S(2)}) collective-permute-start(bf16[64,1024]{1,0:T(8,128)(2,1)S(1)} %constant_dynamic-update-slice_fusion), channel_id=1, source_target_pairs={{0,0},{1,4},{2,32},{3,36},{4,1},{5,5},{6,33},{7,37},{8,8},{9,12},{... | collective-permute-start | bytes 393224 | tf_op jit(solution)/shard_map/ppermute | solution.py:218
  21.0 6.6 %collective-permute-start.5 = (bf16[64,1024]{1,0:T(8,128)(2,1)S(1)}, bf16[64,1024]{1,0:T(8,128)(2,1)S(1)}, u32[]{:S(2)}, u32[]{:S(2)}) collective-permute-start(bf16[64,1024]{1,0:T(8,128)(2,1)S(1)} %constant_dynamic-update-slice_fusion), channel_id=1, source_target_pairs={{0,32},{1,36},{2,0},{3,4},{4,33},{5,37},{6,1},{7,5},{8,40},{9,44},... | collective-permute-start | bytes 393224 | tf_op jit(solution)/shard_map/ppermute | solution.py:218
  24.2 7.4 %collective-permute-start.9 = (bf16[144,1024]{1,0:T(8,128)(2,1)S(1)}, bf16[144,1024]{1,0:T(8,128)(2,1)S(1)}, u32[]{:S(2)}, u32[]{:S(2)}) collective-permute-start(bf16[144,1024]{1,0:T(8,128)(2,1)S(1)} %collective-permute-done.8.rec2), channel_id=1, source_target_pairs={{0,1},{1,0},{2,3},{3,2},{4,5},{5,4},{6,7},{7,6},{8,9},{9,8},{10,11... | collective-permute-start | bytes 884744 | tf_op jit(solution)/shard_map/ppermute | solution.py:204
  27.6 8.3 %collective-permute-start.17 = (bf16[128,1024]{1,0:T(8,128)(2,1)S(1)}, bf16[128,1024]{1,0:T(8,128)(2,1)S(1)}, u32[]{:S(2)}, u32[]{:S(2)}) collective-permute-start(bf16[128,1024]{1,0:T(8,128)(2,1)S(1)} %constant_dynamic-update-slice_fusion.5.src_ref), channel_id=1, source_target_pairs={{0,64},{4,68},{8,72},{12,76},{16,80},{20,84},{24,88},{28,92},{32,9... | collective-permute-start | bytes 786440 | tf_op jit(solution)/shard_map/ppermute | solution.py:208
  29.0 15.0 %collective-permute-start.13 = (bf16[128,1024]{1,0:T(8,128)(2,1)S(1)}, bf16[128,1024]{1,0:T(8,128)(2,1)S(1)}, u32[]{:S(2)}, u32[]{:S(2)}) collective-permute-start(bf16[128,1024]{1,0:T(8,128)(2,1)S(1)} %constant_dynamic-update-slice_fusion.5.src_ref), channel_id=1, source_target_pairs={{0,192},{4,196},{8,200},{12,204},{16,208},{20,212},{24,216},{28,22... | collective-permute-start | bytes 786440 | tf_op jit(solution)/shard_map/ppermute | solution.py:208
  30.9 16.7 %collective-permute-start.6 = (bf16[128,1024]{1,0:T(8,128)(2,1)S(1)}, bf16[128,1024]{1,0:T(8,128)(2,1)S(1)}, u32[]{:S(2)}, u32[]{:S(2)}) collective-permute-start(bf16[128,1024]{1,0:T(8,128)(2,1)S(1)} %constant_dynamic-update-slice_fusion.5.src_ref), channel_id=1, source_target_pairs={{0,128},{4,132},{8,136},{12,140},{16,144},{20,148},{24,152},{28,15... | collective-permute-start | bytes 786440 | tf_op jit(solution)/shard_map/ppermute | solution.py:208
  39.2 9.9 %collective-permute-start.19 = (bf16[2,4,16,512]{3,2,1,0:T(8,128)(2,1)S(1)}, bf16[2,4,16,512]{3,2,1,0:T(8,128)(2,1)S(1)}, u32[]{:S(2)}, u32[]{:S(2)}) collective-permute-start(bf16[2,4,16,512]{3,2,1,0:T(8,128)(2,1)S(1)} %stack_group.7.refs_0_), channel_id=1, source_target_pairs={{0,2},{1,3},{2,0},{3,1},{4,6},{5,7},{6,4},{7,5},{8,10},{9,11},{10,... | collective-permute-start | bytes 393224 | tf_op jit(solution)/shard_map/ppermute | solution.py:204
  41.7 11.4 %collective-permute-start.18 = (bf16[2,4,16,512]{3,2,1,0:T(8,128)(2,1)S(1)}, bf16[2,4,16,512]{3,2,1,0:T(8,128)(2,1)S(1)}, u32[]{:S(2)}, u32[]{:S(2)}) collective-permute-start(bf16[2,4,16,512]{3,2,1,0:T(8,128)(2,1)S(1)} %stack_group.7.refs_0_), channel_id=1, source_target_pairs={{0,1},{1,0},{2,3},{3,2},{4,5},{5,4},{6,7},{7,6},{8,9},{9,8},{10,11... | collective-permute-start | bytes 393224 | tf_op jit(solution)/shard_map/ppermute | solution.py:204
  43.9 5.7 %collective-permute-start.22 = (bf16[2,4,16,512]{3,2,1,0:T(8,128)(2,1)S(1)}, bf16[2,4,16,512]{3,2,1,0:T(8,128)(2,1)S(1)}, u32[]{:S(2)}, u32[]{:S(2)}) collective-permute-start(bf16[2,4,16,512]{3,2,1,0:T(8,128)(2,1)S(1)} %stack_group.4.refs_0_), channel_id=1, source_target_pairs={{0,2},{1,3},{2,0},{3,1},{4,6},{5,7},{6,4},{7,5},{8,10},{9,11},{10,... | collective-permute-start | bytes 393224 | tf_op jit(solution)/shard_map/ppermute | solution.py:204
  43.9 11.1 %collective-permute-start.21 = (bf16[2,4,16,512]{3,2,1,0:T(8,128)(2,1)S(1)}, bf16[2,4,16,512]{3,2,1,0:T(8,128)(2,1)S(1)}, u32[]{:S(2)}, u32[]{:S(2)}) collective-permute-start(bf16[2,4,16,512]{3,2,1,0:T(8,128)(2,1)S(1)} %stack_group.4.refs_0_), channel_id=1, source_target_pairs={{0,1},{1,0},{2,3},{3,2},{4,5},{5,4},{6,7},{7,6},{8,9},{9,8},{10,11... | collective-permute-start | bytes 393224 | tf_op jit(solution)/shard_map/ppermute | solution.py:204
  47.6 5.9 %collective-permute-start.15 = (bf16[2,4,16,512]{3,2,1,0:T(8,128)(2,1)S(1)}, bf16[2,4,16,512]{3,2,1,0:T(8,128)(2,1)S(1)}, u32[]{:S(2)}, u32[]{:S(2)}) collective-permute-start(bf16[2,4,16,512]{3,2,1,0:T(8,128)(2,1)S(1)} %stack_group.6.refs_0_), channel_id=1, source_target_pairs={{0,2},{1,3},{2,0},{3,1},{4,6},{5,7},{6,4},{7,5},{8,10},{9,11},{10,... | collective-permute-start | bytes 393224 | tf_op jit(solution)/shard_map/ppermute | solution.py:204
  49.1 6.0 %collective-permute-start.20 = (bf16[2,4,16,512]{3,2,1,0:T(8,128)(2,1)S(1)}, bf16[2,4,16,512]{3,2,1,0:T(8,128)(2,1)S(1)}, u32[]{:S(2)}, u32[]{:S(2)}) collective-permute-start(bf16[2,4,16,512]{3,2,1,0:T(8,128)(2,1)S(1)} %collective-permute-done.19.refs_2_), channel_id=1, source_target_pairs={{0,1},{1,0},{2,3},{3,2},{4,5},{5,4},{6,7},{7,6},{8,9},{9,8},{10,11... | collective-permute-start | bytes 393224 | tf_op jit(solution)/shard_map/ppermute | solution.py:204
  49.6 6.1 %collective-permute-start.23 = (bf16[2,4,16,512]{3,2,1,0:T(8,128)(2,1)S(1)}, bf16[2,4,16,512]{3,2,1,0:T(8,128)(2,1)S(1)}, u32[]{:S(2)}, u32[]{:S(2)}) collective-permute-start(bf16[2,4,16,512]{3,2,1,0:T(8,128)(2,1)S(1)} %collective-permute-done.22.refs_2_), channel_id=1, source_target_pairs={{0,1},{1,0},{2,3},{3,2},{4,5},{5,4},{6,7},{7,6},{8,9},{9,8},{10,11... | collective-permute-start | bytes 393224 | tf_op jit(solution)/shard_map/ppermute | solution.py:204
  49.8 6.0 %copy-start = (bf16[512,512]{1,0:T(8,128)(2,1)S(1)}, bf16[512,512]{1,0:T(8,128)(2,1)}, u32[]{:S(2)}) copy-start(bf16[512,512]{1,0:T(8,128)(2,1)} %constant.25.clone.order_ref) | copy-start | bytes 1572868
  53.1 6.5 %collective-permute-start.14 = (bf16[2,4,16,512]{3,2,1,0:T(8,128)(2,1)S(1)}, bf16[2,4,16,512]{3,2,1,0:T(8,128)(2,1)S(1)}, u32[]{:S(2)}, u32[]{:S(2)}) collective-permute-start(bf16[2,4,16,512]{3,2,1,0:T(8,128)(2,1)S(1)} %stack_group.6.refs_0_), channel_id=1, source_target_pairs={{0,1},{1,0},{2,3},{3,2},{4,5},{5,4},{6,7},{7,6},{8,9},{9,8},{10,11... | collective-permute-start | bytes 393224 | tf_op jit(solution)/shard_map/ppermute | solution.py:204
  53.5 8.1 %collective-permute-start.12 = (bf16[2,4,16,512]{3,2,1,0:T(8,128)(2,1)S(1)}, bf16[2,4,16,512]{3,2,1,0:T(8,128)(2,1)S(1)}, u32[]{:S(2)}, u32[]{:S(2)}) collective-permute-start(bf16[2,4,16,512]{3,2,1,0:T(8,128)(2,1)S(1)} %stack_group.5.refs_0_), channel_id=1, source_target_pairs={{0,3},{1,2},{2,1},{3,0},{4,7},{5,6},{6,5},{7,4},{8,11},{9,10},{10,... | collective-permute-start | bytes 393224 | tf_op jit(solution)/shard_map/ppermute | solution.py:204
  55.0 6.6 %collective-permute-start.11 = (bf16[2,4,16,512]{3,2,1,0:T(8,128)(2,1)S(1)}, bf16[2,4,16,512]{3,2,1,0:T(8,128)(2,1)S(1)}, u32[]{:S(2)}, u32[]{:S(2)}) collective-permute-start(bf16[2,4,16,512]{3,2,1,0:T(8,128)(2,1)S(1)} %stack_group.5.refs_0_), channel_id=1, source_target_pairs={{0,2},{1,3},{2,0},{3,1},{4,6},{5,7},{6,4},{7,5},{8,10},{9,11},{10,... | collective-permute-start | bytes 393224 | tf_op jit(solution)/shard_map/ppermute | solution.py:204
  55.1 6.5 %collective-permute-start.10 = (bf16[2,4,16,512]{3,2,1,0:T(8,128)(2,1)S(1)}, bf16[2,4,16,512]{3,2,1,0:T(8,128)(2,1)S(1)}, u32[]{:S(2)}, u32[]{:S(2)}) collective-permute-start(bf16[2,4,16,512]{3,2,1,0:T(8,128)(2,1)S(1)} %stack_group.5.refs_0_), channel_id=1, source_target_pairs={{0,1},{1,0},{2,3},{3,2},{4,5},{5,4},{6,7},{7,6},{8,9},{9,8},{10,11... | collective-permute-start | bytes 393224 | tf_op jit(solution)/shard_map/ppermute | solution.py:204
  55.7 4.0 %collective-permute-start.16 = (bf16[2,4,16,512]{3,2,1,0:T(8,128)(2,1)S(1)}, bf16[2,4,16,512]{3,2,1,0:T(8,128)(2,1)S(1)}, u32[]{:S(2)}, u32[]{:S(2)}) collective-permute-start(bf16[2,4,16,512]{3,2,1,0:T(8,128)(2,1)S(1)} %collective-permute-done.15.refs_2_), channel_id=1, source_target_pairs={{0,1},{1,0},{2,3},{3,2},{4,5},{5,4},{6,7},{7,6},{8,9},{9,8},{10,11... | collective-permute-start | bytes 393224 | tf_op jit(solution)/shard_map/ppermute | solution.py:204

commit v3 on v2

v3 whole, which is shorter than its diff:
```python
import functools
import math

import jax
import jax.numpy as jnp
import numpy as np
from jax import lax
from jax.experimental import pallas as pl
from jax.experimental.pallas import tpu as pltpu
from jax.sharding import PartitionSpec as P

MAXLAG = 200
HALF = 256
TILES, DAYS = 64, 4

PER = 4


def fold_basis(frequency_count):
    samples, half, lanes = 2 * frequency_count, frequency_count // 2, HALF // 2
    even, odd = np.arange(0, MAXLAG + 1, 2)[None, :], np.arange(1, MAXLAG + 1, 2)[None, :]
    freq = np.arange(half)[:, None]
    tables = np.zeros((2, half, HALF))

    def angles(f, lag):
        return ((f * lag) % samples) * (2.0 * math.pi / samples)

    tables[0, :, : even.size] = np.cos(angles(freq, even))
    tables[0, :, lanes : lanes + odd.size] = np.sin(angles(freq, odd))
    tables[1, :, : odd.size] = np.cos(angles(freq, odd))
    tables[1, :, lanes : lanes + even.size] = np.sin(angles(freq, even))
    tables[0, 0, : even.size] = np.cos(angles(half, even))[0]
    tables[0, 0, lanes : lanes + odd.size] = np.sin(angles(half, odd))[0]
    tables[1, 0, : odd.size] = 0.5
    tables[1, 0, lanes - 1] = 0.5
    return jnp.asarray(tables * frequency_count ** (-0.5), jnp.bfloat16)


def reversal(half):
    table = np.zeros((half, half))
    table[0, 0] = 1.0
    table[np.arange(half - 1, 0, -1), np.arange(1, half)] = 1.0
    return jnp.asarray(table, jnp.bfloat16)


def lag_order():
    table = np.zeros((2 * HALF, 2 * HALF))
    lag = np.arange(MAXLAG + 1)
    lane = lag % 2 * (HALF // 2) + lag // 2
    table[lane, MAXLAG + lag] = 1.0
    table[HALF + lane[1:], MAXLAG - lag[1:]] = 1.0
    return jnp.asarray(table, jnp.bfloat16)


def fold_order(x, flip):
    half = x.shape[-1] // 2
    upper = jnp.dot(x[:, half:], flip, preferred_element_type=jnp.float32)
    return x[:, :half].astype(jnp.float32), upper


def widen_kernel(where_ref, rec0, rec1, rec2, rec3, flip_ref, out_ref, mask_ref, rows_ref):
    y, middle, day, shift = (where_ref[i] for i in range(4))
    width = out_ref.shape[-1]
    size, half = 32 * PER, width // 2
    for j, rec in enumerate((rec0, rec1, rec2, rec3)):
        k = j ^ shift
        lower, upper = fold_order(rec[:size], flip_ref[...])
        out_ref[pl.ds(k * PER, PER), :, :, :half] = lower.reshape(PER, 2, 16, half)
        out_ref[pl.ds(k * PER, PER), :, :, half:] = upper.reshape(PER, 2, 16, half)
        rows_ref[k] = rec[size:]
    rows = rows_ref[...].reshape(64, width)
    gap = lax.broadcasted_iota(jnp.int32, (16, width), 1) - lax.broadcasted_iota(jnp.int32, (16, width), 0)
    for k3 in range(4):
        picks = []
        for k2 in range(PER):
            source = source_index(y ^ k3, day, middle ^ k2)
            picks.append(jnp.where(gap == source * 16, 1.0, 0.0).astype(jnp.bfloat16))
        chosen = lax.dot_general(
            jnp.concatenate(picks, axis=0), rows, (((1,), (1,)), ((), ())),
            preferred_element_type=jnp.float32,
        )
        mask_ref[k3, :, :, :64] = chosen.reshape(PER, 16, 64)


def source_index(y, day, middle):
    return (y << 4) | ((day >> 1) << 3) | (middle << 1) | (day & 1)


def widen_receivers(where, receivers, flip):
    whole = pl.BlockSpec(memory_space=pltpu.VMEM)
    width = receivers[0].shape[-1]
    return pl.pallas_call(
        widen_kernel,
        out_shape=(
            jax.ShapeDtypeStruct((4 * PER, 2, 16, width), jnp.float32),
            jax.ShapeDtypeStruct((4, PER, 16, 128), jnp.float32),
        ),
        in_specs=[pl.BlockSpec(memory_space=pltpu.SMEM)] + [whole] * 5,
        out_specs=(whole, whole),
        scratch_shapes=[pltpu.VMEM((4, 16, width), jnp.bfloat16)],
        compiler_params=pltpu.CompilerParams(vmem_limit_bytes=16 * 2**20),
        name="widen_receivers",
    )(where, *receivers, flip)


def stack_kernel(src_ref, rec_ref, mask_ref, basis_ref, flip_ref, *refs):
    out_ref, src_f32, lhs, res, done = refs[-5:]
    days = 4 * PER
    size, half = days * 16, basis_ref.shape[1]
    lower, upper = fold_order(src_ref[...], flip_ref[...])
    src_f32[:, :half] = lower
    src_f32[:, half:] = upper
    alone = lax.broadcasted_iota(jnp.int32, (16, 256), 1) == 0
    for s in range(PER):
        p = s % 2
        for d in range(days):
            row = (d // PER * PER + s) * 2 * PER + d % PER * 2
            for lane in range(0, half, 256):
                pair = []
                for start in (lane, half + lane):
                    cols = slice(start, start + 256)
                    a = src_f32[row : row + 1, cols]
                    b = src_f32[row + 1 : row + 2, cols]
                    c = rec_ref[d, 0, :, cols]
                    e = rec_ref[d, 1, :, cols]
                    pair.append((a * c + b * e, a * e - b * c))
                cols = slice(lane, lane + 256)
                for i, (f, g) in enumerate(zip(*pair)):
                    plus, minus = f + g, f - g
                    if lane == 0:
                        plus, minus = jnp.where(alone, g, plus), jnp.where(alone, f, minus)
                    rows = slice(i * size + d * 16, i * size + d * 16 + 16)
                    lhs[p, 0, rows, cols] = plus.astype(jnp.bfloat16)
                    lhs[p, 1, rows, cols] = minus.astype(jnp.bfloat16)
        for i in range(2):
            res[p, i] = jnp.dot(lhs[p, i], basis_ref[i], preferred_element_type=jnp.float32)
        for h in range(0, 16, 8):
            zero = jnp.zeros((8, 128), jnp.float32)
            sums = [[zero] * 6 for _ in range(2)]
            count = zero
            for d in range(days):
                rows = slice(d * 16 + h, d * 16 + h + 8)
                low = slice(size + d * 16 + h, size + d * 16 + h + 8)
                col = (d // PER) * 16 + d % PER
                m = jnp.broadcast_to(mask_ref[s, h : h + 8, col : col + 1], (8, 128))
                count = count + m
                for i in range(2):
                    cos, sin = slice(0, 128), slice(128, 256)
                    rc, rs = res[p, i, rows, cos], res[p, 1 - i, rows, sin]
                    ic, is_ = res[p, i, low, cos], res[p, 1 - i, low, sin]
                    if i == 0:
                        rc = rc + res[p, 1, rows, 127:128]
                        ic = ic + res[p, 1, low, 127:128]
                    for sign, (u, v) in enumerate(((rc - is_, ic + rs), (rc + is_, ic - rs))):
                        w = m * lax.rsqrt(u * u + v * v + 0.0625)
                        acc = sums[i]
                        acc[3 * sign] = acc[3 * sign] + m * u
                        acc[3 * sign + 1] = acc[3 * sign + 1] + w * u
                        acc[3 * sign + 2] = acc[3 * sign + 2] + w * v
            inverse = 1.0 / jnp.maximum(count, 1.0)
            for i in range(2):
                for sign in range(2):
                    linear, real, imag = sums[i][3 * sign : 3 * sign + 3]
                    mean = linear * inverse
                    cols = slice(sign * HALF + i * 128, sign * HALF + i * 128 + 128)
                    done[0, h : h + 8, cols] = mean
                    done[1, h : h + 8, cols] = mean * ((real * real + imag * imag) * (inverse * inverse))
        out_ref[0, 0, s] = done[0].astype(jnp.bfloat16)
        out_ref[0, 1, s] = done[1].astype(jnp.bfloat16)


def stack_group(sources, receivers, mask, basis, flip, earlier):
    width = sources.shape[-1]
    whole = pl.BlockSpec(memory_space=pltpu.VMEM)
    rows = 2 * 4 * PER * 16
    return pl.pallas_call(
        stack_kernel,
        out_shape=jax.ShapeDtypeStruct((1, 2, PER, 16, 2 * HALF), jnp.bfloat16),
        in_specs=[whole] * 5 + [pl.BlockSpec(memory_space=pl.ANY)] * len(earlier),
        out_specs=whole,
        scratch_shapes=[
            pltpu.VMEM(sources.shape, jnp.float32),
            pltpu.VMEM((2, 2, rows, width // 2), jnp.bfloat16),
            pltpu.VMEM((2, 2, rows, HALF), jnp.float32),
            pltpu.VMEM((2, 16, 2 * HALF), jnp.float32),
        ],
        compiler_params=pltpu.CompilerParams(vmem_limit_bytes=24 * 2**20),
        cost_estimate=pl.CostEstimate(
            flops=2 * PER * rows * width * 2 * HALF, bytes_accessed=3 * 2**20, transcendentals=0
        ),
        name="stack_group",
    )(sources, receivers, mask, basis, flip, *earlier)


def order_kernel(count, place_ref, order_ref, *refs):
    parts = refs[:count]
    mean_ref, weighted_ref = refs[-2:]
    middle, day = place_ref[0], place_ref[1]
    size = 2 * PER * 16

    if parts[0].shape[0] == 2:
        parts = [ref.at[i : i + 1] for i in range(2) for ref in parts]
    full = jnp.dot(
        jnp.concatenate([part[...].reshape(size, 2 * HALF) for part in parts], axis=0),
        order_ref[...],
        preferred_element_type=jnp.float32,
    )
    for j in range(4):
        for k2 in range(PER):
            place = (0, (day ^ j) >> 1, middle ^ k2, (day ^ j) & 1)
            top = j * size + k2 * 16
            mean_ref[place] = full[top : top + 16, : 2 * MAXLAG + 1]
            top = top + PER * 16
            weighted_ref[place] = full[top : top + 16, : 2 * MAXLAG + 1]


def order_groups(places, order, parts, outputs):
    whole = pl.BlockSpec(memory_space=pltpu.VMEM)
    shape = jax.ShapeDtypeStruct((4, 2, 4, 2, 16, 2 * MAXLAG + 1), jnp.float32)
    block = pl.BlockSpec(
        (1, 2, 4, 2, 16, 2 * MAXLAG + 1), lambda i, place: (place[2 + i], 0, 0, 0, 0, 0)
    )
    return pl.pallas_call(
        functools.partial(order_kernel, len(parts)),
        out_shape=(shape, shape),
        grid_spec=pltpu.PrefetchScalarGridSpec(
            num_scalar_prefetch=1,
            grid=(1,),
            in_specs=[whole] * (1 + len(parts)) + [pl.BlockSpec(memory_space=pl.ANY)] * len(outputs),
            out_specs=(block, block),
        ),
        input_output_aliases={2 + len(parts) + i: i for i in range(len(outputs))},
        compiler_params=pltpu.CompilerParams(vmem_limit_bytes=24 * 2**20),
        cost_estimate=pl.CostEstimate(flops=2**28, bytes_accessed=2**26, transcendentals=0),
        name="order_groups",
    )(places, order, *parts, *outputs)


def day_swap(x, k):
    return lax.ppermute(x, "day", [(i, i ^ k) for i in range(DAYS)])


def tile_swap(x, k):
    return lax.ppermute(x, "tile", [(i, i ^ k) for i in range(TILES)])


def turn(x, k):
    pairs = []
    for t in range(TILES):
        for xl in range(2):
            for core in range(2):
                to = (t & ~9) | ((xl ^ k) << 3) | core
                pairs.append((t * DAYS + 2 * xl + core, to * DAYS + 2 * ((t >> 3) & 1) + (t & 1)))
    return lax.ppermute(x, ("tile", "day"), pairs)


def on_device(source_spectra, receiver_spectra, valid_pairs):
    width = source_spectra.shape[3]
    tile, day = lax.axis_index("tile"), lax.axis_index("day")
    y, middle = tile >> 4, (tile >> 1) & 3
    shift = (((tile >> 3) & 1) * 2 + (tile & 1)) ^ day
    where = jnp.stack([y, middle, day, shift]).astype(jnp.int32)

    rec0 = jnp.transpose(receiver_spectra, (0, 2, 1, 3)).reshape(32 * PER, width)
    m0 = valid_pairs.reshape(PER, width).astype(jnp.bfloat16)
    rec0 = jnp.concatenate([rec0, jnp.pad(m0, ((0, 16 - PER), (0, 0)))], axis=0)
    rec2 = day_swap(rec0, 2)
    rec1 = day_swap(rec0, 1)
    rec3 = day_swap(rec2, 1)

    own = source_spectra.reshape(2 * PER, width)
    line = jnp.concatenate([own] + [tile_swap(own, 2 * k) for k in (1, 2, 3)], axis=0)
    pair = jnp.concatenate([line, day_swap(line, 1)], axis=0)
    second = jnp.concatenate([turn(pair, k) for k in range(2)], axis=0)
    groups = [second] + [tile_swap(second, 16 * k) for k in (1, 2, 3)]

    basis, flip, order = fold_basis(width), reversal(width // 2), lag_order()
    receivers, masks = widen_receivers(where, (rec0, rec1, rec2, rec3), flip)
    parts, earlier = {}, ()
    for k3 in (0, 1, 3, 2):
        mine = stack_group(groups[k3], receivers, masks[k3], basis, flip, earlier)
        other = day_swap(mine, 2)
        if k3 == 2:
            parts[k3] = [mine, day_swap(mine, 1), other, day_swap(mine, 3)]
        else:
            near = jnp.concatenate([mine, other], axis=0)
            parts[k3] = [near, day_swap(near, 1)]
        earlier = earlier or (mine,)
    outputs = ()
    for k3 in (0, 1, 3, 2):
        places = jnp.stack([middle, day, y ^ k3]).astype(jnp.int32)
        outputs = order_groups(places, order, parts[k3], tuple(outputs))
    return tuple(out.reshape(TILES, 16, 2 * MAXLAG + 1) for out in outputs)


def solution(mesh):
    in_specs = (P("day", "tile", None, None), P("day", "tile", None, None), P("day", None, "tile"))
    out_specs = (P(None, "tile", None), P(None, "tile", None))
    return jax.shard_map(
        on_device, mesh=mesh, in_specs=in_specs, out_specs=out_specs, check_vma=False
    )
```

time: 63.8 us -> 62.9 us (0.986)
  Pallas kernels: 21.8 us -> 20.9 us
    pallas_call x8, Pallas kernels: 20.9 us -> 19.7 us  [the longest x4 12 us: stack_group(): pl.pallas_call(stack_kernel, out_shape=jax.ShapeDtypeStruct((1, 2, PER, 1...]
    ppermute x16 -> x13, starting transfers between devices: 14.4 us -> 14.4 us  [day_swap(): return lax.ppermute(x, 'day', [(i, i ^ k) for i in range(DAYS)])]
  transfers between devices with their start and end apart: 24 -> 21, of which waited for: 3 -> 3; matrix products, arithmetic and copies ran while one was open for 4% -> 4% of each run, Pallas kernels for 31% -> 30%
where the time goes in v3:
time: 62.9 us; the launch traced here: 62.7 us
  starting transfers between devices  33.7 us (54%)
  Pallas kernels  20.9 us (33%)
  waiting for transfers between devices  4.24 us (7%)
  local copies, waits for them, and re-layouts  2.08 us (3%)
  other arithmetic  1.1 us (2%)
  between operations  0.82 us (1%)
    ppermute x13, starting transfers between devices, day_swap(): return lax.ppermute(x, 'day', [(i, i ^ k) for i in range(DAYS)])  14.4 us
    ppermute x6, starting transfers between devices, tile_swap(): return lax.ppermute(x, 'tile', [(i, i ^ k) for i in range(TILES)])  13.1 us
    pallas_call x4, Pallas kernels, stack_group(): pl.pallas_call(stack_kernel, out_shape=jax.ShapeDtypeStruct((1, 2, PER, 1...  12 us
    pallas_call x4, Pallas kernels, order_groups(): pl.pallas_call(functools.partial(order_kernel, len(parts)), out_shape=(sh...  7.72 us
    ppermute x2, starting transfers between devices, turn(): return lax.ppermute(x, ('tile', 'day'), pairs)  6.1 us
    ppermute x2, waiting for transfers between devices, turn(): return lax.ppermute(x, ('tile', 'day'), pairs)  3.29 us
  transfers between devices with their start and end apart: 21, of which 3 were waited for; matrix products, arithmetic and copies ran while one was open for 4% of the time, Pallas kernels for 30%

profile of v3, /device:TPU:1, one launch (start us, length us, event | category | flops | bytes accessed | tf_op | source)
XLA Modules:
  0.0 62.7 jit_solution(16584318114899626177)
XLA Ops:
  0.6 0.0 copy-start.1
  0.6 0.8 %reshape.18 = bf16[8,1024]{1,0:T(8,128)(2,1)S(1)} reshape(bf16[4,1,2,1024]{3,2,1,0:T(2,128)(2,1)} %param.6) | data formatting | bytes 32768 | tf_op jit(solution)/shard_map/reshape | solution.py:271
  1.4 6.9 %collective-permute-start.2 = (bf16[8,1024]{1,0:T(8,128)(2,1)S(1)}, bf16[8,1024]{1,0:T(8,128)(2,1)S(1)}, u32[]{:S(2)}, u32[]{:S(2)}) collective-permute-start(bf16[8,1024]{1,0:T(8,128)(2,1)S(1)} %reshape.18), channel_id=1, source_target_pairs={{0,24},{4,28},{8,16},{12,20},{16,8},{20,12},{24,0},{28,4},{32,56},... | collective-permute-start | bytes 49160 | tf_op jit(solution)/shard_map/ppermute | solution.py:244
  8.4 1.0 %collective-permute-start.1 = (bf16[8,1024]{1,0:T(8,128)(2,1)S(1)}, bf16[8,1024]{1,0:T(8,128)(2,1)S(1)}, u32[]{:S(2)}, u32[]{:S(2)}) collective-permute-start(bf16[8,1024]{1,0:T(8,128)(2,1)S(1)} %reshape.18), channel_id=1, source_target_pairs={{0,16},{4,20},{8,24},{12,28},{16,0},{20,4},{24,8},{28,12},{32,48},... | collective-permute-start | bytes 49160 | tf_op jit(solution)/shard_map/ppermute | solution.py:244
  9.4 1.2 %collective-permute-start = (bf16[8,1024]{1,0:T(8,128)(2,1)S(1)}, bf16[8,1024]{1,0:T(8,128)(2,1)S(1)}, u32[]{:S(2)}, u32[]{:S(2)}) collective-permute-start(bf16[8,1024]{1,0:T(8,128)(2,1)S(1)} %reshape.18), channel_id=1, source_target_pairs={{0,8},{4,12},{8,0},{12,4},{16,24},{20,28},{24,16},{28,20},{32,40},... | collective-permute-start | bytes 49160 | tf_op jit(solution)/shard_map/ppermute | solution.py:244
  10.5 0.8 %convert_element_type.8 = bf16[4,64,16]{1,2,0:T(8,128)(2,1)S(1)} convert(s32[4,64,16]{1,2,0:T(8,128)} %param.8) | non-fusion elementwise | flops 4096 | bytes 24576 | tf_op jit(solution)/shard_map/convert_element_type | solution.py:265
  11.3 0.0 copy-start.2
  11.3 0.1 copy.17
  11.4 0.1 convert_element_type.9
  11.5 1.0 %copy.16 = bf16[4,2,16,1024]{3,2,1,0:T(8,128)(2,1)S(1)} copy(bf16[4,2,16,1024]{3,1,2,0:T(2,128)(2,1)} %bitcast.22) | data formatting | bytes 524288 | tf_op jit(solution)/shard_map/transpose | solution.py:264
  12.6 1.3 %collective-permute-start.8 = (bf16[144,1024]{1,0:T(8,128)(2,1)S(1)}, bf16[144,1024]{1,0:T(8,128)(2,1)S(1)}, u32[]{:S(2)}, u32[]{:S(2)}) collective-permute-start(bf16[144,1024]{1,0:T(8,128)(2,1)S(1)} %fusion.1.rec0), channel_id=1, source_target_pairs={{0,2},{1,3},{2,0},{3,1},{4,6},{5,7},{6,4},{7,5},{8,10},{9,11},{10,... | collective-permute-start | bytes 884744 | tf_op jit(solution)/shard_map/ppermute | solution.py:240
  13.9 1.5 %collective-permute-start.7 = (bf16[144,1024]{1,0:T(8,128)(2,1)S(1)}, bf16[144,1024]{1,0:T(8,128)(2,1)S(1)}, u32[]{:S(2)}, u32[]{:S(2)}) collective-permute-start(bf16[144,1024]{1,0:T(8,128)(2,1)S(1)} %fusion.1.rec0), channel_id=1, source_target_pairs={{0,1},{1,0},{2,3},{3,2},{4,5},{5,4},{6,7},{7,6},{8,9},{9,8},{10,11... | collective-permute-start | bytes 884744 | tf_op jit(solution)/shard_map/ppermute | solution.py:240
  15.4 0.0 collective-permute-done.2
  15.4 0.0 collective-permute-done.1
  15.4 0.0 collective-permute-done
  15.4 1.6 %collective-permute-start.3 = (bf16[32,1024]{1,0:T(8,128)(2,1)S(1)}, bf16[32,1024]{1,0:T(8,128)(2,1)S(1)}, u32[]{:S(2)}, u32[]{:S(2)}) collective-permute-start(bf16[32,1024]{1,0:T(8,128)(2,1)S(1)} %pad_maximum_fusion.3), channel_id=1, source_target_pairs={{0,1},{1,0},{2,3},{3,2},{4,5},{5,4},{6,7},{7,6},{8,9},{9,8},{10,11... | collective-permute-start | bytes 196616 | tf_op jit(solution)/shard_map/ppermute | solution.py:240
  17.1 0.9 %collective-permute-done.3 = bf16[32,1024]{1,0:T(8,128)(2,1)S(1)} collective-permute-done((bf16[32,1024]{1,0:T(8,128)(2,1)S(1)}, bf16[32,1024]{1,0:T(8,128)(2,1)S(1)}, u32[]{:S(2)}, u32[]{:S(2)}) %collective-permute-start.3) | collective-permute-done | bytes 65568 | tf_op jit(solution)/shard_map/ppermute | solution.py:240
  18.0 2.9 %collective-permute-start.4 = (bf16[64,1024]{1,0:T(8,128)(2,1)S(1)}, bf16[64,1024]{1,0:T(8,128)(2,1)S(1)}, u32[]{:S(2)}, u32[]{:S(2)}) collective-permute-start(bf16[64,1024]{1,0:T(8,128)(2,1)S(1)} %constant_dynamic-update-slice_fusion), channel_id=1, source_target_pairs={{0,0},{1,4},{2,32},{3,36},{4,1},{5,5},{6,33},{7,37},{8,8},{9,12},{... | collective-permute-start | bytes 393224 | tf_op jit(solution)/shard_map/ppermute | solution.py:254
  20.9 0.1 pad_add_fusion.5
  20.9 3.2 %collective-permute-start.5 = (bf16[64,1024]{1,0:T(8,128)(2,1)S(1)}, bf16[64,1024]{1,0:T(8,128)(2,1)S(1)}, u32[]{:S(2)}, u32[]{:S(2)}) collective-permute-start(bf16[64,1024]{1,0:T(8,128)(2,1)S(1)} %constant_dynamic-update-slice_fusion), channel_id=1, source_target_pairs={{0,32},{1,36},{2,0},{3,4},{4,33},{5,37},{6,1},{7,5},{8,40},{9,44},... | collective-permute-start | bytes 393224 | tf_op jit(solution)/shard_map/ppermute | solution.py:254
  24.2 0.0 collective-permute-done.8.rec2
  24.2 0.0 collective-permute-start.9
  24.2 0.1 pad_add_fusion.2.where_ref
  24.2 0.3 collective-permute-done.4
  24.6 3.0 %collective-permute-done.5 = bf16[64,1024]{1,0:T(8,128)(2,1)S(1)} collective-permute-done((bf16[64,1024]{1,0:T(8,128)(2,1)S(1)}, bf16[64,1024]{1,0:T(8,128)(2,1)S(1)}, u32[]{:S(2)}, u32[]{:S(2)}) %collective-permute-start.5) | collective-permute-done | bytes 131104 | tf_op jit(solution)/shard_map/ppermute | solution.py:254
  27.6 1.4 %collective-permute-start.16 = (bf16[128,1024]{1,0:T(8,128)(2,1)S(1)}, bf16[128,1024]{1,0:T(8,128)(2,1)S(1)}, u32[]{:S(2)}, u32[]{:S(2)}) collective-permute-start(bf16[128,1024]{1,0:T(8,128)(2,1)S(1)} %constant_dynamic-update-slice_fusion.5.src_ref), channel_id=1, source_target_pairs={{0,64},{4,68},{8,72},{12,76},{16,80},{20,84},{24,88},{28,92},{32,9... | collective-permute-start | bytes 786440 | tf_op jit(solution)/shard_map/ppermute | solution.py:244
  29.0 1.9 %collective-permute-start.13 = (bf16[128,1024]{1,0:T(8,128)(2,1)S(1)}, bf16[128,1024]{1,0:T(8,128)(2,1)S(1)}, u32[]{:S(2)}, u32[]{:S(2)}) collective-permute-start(bf16[128,1024]{1,0:T(8,128)(2,1)S(1)} %constant_dynamic-update-slice_fusion.5.src_ref), channel_id=1, source_target_pairs={{0,192},{4,196},{8,200},{12,204},{16,208},{20,212},{24,216},{28,22... | collective-permute-start | bytes 786440 | tf_op jit(solution)/shard_map/ppermute | solution.py:244
  30.9 0.7 %collective-permute-start.6 = (bf16[128,1024]{1,0:T(8,128)(2,1)S(1)}, bf16[128,1024]{1,0:T(8,128)(2,1)S(1)}, u32[]{:S(2)}, u32[]{:S(2)}) collective-permute-start(bf16[128,1024]{1,0:T(8,128)(2,1)S(1)} %constant_dynamic-update-slice_fusion.5.src_ref), channel_id=1, source_target_pairs={{0,128},{4,132},{8,136},{12,140},{16,144},{20,148},{24,152},{28,15... | collective-permute-start | bytes 786440 | tf_op jit(solution)/shard_map/ppermute | solution.py:244
  31.6 0.0 collective-permute-done.7.rec1
  31.6 0.0 collective-permute-done.9.rec3
  31.6 0.0 copy-done.1
  31.6 1.2 %widen_receivers.1 = (f32[16,2,16,1024]{3,2,1,0:T(8,128)S(1)}, f32[4,4,16,128]{3,2,1,0:T(8,128)S(1)}) custom-call(s32[4]{0:T(128)S(1)} %pad_add_fusion.2.where_ref, bf16[144,1024]{1,0:T(8,128)(2,1)S(1)} %fusion.1.rec0, bf16[144,1024]{1,0:T(8,128)(2,1)S(1)} %collective-permute-done.7.rec1, bf16[144,1024]{1,0:T(8,128)(2,1)S(1)} %collective-permute-done.8.rec2, ...), custom_call_target="tpu_custom_call" | custom-call | tf_op jit(solution)/shard_map/widen_receivers/pallas_call | solution.py:92
  32.8 0.0 copy-done.2
  32.8 3.0 %stack_group.4.refs_0_ = bf16[1,2,4,16,512]{4,3,2,1,0:T(8,128)(2,1)S(1)} custom-call(bf16[128,1024]{1,0:T(8,128)(2,1)S(1)} %constant_dynamic-update-slice_fusion.5.src_ref, f32[16,2,16,1024]{3,2,1,0:T(8,128)S(1)} %get-tuple-element.12.rec_ref, f32[4,16,128]{2,1,0:T(8,128)S(1)} %get-tuple-element.26.mask_ref, bf16[2,512,256]{2,1,0:T(8,128)(2,1)S(1)} %copy-done.2, ...), custom_call_target="tpu_custom_call" | custom-call | flops 2147483648 | bytes 3145728 | tf_op jit(solution)/shard_map/stack_group/pallas_call | solution.py:176
  35.8 2.7 %collective-permute-start.19 = (bf16[1,2,4,16,512]{4,3,2,1,0:T(8,128)(2,1)S(1)}, bf16[1,2,4,16,512]{4,3,2,1,0:T(8,128)(2,1)S(1)}, u32[]{:S(2)}, u32[]{:S(2)}) collective-permute-start(bf16[1,2,4,16,512]{4,3,2,1,0:T(8,128)(2,1)S(1)} %stack_group.4.refs_0_), channel_id=1, source_target_pairs={{0,2},{1,3},{2,0},{3,1},{4,6},{5,7},{6,4},{7,5},{8,10},{9,11},{10,... | collective-permute-start | bytes 393224 | tf_op jit(solution)/shard_map/ppermute | solution.py:240
  38.5 0.0 collective-permute-done.16.src_ref
  38.5 3.0 %stack_group.7 = bf16[1,2,4,16,512]{4,3,2,1,0:T(8,128)(2,1)S(1)} custom-call(bf16[128,1024]{1,0:T(8,128)(2,1)S(1)} %collective-permute-done.16.src_ref, f32[16,2,16,1024]{3,2,1,0:T(8,128)S(1)} %get-tuple-element.12.rec_ref, f32[4,16,128]{2,1,0:T(8,128)S(1)} %get-tuple-element.24.mask_ref, bf16[2,512,256]{2,1,0:T(8,128)(2,1)S(1)} %copy-done.2, ...), custom_call_target="tpu_custom_call" | custom-call | flops 2147483648 | bytes 3145728 | tf_op jit(solution)/shard_map/stack_group/pallas_call | solution.py:176
  41.5 0.1 collective-permute-start.17
  41.6 0.0 collective-permute-done.13.src_ref
  41.6 3.0 %stack_group.6 = bf16[1,2,4,16,512]{4,3,2,1,0:T(8,128)(2,1)S(1)} custom-call(bf16[128,1024]{1,0:T(8,128)(2,1)S(1)} %collective-permute-done.13.src_ref, f32[16,2,16,1024]{3,2,1,0:T(8,128)S(1)} %get-tuple-element.12.rec_ref, f32[4,16,128]{2,1,0:T(8,128)S(1)} %get-tuple-element.25.mask_ref, bf16[2,512,256]{2,1,0:T(8,128)(2,1)S(1)} %copy-done.2, ...), custom_call_target="tpu_custom_call" | custom-call | flops 2147483648 | bytes 3145728 | tf_op jit(solution)/shard_map/stack_group/pallas_call | solution.py:176
  44.6 1.5 %collective-permute-start.14 = (bf16[1,2,4,16,512]{4,3,2,1,0:T(8,128)(2,1)S(1)}, bf16[1,2,4,16,512]{4,3,2,1,0:T(8,128)(2,1)S(1)}, u32[]{:S(2)}, u32[]{:S(2)}) collective-permute-start(bf16[1,2,4,16,512]{4,3,2,1,0:T(8,128)(2,1)S(1)} %stack_group.6), channel_id=1, source_target_pairs={{0,2},{1,3},{2,0},{3,1},{4,6},{5,7},{6,4},{7,5},{8,10},{9,11},{10,... | collective-permute-start | bytes 393224 | tf_op jit(solution)/shard_map/ppermute | solution.py:240
  46.2 0.0 collective-permute-done.19
  46.2 2.7 %collective-permute-start.20 = (bf16[2,2,4,16,512]{4,3,2,1,0:T(8,128)(2,1)S(1)}, bf16[2,2,4,16,512]{4,3,2,1,0:T(8,128)(2,1)S(1)}, u32[]{:S(2)}, u32[]{:S(2)}) collective-permute-start(bf16[2,2,4,16,512]{4,3,2,1,0:T(8,128)(2,1)S(1)} %pad_maximum_fusion.2.refs_0_), channel_id=1, source_target_pairs={{0,1},{1,0},{2,3},{3,2},{4,5},{5,4},{6,7},{7,6},{8,9},{9,8},{10,11... | collective-permute-start | bytes 786440 | tf_op jit(solution)/shard_map/ppermute | solution.py:240
  48.9 0.0 collective-permute-done.6.src_ref
  48.9 3.0 %stack_group.5.refs_0_ = bf16[1,2,4,16,512]{4,3,2,1,0:T(8,128)(2,1)S(1)} custom-call(bf16[128,1024]{1,0:T(8,128)(2,1)S(1)} %collective-permute-done.6.src_ref, f32[16,2,16,1024]{3,2,1,0:T(8,128)S(1)} %get-tuple-element.12.rec_ref, f32[4,16,128]{2,1,0:T(8,128)S(1)} %get-tuple-element.27.mask_ref, bf16[2,512,256]{2,1,0:T(8,128)(2,1)S(1)} %copy-done.2, ...), custom_call_target="tpu_custom_call" | custom-call | flops 2147483648 | bytes 3145728 | tf_op jit(solution)/shard_map/stack_group/pallas_call | solution.py:176
  51.9 0.1 collective-permute-start.12
  52.0 1.4 %collective-permute-start.11 = (bf16[1,2,4,16,512]{4,3,2,1,0:T(8,128)(2,1)S(1)}, bf16[1,2,4,16,512]{4,3,2,1,0:T(8,128)(2,1)S(1)}, u32[]{:S(2)}, u32[]{:S(2)}) collective-permute-start(bf16[1,2,4,16,512]{4,3,2,1,0:T(8,128)(2,1)S(1)} %stack_group.5.refs_0_), channel_id=1, source_target_pairs={{0,2},{1,3},{2,0},{3,1},{4,6},{5,7},{6,4},{7,5},{8,10},{9,11},{10,... | collective-permute-start | bytes 393224 | tf_op jit(solution)/shard_map/ppermute | solution.py:240
  53.4 0.0 collective-permute-done.17
  53.4 0.8 %collective-permute-start.10 = (bf16[1,2,4,16,512]{4,3,2,1,0:T(8,128)(2,1)S(1)}, bf16[1,2,4,16,512]{4,3,2,1,0:T(8,128)(2,1)S(1)}, u32[]{:S(2)}, u32[]{:S(2)}) collective-permute-start(bf16[1,2,4,16,512]{4,3,2,1,0:T(8,128)(2,1)S(1)} %stack_group.5.refs_0_), channel_id=1, source_target_pairs={{0,1},{1,0},{2,3},{3,2},{4,5},{5,4},{6,7},{7,6},{8,9},{9,8},{10,11... | collective-permute-start | bytes 393224 | tf_op jit(solution)/shard_map/ppermute | solution.py:240
  54.2 0.0 collective-permute-done.14
  54.2 0.1 collective-permute-start.18
  54.3 0.0 collective-permute-done.20.refs_1_
  54.4 0.6 collective-permute-start.15
  54.9 0.1 pad_add_fusion.4
  55.0 0.0 copy-done
  55.0 1.9 %order_groups.4 = (f32[4,2,4,2,16,401]{5,4,3,2,1,0:T(8,128)}, f32[4,2,4,2,16,401]{5,4,3,2,1,0:T(8,128)}) custom-call(s32[3]{0:T(128)S(1)} %get-tuple-element.22.place_ref, bf16[512,512]{1,0:T(8,128)(2,1)S(1)} %copy-done, bf16[2,2,4,16,512]{4,3,2,1,0:T(8,128)(2,1)S(1)} %pad_maximum_fusion.2.refs_0_, ...), custom_call_target="tpu_custom_call" | custom-call | flops 268435456 | bytes 67108864 | tf_op jit(solution)/shard_map/order_groups/pallas_call | solution.py:223
  56.9 0.0 collective-permute-done.18.refs_1_
  56.9 1.9 %order_groups.5 = (f32[4,2,4,2,16,401]{5,4,3,2,1,0:T(8,128)}, f32[4,2,4,2,16,401]{5,4,3,2,1,0:T(8,128)}) custom-call(s32[3]{0:T(128)S(1)} %get-tuple-element.28.place_ref, bf16[512,512]{1,0:T(8,128)(2,1)S(1)} %copy-done, bf16[2,2,4,16,512]{4,3,2,1,0:T(8,128)(2,1)S(1)} %pad_maximum_fusion.1.refs_0_, ...), custom_call_target="tpu_custom_call", output_to_operand_aliasing={{0}: (4, {}), {1}: (5, {})} | custom-call | flops 268435456 | bytes 67108864 | tf_op jit(solution)/shard_map/order_groups/pallas_call | solution.py:223
  58.9 0.0 collective-permute-done.15.refs_1_
  58.9 1.9 %order_groups.6 = (f32[4,2,4,2,16,401]{5,4,3,2,1,0:T(8,128)}, f32[4,2,4,2,16,401]{5,4,3,2,1,0:T(8,128)}) custom-call(s32[3]{0:T(128)S(1)} %get-tuple-element.29.place_ref, bf16[512,512]{1,0:T(8,128)(2,1)S(1)} %copy-done, bf16[2,2,4,16,512]{4,3,2,1,0:T(8,128)(2,1)S(1)} %pad_maximum_fusion.refs_0_, ...), custom_call_target="tpu_custom_call", output_to_operand_aliasing={{0}: (4, {}), {1}: (5, {})} | custom-call | flops 268435456 | bytes 67108864 | tf_op jit(solution)/shard_map/order_groups/pallas_call | solution.py:223
  60.8 0.0 collective-permute-done.12.refs_3_
  60.8 0.0 collective-permute-done.11.refs_2_
  60.8 0.0 collective-permute-done.10.refs_1_
  60.8 1.9 %order_groups.7 = (f32[4,2,4,2,16,401]{5,4,3,2,1,0:T(8,128)}, f32[4,2,4,2,16,401]{5,4,3,2,1,0:T(8,128)}) custom-call(s32[3]{0:T(128)S(1)} %get-tuple-element.30.place_ref, bf16[512,512]{1,0:T(8,128)(2,1)S(1)} %copy-done, bf16[1,2,4,16,512]{4,3,2,1,0:T(8,128)(2,1)S(1)} %stack_group.5.refs_0_, ...), custom_call_target="tpu_custom_call", output_to_operand_aliasing={{0}: (6, {}), {1}: (7, {})} | custom-call | flops 268435456 | bytes 67108864 | tf_op jit(solution)/shard_map/order_groups/pallas_call | solution.py:223
  (14 shorter events, 0.2 us)
Async XLA Ops:
  0.6 31.0 %copy-start.1 = (bf16[512,512]{1,0:T(8,128)(2,1)S(1)}, bf16[512,512]{1,0:T(8,128)(2,1)}, u32[]{:S(2)}) copy-start(bf16[512,512]{1,0:T(8,128)(2,1)} %constant.27.clone.flip_ref) | copy-start | bytes 1572868
  1.4 14.0 %collective-permute-start.2 = (bf16[8,1024]{1,0:T(8,128)(2,1)S(1)}, bf16[8,1024]{1,0:T(8,128)(2,1)S(1)}, u32[]{:S(2)}, u32[]{:S(2)}) collective-permute-start(bf16[8,1024]{1,0:T(8,128)(2,1)S(1)} %reshape.18), channel_id=1, source_target_pairs={{0,24},{4,28},{8,16},{12,20},{16,8},{20,12},{24,0},{28,4},{32,56},... | collective-permute-start | bytes 49160 | tf_op jit(solution)/shard_map/ppermute | solution.py:244
  8.4 7.0 %collective-permute-start.1 = (bf16[8,1024]{1,0:T(8,128)(2,1)S(1)}, bf16[8,1024]{1,0:T(8,128)(2,1)S(1)}, u32[]{:S(2)}, u32[]{:S(2)}) collective-permute-start(bf16[8,1024]{1,0:T(8,128)(2,1)S(1)} %reshape.18), channel_id=1, source_target_pairs={{0,16},{4,20},{8,24},{12,28},{16,0},{20,4},{24,8},{28,12},{32,48},... | collective-permute-start | bytes 49160 | tf_op jit(solution)/shard_map/ppermute | solution.py:244
  9.4 6.1 %collective-permute-start = (bf16[8,1024]{1,0:T(8,128)(2,1)S(1)}, bf16[8,1024]{1,0:T(8,128)(2,1)S(1)}, u32[]{:S(2)}, u32[]{:S(2)}) collective-permute-start(bf16[8,1024]{1,0:T(8,128)(2,1)S(1)} %reshape.18), channel_id=1, source_target_pairs={{0,8},{4,12},{8,0},{12,4},{16,24},{20,28},{24,16},{28,20},{32,40},... | collective-permute-start | bytes 49160 | tf_op jit(solution)/shard_map/ppermute | solution.py:244
  11.3 21.5 %copy-start.2 = (bf16[2,512,256]{2,1,0:T(8,128)(2,1)S(1)}, bf16[2,512,256]{2,1,0:T(8,128)(2,1)}, u32[]{:S(2)}) copy-start(bf16[2,512,256]{2,1,0:T(8,128)(2,1)} %constant.26.clone.basis_ref) | copy-start | bytes 1572868
  12.6 11.6 %collective-permute-start.8 = (bf16[144,1024]{1,0:T(8,128)(2,1)S(1)}, bf16[144,1024]{1,0:T(8,128)(2,1)S(1)}, u32[]{:S(2)}, u32[]{:S(2)}) collective-permute-start(bf16[144,1024]{1,0:T(8,128)(2,1)S(1)} %fusion.1.rec0), channel_id=1, source_target_pairs={{0,2},{1,3},{2,0},{3,1},{4,6},{5,7},{6,4},{7,5},{8,10},{9,11},{10,... | collective-permute-start | bytes 884744 | tf_op jit(solution)/shard_map/ppermute | solution.py:240
  13.9 17.7 %collective-permute-start.7 = (bf16[144,1024]{1,0:T(8,128)(2,1)S(1)}, bf16[144,1024]{1,0:T(8,128)(2,1)S(1)}, u32[]{:S(2)}, u32[]{:S(2)}) collective-permute-start(bf16[144,1024]{1,0:T(8,128)(2,1)S(1)} %fusion.1.rec0), channel_id=1, source_target_pairs={{0,1},{1,0},{2,3},{3,2},{4,5},{5,4},{6,7},{7,6},{8,9},{9,8},{10,11... | collective-permute-start | bytes 884744 | tf_op jit(solution)/shard_map/ppermute | solution.py:240
  15.4 2.5 %collective-permute-start.3 = (bf16[32,1024]{1,0:T(8,128)(2,1)S(1)}, bf16[32,1024]{1,0:T(8,128)(2,1)S(1)}, u32[]{:S(2)}, u32[]{:S(2)}) collective-permute-start(bf16[32,1024]{1,0:T(8,128)(2,1)S(1)} %pad_maximum_fusion.3), channel_id=1, source_target_pairs={{0,1},{1,0},{2,3},{3,2},{4,5},{5,4},{6,7},{7,6},{8,9},{9,8},{10,11... | collective-permute-start | bytes 196616 | tf_op jit(solution)/shard_map/ppermute | solution.py:240
  18.0 6.6 %collective-permute-start.4 = (bf16[64,1024]{1,0:T(8,128)(2,1)S(1)}, bf16[64,1024]{1,0:T(8,128)(2,1)S(1)}, u32[]{:S(2)}, u32[]{:S(2)}) collective-permute-start(bf16[64,1024]{1,0:T(8,128)(2,1)S(1)} %constant_dynamic-update-slice_fusion), channel_id=1, source_target_pairs={{0,0},{1,4},{2,32},{3,36},{4,1},{5,5},{6,33},{7,37},{8,8},{9,12},{... | collective-permute-start | bytes 393224 | tf_op jit(solution)/shard_map/ppermute | solution.py:254
  20.9 6.6 %collective-permute-start.5 = (bf16[64,1024]{1,0:T(8,128)(2,1)S(1)}, bf16[64,1024]{1,0:T(8,128)(2,1)S(1)}, u32[]{:S(2)}, u32[]{:S(2)}) collective-permute-start(bf16[64,1024]{1,0:T(8,128)(2,1)S(1)} %constant_dynamic-update-slice_fusion), channel_id=1, source_target_pairs={{0,32},{1,36},{2,0},{3,4},{4,33},{5,37},{6,1},{7,5},{8,40},{9,44},... | collective-permute-start | bytes 393224 | tf_op jit(solution)/shard_map/ppermute | solution.py:254
  24.2 7.4 %collective-permute-start.9 = (bf16[144,1024]{1,0:T(8,128)(2,1)S(1)}, bf16[144,1024]{1,0:T(8,128)(2,1)S(1)}, u32[]{:S(2)}, u32[]{:S(2)}) collective-permute-start(bf16[144,1024]{1,0:T(8,128)(2,1)S(1)} %collective-permute-done.8.rec2), channel_id=1, source_target_pairs={{0,1},{1,0},{2,3},{3,2},{4,5},{5,4},{6,7},{7,6},{8,9},{9,8},{10,11... | collective-permute-start | bytes 884744 | tf_op jit(solution)/shard_map/ppermute | solution.py:240
  27.6 10.9 %collective-permute-start.16 = (bf16[128,1024]{1,0:T(8,128)(2,1)S(1)}, bf16[128,1024]{1,0:T(8,128)(2,1)S(1)}, u32[]{:S(2)}, u32[]{:S(2)}) collective-permute-start(bf16[128,1024]{1,0:T(8,128)(2,1)S(1)} %constant_dynamic-update-slice_fusion.5.src_ref), channel_id=1, source_target_pairs={{0,64},{4,68},{8,72},{12,76},{16,80},{20,84},{24,88},{28,92},{32,9... | collective-permute-start | bytes 786440 | tf_op jit(solution)/shard_map/ppermute | solution.py:244
  29.0 12.7 %collective-permute-start.13 = (bf16[128,1024]{1,0:T(8,128)(2,1)S(1)}, bf16[128,1024]{1,0:T(8,128)(2,1)S(1)}, u32[]{:S(2)}, u32[]{:S(2)}) collective-permute-start(bf16[128,1024]{1,0:T(8,128)(2,1)S(1)} %constant_dynamic-update-slice_fusion.5.src_ref), channel_id=1, source_target_pairs={{0,192},{4,196},{8,200},{12,204},{16,208},{20,212},{24,216},{28,22... | collective-permute-start | bytes 786440 | tf_op jit(solution)/shard_map/ppermute | solution.py:244
  30.9 18.1 %collective-permute-start.6 = (bf16[128,1024]{1,0:T(8,128)(2,1)S(1)}, bf16[128,1024]{1,0:T(8,128)(2,1)S(1)}, u32[]{:S(2)}, u32[]{:S(2)}) collective-permute-start(bf16[128,1024]{1,0:T(8,128)(2,1)S(1)} %constant_dynamic-update-slice_fusion.5.src_ref), channel_id=1, source_target_pairs={{0,128},{4,132},{8,136},{12,140},{16,144},{20,148},{24,152},{28,15... | collective-permute-start | bytes 786440 | tf_op jit(solution)/shard_map/ppermute | solution.py:244
  35.8 10.4 %collective-permute-start.19 = (bf16[1,2,4,16,512]{4,3,2,1,0:T(8,128)(2,1)S(1)}, bf16[1,2,4,16,512]{4,3,2,1,0:T(8,128)(2,1)S(1)}, u32[]{:S(2)}, u32[]{:S(2)}) collective-permute-start(bf16[1,2,4,16,512]{4,3,2,1,0:T(8,128)(2,1)S(1)} %stack_group.4.refs_0_), channel_id=1, source_target_pairs={{0,2},{1,3},{2,0},{3,1},{4,6},{5,7},{6,4},{7,5},{8,10},{9,11},{10,... | collective-permute-start | bytes 393224 | tf_op jit(solution)/shard_map/ppermute | solution.py:240
  41.5 11.9 %collective-permute-start.17 = (bf16[1,2,4,16,512]{4,3,2,1,0:T(8,128)(2,1)S(1)}, bf16[1,2,4,16,512]{4,3,2,1,0:T(8,128)(2,1)S(1)}, u32[]{:S(2)}, u32[]{:S(2)}) collective-permute-start(bf16[1,2,4,16,512]{4,3,2,1,0:T(8,128)(2,1)S(1)} %stack_group.7), channel_id=1, source_target_pairs={{0,2},{1,3},{2,0},{3,1},{4,6},{5,7},{6,4},{7,5},{8,10},{9,11},{10,... | collective-permute-start | bytes 393224 | tf_op jit(solution)/shard_map/ppermute | solution.py:240
  44.6 9.6 %collective-permute-start.14 = (bf16[1,2,4,16,512]{4,3,2,1,0:T(8,128)(2,1)S(1)}, bf16[1,2,4,16,512]{4,3,2,1,0:T(8,128)(2,1)S(1)}, u32[]{:S(2)}, u32[]{:S(2)}) collective-permute-start(bf16[1,2,4,16,512]{4,3,2,1,0:T(8,128)(2,1)S(1)} %stack_group.6), channel_id=1, source_target_pairs={{0,2},{1,3},{2,0},{3,1},{4,6},{5,7},{6,4},{7,5},{8,10},{9,11},{10,... | collective-permute-start | bytes 393224 | tf_op jit(solution)/shard_map/ppermute | solution.py:240
  46.2 8.1 %collective-permute-start.20 = (bf16[2,2,4,16,512]{4,3,2,1,0:T(8,128)(2,1)S(1)}, bf16[2,2,4,16,512]{4,3,2,1,0:T(8,128)(2,1)S(1)}, u32[]{:S(2)}, u32[]{:S(2)}) collective-permute-start(bf16[2,2,4,16,512]{4,3,2,1,0:T(8,128)(2,1)S(1)} %pad_maximum_fusion.2.refs_0_), channel_id=1, source_target_pairs={{0,1},{1,0},{2,3},{3,2},{4,5},{5,4},{6,7},{7,6},{8,9},{9,8},{10,11... | collective-permute-start | bytes 786440 | tf_op jit(solution)/shard_map/ppermute | solution.py:240
  48.9 6.1 %copy-start = (bf16[512,512]{1,0:T(8,128)(2,1)S(1)}, bf16[512,512]{1,0:T(8,128)(2,1)}, u32[]{:S(2)}) copy-start(bf16[512,512]{1,0:T(8,128)(2,1)} %constant.28.clone.order_ref) | copy-start | bytes 1572868
  51.9 8.9 %collective-permute-start.12 = (bf16[1,2,4,16,512]{4,3,2,1,0:T(8,128)(2,1)S(1)}, bf16[1,2,4,16,512]{4,3,2,1,0:T(8,128)(2,1)S(1)}, u32[]{:S(2)}, u32[]{:S(2)}) collective-permute-start(bf16[1,2,4,16,512]{4,3,2,1,0:T(8,128)(2,1)S(1)} %stack_group.5.refs_0_), channel_id=1, source_target_pairs={{0,3},{1,2},{2,1},{3,0},{4,7},{5,6},{6,5},{7,4},{8,11},{9,10},{10,... | collective-permute-start | bytes 393224 | tf_op jit(solution)/shard_map/ppermute | solution.py:240
  52.0 8.8 %collective-permute-start.11 = (bf16[1,2,4,16,512]{4,3,2,1,0:T(8,128)(2,1)S(1)}, bf16[1,2,4,16,512]{4,3,2,1,0:T(8,128)(2,1)S(1)}, u32[]{:S(2)}, u32[]{:S(2)}) collective-permute-start(bf16[1,2,4,16,512]{4,3,2,1,0:T(8,128)(2,1)S(1)} %stack_group.5.refs_0_), channel_id=1, source_target_pairs={{0,2},{1,3},{2,0},{3,1},{4,6},{5,7},{6,4},{7,5},{8,10},{9,11},{10,... | collective-permute-start | bytes 393224 | tf_op jit(solution)/shard_map/ppermute | solution.py:240
  53.4 7.4 %collective-permute-start.10 = (bf16[1,2,4,16,512]{4,3,2,1,0:T(8,128)(2,1)S(1)}, bf16[1,2,4,16,512]{4,3,2,1,0:T(8,128)(2,1)S(1)}, u32[]{:S(2)}, u32[]{:S(2)}) collective-permute-start(bf16[1,2,4,16,512]{4,3,2,1,0:T(8,128)(2,1)S(1)} %stack_group.5.refs_0_), channel_id=1, source_target_pairs={{0,1},{1,0},{2,3},{3,2},{4,5},{5,4},{6,7},{7,6},{8,9},{9,8},{10,11... | collective-permute-start | bytes 393224 | tf_op jit(solution)/shard_map/ppermute | solution.py:240
  54.2 2.7 %collective-permute-start.18 = (bf16[2,2,4,16,512]{4,3,2,1,0:T(8,128)(2,1)S(1)}, bf16[2,2,4,16,512]{4,3,2,1,0:T(8,128)(2,1)S(1)}, u32[]{:S(2)}, u32[]{:S(2)}) collective-permute-start(bf16[2,2,4,16,512]{4,3,2,1,0:T(8,128)(2,1)S(1)} %pad_maximum_fusion.1.refs_0_), channel_id=1, source_target_pairs={{0,1},{1,0},{2,3},{3,2},{4,5},{5,4},{6,7},{7,6},{8,9},{9,8},{10,11... | collective-permute-start | bytes 786440 | tf_op jit(solution)/shard_map/ppermute | solution.py:240
  54.4 4.5 %collective-permute-start.15 = (bf16[2,2,4,16,512]{4,3,2,1,0:T(8,128)(2,1)S(1)}, bf16[2,2,4,16,512]{4,3,2,1,0:T(8,128)(2,1)S(1)}, u32[]{:S(2)}, u32[]{:S(2)}) collective-permute-start(bf16[2,2,4,16,512]{4,3,2,1,0:T(8,128)(2,1)S(1)} %pad_maximum_fusion.refs_0_), channel_id=1, source_target_pairs={{0,1},{1,0},{2,3},{3,2},{4,5},{5,4},{6,7},{7,6},{8,9},{9,8},{10,11... | collective-permute-start | bytes 786440 | tf_op jit(solution)/shard_map/ppermute | solution.py:240

commit v4 on v3

--- a/solution.py
+++ b/solution.py
@@ -126,12 +126,13 @@
                     pair.append((a * c + b * e, a * e - b * c))
                 cols = slice(lane, lane + 256)
                 for i, (f, g) in enumerate(zip(*pair)):
+                    f, g = f.astype(jnp.bfloat16), g.astype(jnp.bfloat16)
                     plus, minus = f + g, f - g
                     if lane == 0:
                         plus, minus = jnp.where(alone, g, plus), jnp.where(alone, f, minus)
                     rows = slice(i * size + d * 16, i * size + d * 16 + 16)
-                    lhs[p, 0, rows, cols] = plus.astype(jnp.bfloat16)
-                    lhs[p, 1, rows, cols] = minus.astype(jnp.bfloat16)
+                    lhs[p, 0, rows, cols] = plus
+                    lhs[p, 1, rows, cols] = minus
         for i in range(2):
             res[p, i] = jnp.dot(lhs[p, i], basis_ref[i], preferred_element_type=jnp.float32)
         for h in range(0, 16, 8):

time: 62.9 us -> 62.8 us (level)
  no operation moved by 1% of the time
where the time goes in v4:
time: 62.8 us; the launch traced here: 62.6 us
  starting transfers between devices  33.8 us (54%)
  Pallas kernels  20.6 us (33%)
  waiting for transfers between devices  4.24 us (7%)
  local copies, waits for them, and re-layouts  2.08 us (3%)
  other arithmetic  1.1 us (2%)
  between operations  0.82 us (1%)
    ppermute x13, starting transfers between devices, day_swap(): return lax.ppermute(x, 'day', [(i, i ^ k) for i in range(DAYS)])  14.6 us
    ppermute x6, starting transfers between devices, tile_swap(): return lax.ppermute(x, 'tile', [(i, i ^ k) for i in range(TILES)])  13.1 us
    pallas_call x4, Pallas kernels, stack_group(): pl.pallas_call(stack_kernel, out_shape=jax.ShapeDtypeStruct((1, 2, PER, 1...  11.7 us
    pallas_call x4, Pallas kernels, order_groups(): pl.pallas_call(functools.partial(order_kernel, len(parts)), out_shape=(sh...  7.71 us
    ppermute x2, starting transfers between devices, turn(): return lax.ppermute(x, ('tile', 'day'), pairs)  6.1 us
    ppermute x2, waiting for transfers between devices, turn(): return lax.ppermute(x, ('tile', 'day'), pairs)  3.29 us
  transfers between devices with their start and end apart: 21, of which 3 were waited for; matrix products, arithmetic and copies ran while one was open for 4% of the time, Pallas kernels for 30%

profile of v4, /device:TPU:1, one launch (start us, length us, event | category | flops | bytes accessed | tf_op | source)
XLA Modules:
  0.0 62.6 jit_solution(16660481101528494024)
XLA Ops:
  0.6 0.0 copy-start.1
  0.6 0.8 %reshape.18 = bf16[8,1024]{1,0:T(8,128)(2,1)S(1)} reshape(bf16[4,1,2,1024]{3,2,1,0:T(2,128)(2,1)} %param.6) | data formatting | bytes 32768 | tf_op jit(solution)/shard_map/reshape | solution.py:272
  1.4 6.9 %collective-permute-start.2 = (bf16[8,1024]{1,0:T(8,128)(2,1)S(1)}, bf16[8,1024]{1,0:T(8,128)(2,1)S(1)}, u32[]{:S(2)}, u32[]{:S(2)}) collective-permute-start(bf16[8,1024]{1,0:T(8,128)(2,1)S(1)} %reshape.18), channel_id=1, source_target_pairs={{0,24},{4,28},{8,16},{12,20},{16,8},{20,12},{24,0},{28,4},{32,56},... | collective-permute-start | bytes 49160 | tf_op jit(solution)/shard_map/ppermute | solution.py:245
  8.4 1.0 %collective-permute-start.1 = (bf16[8,1024]{1,0:T(8,128)(2,1)S(1)}, bf16[8,1024]{1,0:T(8,128)(2,1)S(1)}, u32[]{:S(2)}, u32[]{:S(2)}) collective-permute-start(bf16[8,1024]{1,0:T(8,128)(2,1)S(1)} %reshape.18), channel_id=1, source_target_pairs={{0,16},{4,20},{8,24},{12,28},{16,0},{20,4},{24,8},{28,12},{32,48},... | collective-permute-start | bytes 49160 | tf_op jit(solution)/shard_map/ppermute | solution.py:245
  9.4 1.2 %collective-permute-start = (bf16[8,1024]{1,0:T(8,128)(2,1)S(1)}, bf16[8,1024]{1,0:T(8,128)(2,1)S(1)}, u32[]{:S(2)}, u32[]{:S(2)}) collective-permute-start(bf16[8,1024]{1,0:T(8,128)(2,1)S(1)} %reshape.18), channel_id=1, source_target_pairs={{0,8},{4,12},{8,0},{12,4},{16,24},{20,28},{24,16},{28,20},{32,40},... | collective-permute-start | bytes 49160 | tf_op jit(solution)/shard_map/ppermute | solution.py:245
  10.5 0.8 %convert_element_type.8 = bf16[4,64,16]{1,2,0:T(8,128)(2,1)S(1)} convert(s32[4,64,16]{1,2,0:T(8,128)} %param.8) | non-fusion elementwise | flops 4096 | bytes 24576 | tf_op jit(solution)/shard_map/convert_element_type | solution.py:266
  11.3 0.0 copy-start.2
  11.3 0.1 copy.17
  11.4 0.1 convert_element_type.9
  11.5 1.0 %copy.16 = bf16[4,2,16,1024]{3,2,1,0:T(8,128)(2,1)S(1)} copy(bf16[4,2,16,1024]{3,1,2,0:T(2,128)(2,1)} %bitcast.22) | data formatting | bytes 524288 | tf_op jit(solution)/shard_map/transpose | solution.py:265
  12.6 1.3 %collective-permute-start.8 = (bf16[144,1024]{1,0:T(8,128)(2,1)S(1)}, bf16[144,1024]{1,0:T(8,128)(2,1)S(1)}, u32[]{:S(2)}, u32[]{:S(2)}) collective-permute-start(bf16[144,1024]{1,0:T(8,128)(2,1)S(1)} %fusion.1.rec0), channel_id=1, source_target_pairs={{0,2},{1,3},{2,0},{3,1},{4,6},{5,7},{6,4},{7,5},{8,10},{9,11},{10,... | collective-permute-start | bytes 884744 | tf_op jit(solution)/shard_map/ppermute | solution.py:241
  13.9 1.5 %collective-permute-start.7 = (bf16[144,1024]{1,0:T(8,128)(2,1)S(1)}, bf16[144,1024]{1,0:T(8,128)(2,1)S(1)}, u32[]{:S(2)}, u32[]{:S(2)}) collective-permute-start(bf16[144,1024]{1,0:T(8,128)(2,1)S(1)} %fusion.1.rec0), channel_id=1, source_target_pairs={{0,1},{1,0},{2,3},{3,2},{4,5},{5,4},{6,7},{7,6},{8,9},{9,8},{10,11... | collective-permute-start | bytes 884744 | tf_op jit(solution)/shard_map/ppermute | solution.py:241
  15.4 0.0 collective-permute-done.2
  15.4 0.0 collective-permute-done.1
  15.4 0.0 collective-permute-done
  15.4 1.6 %collective-permute-start.3 = (bf16[32,1024]{1,0:T(8,128)(2,1)S(1)}, bf16[32,1024]{1,0:T(8,128)(2,1)S(1)}, u32[]{:S(2)}, u32[]{:S(2)}) collective-permute-start(bf16[32,1024]{1,0:T(8,128)(2,1)S(1)} %pad_maximum_fusion.3), channel_id=1, source_target_pairs={{0,1},{1,0},{2,3},{3,2},{4,5},{5,4},{6,7},{7,6},{8,9},{9,8},{10,11... | collective-permute-start | bytes 196616 | tf_op jit(solution)/shard_map/ppermute | solution.py:241
  17.1 0.9 %collective-permute-done.3 = bf16[32,1024]{1,0:T(8,128)(2,1)S(1)} collective-permute-done((bf16[32,1024]{1,0:T(8,128)(2,1)S(1)}, bf16[32,1024]{1,0:T(8,128)(2,1)S(1)}, u32[]{:S(2)}, u32[]{:S(2)}) %collective-permute-start.3) | collective-permute-done | bytes 65568 | tf_op jit(solution)/shard_map/ppermute | solution.py:241
  18.0 2.9 %collective-permute-start.4 = (bf16[64,1024]{1,0:T(8,128)(2,1)S(1)}, bf16[64,1024]{1,0:T(8,128)(2,1)S(1)}, u32[]{:S(2)}, u32[]{:S(2)}) collective-permute-start(bf16[64,1024]{1,0:T(8,128)(2,1)S(1)} %constant_dynamic-update-slice_fusion), channel_id=1, source_target_pairs={{0,0},{1,4},{2,32},{3,36},{4,1},{5,5},{6,33},{7,37},{8,8},{9,12},{... | collective-permute-start | bytes 393224 | tf_op jit(solution)/shard_map/ppermute | solution.py:255
  20.9 0.1 pad_add_fusion.5
  20.9 3.2 %collective-permute-start.5 = (bf16[64,1024]{1,0:T(8,128)(2,1)S(1)}, bf16[64,1024]{1,0:T(8,128)(2,1)S(1)}, u32[]{:S(2)}, u32[]{:S(2)}) collective-permute-start(bf16[64,1024]{1,0:T(8,128)(2,1)S(1)} %constant_dynamic-update-slice_fusion), channel_id=1, source_target_pairs={{0,32},{1,36},{2,0},{3,4},{4,33},{5,37},{6,1},{7,5},{8,40},{9,44},... | collective-permute-start | bytes 393224 | tf_op jit(solution)/shard_map/ppermute | solution.py:255
  24.2 0.0 collective-permute-done.8.rec2
  24.2 0.0 collective-permute-start.9
  24.2 0.1 pad_add_fusion.2.where_ref
  24.2 0.3 collective-permute-done.4
  24.6 3.0 %collective-permute-done.5 = bf16[64,1024]{1,0:T(8,128)(2,1)S(1)} collective-permute-done((bf16[64,1024]{1,0:T(8,128)(2,1)S(1)}, bf16[64,1024]{1,0:T(8,128)(2,1)S(1)}, u32[]{:S(2)}, u32[]{:S(2)}) %collective-permute-start.5) | collective-permute-done | bytes 131104 | tf_op jit(solution)/shard_map/ppermute | solution.py:255
  27.6 1.4 %collective-permute-start.16 = (bf16[128,1024]{1,0:T(8,128)(2,1)S(1)}, bf16[128,1024]{1,0:T(8,128)(2,1)S(1)}, u32[]{:S(2)}, u32[]{:S(2)}) collective-permute-start(bf16[128,1024]{1,0:T(8,128)(2,1)S(1)} %constant_dynamic-update-slice_fusion.5.src_ref), channel_id=1, source_target_pairs={{0,64},{4,68},{8,72},{12,76},{16,80},{20,84},{24,88},{28,92},{32,9... | collective-permute-start | bytes 786440 | tf_op jit(solution)/shard_map/ppermute | solution.py:245
  29.0 1.9 %collective-permute-start.13 = (bf16[128,1024]{1,0:T(8,128)(2,1)S(1)}, bf16[128,1024]{1,0:T(8,128)(2,1)S(1)}, u32[]{:S(2)}, u32[]{:S(2)}) collective-permute-start(bf16[128,1024]{1,0:T(8,128)(2,1)S(1)} %constant_dynamic-update-slice_fusion.5.src_ref), channel_id=1, source_target_pairs={{0,192},{4,196},{8,200},{12,204},{16,208},{20,212},{24,216},{28,22... | collective-permute-start | bytes 786440 | tf_op jit(solution)/shard_map/ppermute | solution.py:245
  30.9 0.7 %collective-permute-start.6 = (bf16[128,1024]{1,0:T(8,128)(2,1)S(1)}, bf16[128,1024]{1,0:T(8,128)(2,1)S(1)}, u32[]{:S(2)}, u32[]{:S(2)}) collective-permute-start(bf16[128,1024]{1,0:T(8,128)(2,1)S(1)} %constant_dynamic-update-slice_fusion.5.src_ref), channel_id=1, source_target_pairs={{0,128},{4,132},{8,136},{12,140},{16,144},{20,148},{24,152},{28,15... | collective-permute-start | bytes 786440 | tf_op jit(solution)/shard_map/ppermute | solution.py:245
  31.6 0.0 collective-permute-done.7.rec1
  31.6 0.0 collective-permute-done.9.rec3
  31.6 0.0 copy-done.1
  31.6 1.2 %widen_receivers.1 = (f32[16,2,16,1024]{3,2,1,0:T(8,128)S(1)}, f32[4,4,16,128]{3,2,1,0:T(8,128)S(1)}) custom-call(s32[4]{0:T(128)S(1)} %pad_add_fusion.2.where_ref, bf16[144,1024]{1,0:T(8,128)(2,1)S(1)} %fusion.1.rec0, bf16[144,1024]{1,0:T(8,128)(2,1)S(1)} %collective-permute-done.7.rec1, bf16[144,1024]{1,0:T(8,128)(2,1)S(1)} %collective-permute-done.8.rec2, ...), custom_call_target="tpu_custom_call" | custom-call | tf_op jit(solution)/shard_map/widen_receivers/pallas_call | solution.py:92
  32.8 0.0 copy-done.2
  32.8 2.9 %stack_group.4.refs_0_ = bf16[1,2,4,16,512]{4,3,2,1,0:T(8,128)(2,1)S(1)} custom-call(bf16[128,1024]{1,0:T(8,128)(2,1)S(1)} %constant_dynamic-update-slice_fusion.5.src_ref, f32[16,2,16,1024]{3,2,1,0:T(8,128)S(1)} %get-tuple-element.12.rec_ref, f32[4,16,128]{2,1,0:T(8,128)S(1)} %get-tuple-element.26.mask_ref, bf16[2,512,256]{2,1,0:T(8,128)(2,1)S(1)} %copy-done.2, ...), custom_call_target="tpu_custom_call" | custom-call | flops 2147483648 | bytes 3145728 | tf_op jit(solution)/shard_map/stack_group/pallas_call | solution.py:177
  35.7 2.7 %collective-permute-start.19 = (bf16[1,2,4,16,512]{4,3,2,1,0:T(8,128)(2,1)S(1)}, bf16[1,2,4,16,512]{4,3,2,1,0:T(8,128)(2,1)S(1)}, u32[]{:S(2)}, u32[]{:S(2)}) collective-permute-start(bf16[1,2,4,16,512]{4,3,2,1,0:T(8,128)(2,1)S(1)} %stack_group.4.refs_0_), channel_id=1, source_target_pairs={{0,2},{1,3},{2,0},{3,1},{4,6},{5,7},{6,4},{7,5},{8,10},{9,11},{10,... | collective-permute-start | bytes 393224 | tf_op jit(solution)/shard_map/ppermute | solution.py:241
  38.4 0.0 collective-permute-done.16.src_ref
  38.4 2.9 %stack_group.7 = bf16[1,2,4,16,512]{4,3,2,1,0:T(8,128)(2,1)S(1)} custom-call(bf16[128,1024]{1,0:T(8,128)(2,1)S(1)} %collective-permute-done.16.src_ref, f32[16,2,16,1024]{3,2,1,0:T(8,128)S(1)} %get-tuple-element.12.rec_ref, f32[4,16,128]{2,1,0:T(8,128)S(1)} %get-tuple-element.24.mask_ref, bf16[2,512,256]{2,1,0:T(8,128)(2,1)S(1)} %copy-done.2, ...), custom_call_target="tpu_custom_call" | custom-call | flops 2147483648 | bytes 3145728 | tf_op jit(solution)/shard_map/stack_group/pallas_call | solution.py:177
  41.4 0.1 collective-permute-start.17
  41.5 0.0 collective-permute-done.13.src_ref
  41.5 2.9 %stack_group.6 = bf16[1,2,4,16,512]{4,3,2,1,0:T(8,128)(2,1)S(1)} custom-call(bf16[128,1024]{1,0:T(8,128)(2,1)S(1)} %collective-permute-done.13.src_ref, f32[16,2,16,1024]{3,2,1,0:T(8,128)S(1)} %get-tuple-element.12.rec_ref, f32[4,16,128]{2,1,0:T(8,128)S(1)} %get-tuple-element.25.mask_ref, bf16[2,512,256]{2,1,0:T(8,128)(2,1)S(1)} %copy-done.2, ...), custom_call_target="tpu_custom_call" | custom-call | flops 2147483648 | bytes 3145728 | tf_op jit(solution)/shard_map/stack_group/pallas_call | solution.py:177
  44.4 1.5 %collective-permute-start.14 = (bf16[1,2,4,16,512]{4,3,2,1,0:T(8,128)(2,1)S(1)}, bf16[1,2,4,16,512]{4,3,2,1,0:T(8,128)(2,1)S(1)}, u32[]{:S(2)}, u32[]{:S(2)}) collective-permute-start(bf16[1,2,4,16,512]{4,3,2,1,0:T(8,128)(2,1)S(1)} %stack_group.6), channel_id=1, source_target_pairs={{0,2},{1,3},{2,0},{3,1},{4,6},{5,7},{6,4},{7,5},{8,10},{9,11},{10,... | collective-permute-start | bytes 393224 | tf_op jit(solution)/shard_map/ppermute | solution.py:241
  46.0 0.0 collective-permute-done.19
  46.0 2.9 %collective-permute-start.20 = (bf16[2,2,4,16,512]{4,3,2,1,0:T(8,128)(2,1)S(1)}, bf16[2,2,4,16,512]{4,3,2,1,0:T(8,128)(2,1)S(1)}, u32[]{:S(2)}, u32[]{:S(2)}) collective-permute-start(bf16[2,2,4,16,512]{4,3,2,1,0:T(8,128)(2,1)S(1)} %pad_maximum_fusion.2.refs_0_), channel_id=1, source_target_pairs={{0,1},{1,0},{2,3},{3,2},{4,5},{5,4},{6,7},{7,6},{8,9},{9,8},{10,11... | collective-permute-start | bytes 786440 | tf_op jit(solution)/shard_map/ppermute | solution.py:241
  48.9 0.0 collective-permute-done.6.src_ref
  48.9 2.9 %stack_group.5.refs_0_ = bf16[1,2,4,16,512]{4,3,2,1,0:T(8,128)(2,1)S(1)} custom-call(bf16[128,1024]{1,0:T(8,128)(2,1)S(1)} %collective-permute-done.6.src_ref, f32[16,2,16,1024]{3,2,1,0:T(8,128)S(1)} %get-tuple-element.12.rec_ref, f32[4,16,128]{2,1,0:T(8,128)S(1)} %get-tuple-element.27.mask_ref, bf16[2,512,256]{2,1,0:T(8,128)(2,1)S(1)} %copy-done.2, ...), custom_call_target="tpu_custom_call" | custom-call | flops 2147483648 | bytes 3145728 | tf_op jit(solution)/shard_map/stack_group/pallas_call | solution.py:177
  51.8 0.1 collective-permute-start.12
  51.9 1.4 %collective-permute-start.11 = (bf16[1,2,4,16,512]{4,3,2,1,0:T(8,128)(2,1)S(1)}, bf16[1,2,4,16,512]{4,3,2,1,0:T(8,128)(2,1)S(1)}, u32[]{:S(2)}, u32[]{:S(2)}) collective-permute-start(bf16[1,2,4,16,512]{4,3,2,1,0:T(8,128)(2,1)S(1)} %stack_group.5.refs_0_), channel_id=1, source_target_pairs={{0,2},{1,3},{2,0},{3,1},{4,6},{5,7},{6,4},{7,5},{8,10},{9,11},{10,... | collective-permute-start | bytes 393224 | tf_op jit(solution)/shard_map/ppermute | solution.py:241
  53.3 0.0 collective-permute-done.17
  53.3 0.8 %collective-permute-start.10 = (bf16[1,2,4,16,512]{4,3,2,1,0:T(8,128)(2,1)S(1)}, bf16[1,2,4,16,512]{4,3,2,1,0:T(8,128)(2,1)S(1)}, u32[]{:S(2)}, u32[]{:S(2)}) collective-permute-start(bf16[1,2,4,16,512]{4,3,2,1,0:T(8,128)(2,1)S(1)} %stack_group.5.refs_0_), channel_id=1, source_target_pairs={{0,1},{1,0},{2,3},{3,2},{4,5},{5,4},{6,7},{7,6},{8,9},{9,8},{10,11... | collective-permute-start | bytes 393224 | tf_op jit(solution)/shard_map/ppermute | solution.py:241
  54.1 0.0 collective-permute-done.14
  54.1 0.1 collective-permute-start.18
  54.2 0.0 collective-permute-done.20.refs_1_
  54.2 0.6 collective-permute-start.15
  54.8 0.1 pad_add_fusion.4
  54.9 0.0 copy-done
  54.9 1.9 %order_groups.4 = (f32[4,2,4,2,16,401]{5,4,3,2,1,0:T(8,128)}, f32[4,2,4,2,16,401]{5,4,3,2,1,0:T(8,128)}) custom-call(s32[3]{0:T(128)S(1)} %get-tuple-element.22.place_ref, bf16[512,512]{1,0:T(8,128)(2,1)S(1)} %copy-done, bf16[2,2,4,16,512]{4,3,2,1,0:T(8,128)(2,1)S(1)} %pad_maximum_fusion.2.refs_0_, ...), custom_call_target="tpu_custom_call" | custom-call | flops 268435456 | bytes 67108864 | tf_op jit(solution)/shard_map/order_groups/pallas_call | solution.py:224
  56.8 0.0 collective-permute-done.18.refs_1_
  56.8 1.9 %order_groups.5 = (f32[4,2,4,2,16,401]{5,4,3,2,1,0:T(8,128)}, f32[4,2,4,2,16,401]{5,4,3,2,1,0:T(8,128)}) custom-call(s32[3]{0:T(128)S(1)} %get-tuple-element.28.place_ref, bf16[512,512]{1,0:T(8,128)(2,1)S(1)} %copy-done, bf16[2,2,4,16,512]{4,3,2,1,0:T(8,128)(2,1)S(1)} %pad_maximum_fusion.1.refs_0_, ...), custom_call_target="tpu_custom_call", output_to_operand_aliasing={{0}: (4, {}), {1}: (5, {})} | custom-call | flops 268435456 | bytes 67108864 | tf_op jit(solution)/shard_map/order_groups/pallas_call | solution.py:224
  58.7 0.0 collective-permute-done.15.refs_1_
  58.7 1.9 %order_groups.6 = (f32[4,2,4,2,16,401]{5,4,3,2,1,0:T(8,128)}, f32[4,2,4,2,16,401]{5,4,3,2,1,0:T(8,128)}) custom-call(s32[3]{0:T(128)S(1)} %get-tuple-element.29.place_ref, bf16[512,512]{1,0:T(8,128)(2,1)S(1)} %copy-done, bf16[2,2,4,16,512]{4,3,2,1,0:T(8,128)(2,1)S(1)} %pad_maximum_fusion.refs_0_, ...), custom_call_target="tpu_custom_call", output_to_operand_aliasing={{0}: (4, {}), {1}: (5, {})} | custom-call | flops 268435456 | bytes 67108864 | tf_op jit(solution)/shard_map/order_groups/pallas_call | solution.py:224
  60.7 0.0 collective-permute-done.12.refs_3_
  60.7 0.0 collective-permute-done.11.refs_2_
  60.7 0.0 collective-permute-done.10.refs_1_
  60.7 1.9 %order_groups.7 = (f32[4,2,4,2,16,401]{5,4,3,2,1,0:T(8,128)}, f32[4,2,4,2,16,401]{5,4,3,2,1,0:T(8,128)}) custom-call(s32[3]{0:T(128)S(1)} %get-tuple-element.30.place_ref, bf16[512,512]{1,0:T(8,128)(2,1)S(1)} %copy-done, bf16[1,2,4,16,512]{4,3,2,1,0:T(8,128)(2,1)S(1)} %stack_group.5.refs_0_, ...), custom_call_target="tpu_custom_call", output_to_operand_aliasing={{0}: (6, {}), {1}: (7, {})} | custom-call | flops 268435456 | bytes 67108864 | tf_op jit(solution)/shard_map/order_groups/pallas_call | solution.py:224
  (14 shorter events, 0.2 us)
Async XLA Ops:
  0.6 31.0 %copy-start.1 = (bf16[512,512]{1,0:T(8,128)(2,1)S(1)}, bf16[512,512]{1,0:T(8,128)(2,1)}, u32[]{:S(2)}) copy-start(bf16[512,512]{1,0:T(8,128)(2,1)} %constant.27.clone.flip_ref) | copy-start | bytes 1572868
  1.4 14.0 %collective-permute-start.2 = (bf16[8,1024]{1,0:T(8,128)(2,1)S(1)}, bf16[8,1024]{1,0:T(8,128)(2,1)S(1)}, u32[]{:S(2)}, u32[]{:S(2)}) collective-permute-start(bf16[8,1024]{1,0:T(8,128)(2,1)S(1)} %reshape.18), channel_id=1, source_target_pairs={{0,24},{4,28},{8,16},{12,20},{16,8},{20,12},{24,0},{28,4},{32,56},... | collective-permute-start | bytes 49160 | tf_op jit(solution)/shard_map/ppermute | solution.py:245
  8.4 7.0 %collective-permute-start.1 = (bf16[8,1024]{1,0:T(8,128)(2,1)S(1)}, bf16[8,1024]{1,0:T(8,128)(2,1)S(1)}, u32[]{:S(2)}, u32[]{:S(2)}) collective-permute-start(bf16[8,1024]{1,0:T(8,128)(2,1)S(1)} %reshape.18), channel_id=1, source_target_pairs={{0,16},{4,20},{8,24},{12,28},{16,0},{20,4},{24,8},{28,12},{32,48},... | collective-permute-start | bytes 49160 | tf_op jit(solution)/shard_map/ppermute | solution.py:245
  9.4 6.1 %collective-permute-start = (bf16[8,1024]{1,0:T(8,128)(2,1)S(1)}, bf16[8,1024]{1,0:T(8,128)(2,1)S(1)}, u32[]{:S(2)}, u32[]{:S(2)}) collective-permute-start(bf16[8,1024]{1,0:T(8,128)(2,1)S(1)} %reshape.18), channel_id=1, source_target_pairs={{0,8},{4,12},{8,0},{12,4},{16,24},{20,28},{24,16},{28,20},{32,40},... | collective-permute-start | bytes 49160 | tf_op jit(solution)/shard_map/ppermute | solution.py:245
  11.3 21.5 %copy-start.2 = (bf16[2,512,256]{2,1,0:T(8,128)(2,1)S(1)}, bf16[2,512,256]{2,1,0:T(8,128)(2,1)}, u32[]{:S(2)}) copy-start(bf16[2,512,256]{2,1,0:T(8,128)(2,1)} %constant.26.clone.basis_ref) | copy-start | bytes 1572868
  12.6 11.6 %collective-permute-start.8 = (bf16[144,1024]{1,0:T(8,128)(2,1)S(1)}, bf16[144,1024]{1,0:T(8,128)(2,1)S(1)}, u32[]{:S(2)}, u32[]{:S(2)}) collective-permute-start(bf16[144,1024]{1,0:T(8,128)(2,1)S(1)} %fusion.1.rec0), channel_id=1, source_target_pairs={{0,2},{1,3},{2,0},{3,1},{4,6},{5,7},{6,4},{7,5},{8,10},{9,11},{10,... | collective-permute-start | bytes 884744 | tf_op jit(solution)/shard_map/ppermute | solution.py:241
  13.9 17.7 %collective-permute-start.7 = (bf16[144,1024]{1,0:T(8,128)(2,1)S(1)}, bf16[144,1024]{1,0:T(8,128)(2,1)S(1)}, u32[]{:S(2)}, u32[]{:S(2)}) collective-permute-start(bf16[144,1024]{1,0:T(8,128)(2,1)S(1)} %fusion.1.rec0), channel_id=1, source_target_pairs={{0,1},{1,0},{2,3},{3,2},{4,5},{5,4},{6,7},{7,6},{8,9},{9,8},{10,11... | collective-permute-start | bytes 884744 | tf_op jit(solution)/shard_map/ppermute | solution.py:241
  15.4 2.5 %collective-permute-start.3 = (bf16[32,1024]{1,0:T(8,128)(2,1)S(1)}, bf16[32,1024]{1,0:T(8,128)(2,1)S(1)}, u32[]{:S(2)}, u32[]{:S(2)}) collective-permute-start(bf16[32,1024]{1,0:T(8,128)(2,1)S(1)} %pad_maximum_fusion.3), channel_id=1, source_target_pairs={{0,1},{1,0},{2,3},{3,2},{4,5},{5,4},{6,7},{7,6},{8,9},{9,8},{10,11... | collective-permute-start | bytes 196616 | tf_op jit(solution)/shard_map/ppermute | solution.py:241
  18.0 6.6 %collective-permute-start.4 = (bf16[64,1024]{1,0:T(8,128)(2,1)S(1)}, bf16[64,1024]{1,0:T(8,128)(2,1)S(1)}, u32[]{:S(2)}, u32[]{:S(2)}) collective-permute-start(bf16[64,1024]{1,0:T(8,128)(2,1)S(1)} %constant_dynamic-update-slice_fusion), channel_id=1, source_target_pairs={{0,0},{1,4},{2,32},{3,36},{4,1},{5,5},{6,33},{7,37},{8,8},{9,12},{... | collective-permute-start | bytes 393224 | tf_op jit(solution)/shard_map/ppermute | solution.py:255
  20.9 6.6 %collective-permute-start.5 = (bf16[64,1024]{1,0:T(8,128)(2,1)S(1)}, bf16[64,1024]{1,0:T(8,128)(2,1)S(1)}, u32[]{:S(2)}, u32[]{:S(2)}) collective-permute-start(bf16[64,1024]{1,0:T(8,128)(2,1)S(1)} %constant_dynamic-update-slice_fusion), channel_id=1, source_target_pairs={{0,32},{1,36},{2,0},{3,4},{4,33},{5,37},{6,1},{7,5},{8,40},{9,44},... | collective-permute-start | bytes 393224 | tf_op jit(solution)/shard_map/ppermute | solution.py:255
  24.2 7.4 %collective-permute-start.9 = (bf16[144,1024]{1,0:T(8,128)(2,1)S(1)}, bf16[144,1024]{1,0:T(8,128)(2,1)S(1)}, u32[]{:S(2)}, u32[]{:S(2)}) collective-permute-start(bf16[144,1024]{1,0:T(8,128)(2,1)S(1)} %collective-permute-done.8.rec2), channel_id=1, source_target_pairs={{0,1},{1,0},{2,3},{3,2},{4,5},{5,4},{6,7},{7,6},{8,9},{9,8},{10,11... | collective-permute-start | bytes 884744 | tf_op jit(solution)/shard_map/ppermute | solution.py:241
  27.6 10.9 %collective-permute-start.16 = (bf16[128,1024]{1,0:T(8,128)(2,1)S(1)}, bf16[128,1024]{1,0:T(8,128)(2,1)S(1)}, u32[]{:S(2)}, u32[]{:S(2)}) collective-permute-start(bf16[128,1024]{1,0:T(8,128)(2,1)S(1)} %constant_dynamic-update-slice_fusion.5.src_ref), channel_id=1, source_target_pairs={{0,64},{4,68},{8,72},{12,76},{16,80},{20,84},{24,88},{28,92},{32,9... | collective-permute-start | bytes 786440 | tf_op jit(solution)/shard_map/ppermute | solution.py:245
  29.0 12.5 %collective-permute-start.13 = (bf16[128,1024]{1,0:T(8,128)(2,1)S(1)}, bf16[128,1024]{1,0:T(8,128)(2,1)S(1)}, u32[]{:S(2)}, u32[]{:S(2)}) collective-permute-start(bf16[128,1024]{1,0:T(8,128)(2,1)S(1)} %constant_dynamic-update-slice_fusion.5.src_ref), channel_id=1, source_target_pairs={{0,192},{4,196},{8,200},{12,204},{16,208},{20,212},{24,216},{28,22... | collective-permute-start | bytes 786440 | tf_op jit(solution)/shard_map/ppermute | solution.py:245
  30.9 18.0 %collective-permute-start.6 = (bf16[128,1024]{1,0:T(8,128)(2,1)S(1)}, bf16[128,1024]{1,0:T(8,128)(2,1)S(1)}, u32[]{:S(2)}, u32[]{:S(2)}) collective-permute-start(bf16[128,1024]{1,0:T(8,128)(2,1)S(1)} %constant_dynamic-update-slice_fusion.5.src_ref), channel_id=1, source_target_pairs={{0,128},{4,132},{8,136},{12,140},{16,144},{20,148},{24,152},{28,15... | collective-permute-start | bytes 786440 | tf_op jit(solution)/shard_map/ppermute | solution.py:245
  35.7 10.2 %collective-permute-start.19 = (bf16[1,2,4,16,512]{4,3,2,1,0:T(8,128)(2,1)S(1)}, bf16[1,2,4,16,512]{4,3,2,1,0:T(8,128)(2,1)S(1)}, u32[]{:S(2)}, u32[]{:S(2)}) collective-permute-start(bf16[1,2,4,16,512]{4,3,2,1,0:T(8,128)(2,1)S(1)} %stack_group.4.refs_0_), channel_id=1, source_target_pairs={{0,2},{1,3},{2,0},{3,1},{4,6},{5,7},{6,4},{7,5},{8,10},{9,11},{10,... | collective-permute-start | bytes 393224 | tf_op jit(solution)/shard_map/ppermute | solution.py:241
  41.4 11.9 %collective-permute-start.17 = (bf16[1,2,4,16,512]{4,3,2,1,0:T(8,128)(2,1)S(1)}, bf16[1,2,4,16,512]{4,3,2,1,0:T(8,128)(2,1)S(1)}, u32[]{:S(2)}, u32[]{:S(2)}) collective-permute-start(bf16[1,2,4,16,512]{4,3,2,1,0:T(8,128)(2,1)S(1)} %stack_group.7), channel_id=1, source_target_pairs={{0,2},{1,3},{2,0},{3,1},{4,6},{5,7},{6,4},{7,5},{8,10},{9,11},{10,... | collective-permute-start | bytes 393224 | tf_op jit(solution)/shard_map/ppermute | solution.py:241
  44.4 9.6 %collective-permute-start.14 = (bf16[1,2,4,16,512]{4,3,2,1,0:T(8,128)(2,1)S(1)}, bf16[1,2,4,16,512]{4,3,2,1,0:T(8,128)(2,1)S(1)}, u32[]{:S(2)}, u32[]{:S(2)}) collective-permute-start(bf16[1,2,4,16,512]{4,3,2,1,0:T(8,128)(2,1)S(1)} %stack_group.6), channel_id=1, source_target_pairs={{0,2},{1,3},{2,0},{3,1},{4,6},{5,7},{6,4},{7,5},{8,10},{9,11},{10,... | collective-permute-start | bytes 393224 | tf_op jit(solution)/shard_map/ppermute | solution.py:241
  46.0 8.2 %collective-permute-start.20 = (bf16[2,2,4,16,512]{4,3,2,1,0:T(8,128)(2,1)S(1)}, bf16[2,2,4,16,512]{4,3,2,1,0:T(8,128)(2,1)S(1)}, u32[]{:S(2)}, u32[]{:S(2)}) collective-permute-start(bf16[2,2,4,16,512]{4,3,2,1,0:T(8,128)(2,1)S(1)} %pad_maximum_fusion.2.refs_0_), channel_id=1, source_target_pairs={{0,1},{1,0},{2,3},{3,2},{4,5},{5,4},{6,7},{7,6},{8,9},{9,8},{10,11... | collective-permute-start | bytes 786440 | tf_op jit(solution)/shard_map/ppermute | solution.py:241
  48.9 6.0 %copy-start = (bf16[512,512]{1,0:T(8,128)(2,1)S(1)}, bf16[512,512]{1,0:T(8,128)(2,1)}, u32[]{:S(2)}) copy-start(bf16[512,512]{1,0:T(8,128)(2,1)} %constant.28.clone.order_ref) | copy-start | bytes 1572868
  51.8 8.9 %collective-permute-start.12 = (bf16[1,2,4,16,512]{4,3,2,1,0:T(8,128)(2,1)S(1)}, bf16[1,2,4,16,512]{4,3,2,1,0:T(8,128)(2,1)S(1)}, u32[]{:S(2)}, u32[]{:S(2)}) collective-permute-start(bf16[1,2,4,16,512]{4,3,2,1,0:T(8,128)(2,1)S(1)} %stack_group.5.refs_0_), channel_id=1, source_target_pairs={{0,3},{1,2},{2,1},{3,0},{4,7},{5,6},{6,5},{7,4},{8,11},{9,10},{10,... | collective-permute-start | bytes 393224 | tf_op jit(solution)/shard_map/ppermute | solution.py:241
  51.9 8.8 %collective-permute-start.11 = (bf16[1,2,4,16,512]{4,3,2,1,0:T(8,128)(2,1)S(1)}, bf16[1,2,4,16,512]{4,3,2,1,0:T(8,128)(2,1)S(1)}, u32[]{:S(2)}, u32[]{:S(2)}) collective-permute-start(bf16[1,2,4,16,512]{4,3,2,1,0:T(8,128)(2,1)S(1)} %stack_group.5.refs_0_), channel_id=1, source_target_pairs={{0,2},{1,3},{2,0},{3,1},{4,6},{5,7},{6,4},{7,5},{8,10},{9,11},{10,... | collective-permute-start | bytes 393224 | tf_op jit(solution)/shard_map/ppermute | solution.py:241
  53.3 7.4 %collective-permute-start.10 = (bf16[1,2,4,16,512]{4,3,2,1,0:T(8,128)(2,1)S(1)}, bf16[1,2,4,16,512]{4,3,2,1,0:T(8,128)(2,1)S(1)}, u32[]{:S(2)}, u32[]{:S(2)}) collective-permute-start(bf16[1,2,4,16,512]{4,3,2,1,0:T(8,128)(2,1)S(1)} %stack_group.5.refs_0_), channel_id=1, source_target_pairs={{0,1},{1,0},{2,3},{3,2},{4,5},{5,4},{6,7},{7,6},{8,9},{9,8},{10,11... | collective-permute-start | bytes 393224 | tf_op jit(solution)/shard_map/ppermute | solution.py:241
  54.1 2.7 %collective-permute-start.18 = (bf16[2,2,4,16,512]{4,3,2,1,0:T(8,128)(2,1)S(1)}, bf16[2,2,4,16,512]{4,3,2,1,0:T(8,128)(2,1)S(1)}, u32[]{:S(2)}, u32[]{:S(2)}) collective-permute-start(bf16[2,2,4,16,512]{4,3,2,1,0:T(8,128)(2,1)S(1)} %pad_maximum_fusion.1.refs_0_), channel_id=1, source_target_pairs={{0,1},{1,0},{2,3},{3,2},{4,5},{5,4},{6,7},{7,6},{8,9},{9,8},{10,11... | collective-permute-start | bytes 786440 | tf_op jit(solution)/shard_map/ppermute | solution.py:241
  54.2 4.5 %collective-permute-start.15 = (bf16[2,2,4,16,512]{4,3,2,1,0:T(8,128)(2,1)S(1)}, bf16[2,2,4,16,512]{4,3,2,1,0:T(8,128)(2,1)S(1)}, u32[]{:S(2)}, u32[]{:S(2)}) collective-permute-start(bf16[2,2,4,16,512]{4,3,2,1,0:T(8,128)(2,1)S(1)} %pad_maximum_fusion.refs_0_), channel_id=1, source_target_pairs={{0,1},{1,0},{2,3},{3,2},{4,5},{5,4},{6,7},{7,6},{8,9},{9,8},{10,11... | collective-permute-start | bytes 786440 | tf_op jit(solution)/shard_map/ppermute | solution.py:241

commit v5 on v4

--- a/solution.py
+++ b/solution.py
@@ -110,21 +110,21 @@
     lower, upper = fold_order(src_ref[...], flip_ref[...])
     src_f32[:, :half] = lower
     src_f32[:, half:] = upper
-    alone = lax.broadcasted_iota(jnp.int32, (16, 256), 1) == 0
+    alone = lax.broadcasted_iota(jnp.int32, (16, 512), 1) == 0
     for s in range(PER):
         p = s % 2
         for d in range(days):
             row = (d // PER * PER + s) * 2 * PER + d % PER * 2
-            for lane in range(0, half, 256):
+            for lane in range(0, half, 512):
                 pair = []
                 for start in (lane, half + lane):
-                    cols = slice(start, start + 256)
+                    cols = slice(start, start + 512)
                     a = src_f32[row : row + 1, cols]
                     b = src_f32[row + 1 : row + 2, cols]
                     c = rec_ref[d, 0, :, cols]
                     e = rec_ref[d, 1, :, cols]
                     pair.append((a * c + b * e, a * e - b * c))
-                cols = slice(lane, lane + 256)
+                cols = slice(lane, lane + 512)
                 for i, (f, g) in enumerate(zip(*pair)):
                     f, g = f.astype(jnp.bfloat16), g.astype(jnp.bfloat16)
                     plus, minus = f + g, f - g

time: 62.8 us -> 62.7 us (level)
  no operation moved by 1% of the time
where the time goes in v5:
time: 62.7 us; the launch traced here: 62.5 us
  starting transfers between devices  33.8 us (54%)
  Pallas kernels  20.5 us (33%)
  waiting for transfers between devices  4.25 us (7%)
  local copies, waits for them, and re-layouts  2.08 us (3%)
  other arithmetic  1.1 us (2%)
  between operations  0.82 us (1%)
    ppermute x13, starting transfers between devices, day_swap(): return lax.ppermute(x, 'day', [(i, i ^ k) for i in range(DAYS)])  14.6 us
    ppermute x6, starting transfers between devices, tile_swap(): return lax.ppermute(x, 'tile', [(i, i ^ k) for i in range(TILES)])  13.1 us
    pallas_call x4, Pallas kernels, stack_group(): pl.pallas_call(stack_kernel, out_shape=jax.ShapeDtypeStruct((1, 2, PER, 1...  11.6 us
    pallas_call x4, Pallas kernels, order_groups(): pl.pallas_call(functools.partial(order_kernel, len(parts)), out_shape=(sh...  7.71 us
    ppermute x2, starting transfers between devices, turn(): return lax.ppermute(x, ('tile', 'day'), pairs)  6.1 us
    ppermute x2, waiting for transfers between devices, turn(): return lax.ppermute(x, ('tile', 'day'), pairs)  3.29 us
  transfers between devices with their start and end apart: 21, of which 3 were waited for; matrix products, arithmetic and copies ran while one was open for 4% of the time, Pallas kernels for 30%

profile of v5, /device:TPU:1, one launch (start us, length us, event | category | flops | bytes accessed | tf_op | source)
XLA Modules:
  0.0 62.5 jit_solution(13583844267348617295)
XLA Ops:
  0.6 0.0 copy-start.1
  0.6 0.8 %reshape.18 = bf16[8,1024]{1,0:T(8,128)(2,1)S(1)} reshape(bf16[4,1,2,1024]{3,2,1,0:T(2,128)(2,1)} %param.6) | data formatting | bytes 32768 | tf_op jit(solution)/shard_map/reshape | solution.py:272
  1.4 6.9 %collective-permute-start.2 = (bf16[8,1024]{1,0:T(8,128)(2,1)S(1)}, bf16[8,1024]{1,0:T(8,128)(2,1)S(1)}, u32[]{:S(2)}, u32[]{:S(2)}) collective-permute-start(bf16[8,1024]{1,0:T(8,128)(2,1)S(1)} %reshape.18), channel_id=1, source_target_pairs={{0,24},{4,28},{8,16},{12,20},{16,8},{20,12},{24,0},{28,4},{32,56},... | collective-permute-start | bytes 49160 | tf_op jit(solution)/shard_map/ppermute | solution.py:245
  8.4 1.0 %collective-permute-start.1 = (bf16[8,1024]{1,0:T(8,128)(2,1)S(1)}, bf16[8,1024]{1,0:T(8,128)(2,1)S(1)}, u32[]{:S(2)}, u32[]{:S(2)}) collective-permute-start(bf16[8,1024]{1,0:T(8,128)(2,1)S(1)} %reshape.18), channel_id=1, source_target_pairs={{0,16},{4,20},{8,24},{12,28},{16,0},{20,4},{24,8},{28,12},{32,48},... | collective-permute-start | bytes 49160 | tf_op jit(solution)/shard_map/ppermute | solution.py:245
  9.4 1.2 %collective-permute-start = (bf16[8,1024]{1,0:T(8,128)(2,1)S(1)}, bf16[8,1024]{1,0:T(8,128)(2,1)S(1)}, u32[]{:S(2)}, u32[]{:S(2)}) collective-permute-start(bf16[8,1024]{1,0:T(8,128)(2,1)S(1)} %reshape.18), channel_id=1, source_target_pairs={{0,8},{4,12},{8,0},{12,4},{16,24},{20,28},{24,16},{28,20},{32,40},... | collective-permute-start | bytes 49160 | tf_op jit(solution)/shard_map/ppermute | solution.py:245
  10.5 0.8 %convert_element_type.8 = bf16[4,64,16]{1,2,0:T(8,128)(2,1)S(1)} convert(s32[4,64,16]{1,2,0:T(8,128)} %param.8) | non-fusion elementwise | flops 4096 | bytes 24576 | tf_op jit(solution)/shard_map/convert_element_type | solution.py:266
  11.3 0.0 copy-start.2
  11.3 0.1 copy.17
  11.4 0.1 convert_element_type.9
  11.5 1.0 %copy.16 = bf16[4,2,16,1024]{3,2,1,0:T(8,128)(2,1)S(1)} copy(bf16[4,2,16,1024]{3,1,2,0:T(2,128)(2,1)} %bitcast.22) | data formatting | bytes 524288 | tf_op jit(solution)/shard_map/transpose | solution.py:265
  12.6 1.3 %collective-permute-start.8 = (bf16[144,1024]{1,0:T(8,128)(2,1)S(1)}, bf16[144,1024]{1,0:T(8,128)(2,1)S(1)}, u32[]{:S(2)}, u32[]{:S(2)}) collective-permute-start(bf16[144,1024]{1,0:T(8,128)(2,1)S(1)} %fusion.1.rec0), channel_id=1, source_target_pairs={{0,2},{1,3},{2,0},{3,1},{4,6},{5,7},{6,4},{7,5},{8,10},{9,11},{10,... | collective-permute-start | bytes 884744 | tf_op jit(solution)/shard_map/ppermute | solution.py:241
  13.9 1.5 %collective-permute-start.7 = (bf16[144,1024]{1,0:T(8,128)(2,1)S(1)}, bf16[144,1024]{1,0:T(8,128)(2,1)S(1)}, u32[]{:S(2)}, u32[]{:S(2)}) collective-permute-start(bf16[144,1024]{1,0:T(8,128)(2,1)S(1)} %fusion.1.rec0), channel_id=1, source_target_pairs={{0,1},{1,0},{2,3},{3,2},{4,5},{5,4},{6,7},{7,6},{8,9},{9,8},{10,11... | collective-permute-start | bytes 884744 | tf_op jit(solution)/shard_map/ppermute | solution.py:241
  15.4 0.0 collective-permute-done.2
  15.4 0.0 collective-permute-done.1
  15.4 0.0 collective-permute-done
  15.4 1.6 %collective-permute-start.3 = (bf16[32,1024]{1,0:T(8,128)(2,1)S(1)}, bf16[32,1024]{1,0:T(8,128)(2,1)S(1)}, u32[]{:S(2)}, u32[]{:S(2)}) collective-permute-start(bf16[32,1024]{1,0:T(8,128)(2,1)S(1)} %pad_maximum_fusion.3), channel_id=1, source_target_pairs={{0,1},{1,0},{2,3},{3,2},{4,5},{5,4},{6,7},{7,6},{8,9},{9,8},{10,11... | collective-permute-start | bytes 196616 | tf_op jit(solution)/shard_map/ppermute | solution.py:241
  17.1 0.9 %collective-permute-done.3 = bf16[32,1024]{1,0:T(8,128)(2,1)S(1)} collective-permute-done((bf16[32,1024]{1,0:T(8,128)(2,1)S(1)}, bf16[32,1024]{1,0:T(8,128)(2,1)S(1)}, u32[]{:S(2)}, u32[]{:S(2)}) %collective-permute-start.3) | collective-permute-done | bytes 65568 | tf_op jit(solution)/shard_map/ppermute | solution.py:241
  18.0 2.9 %collective-permute-start.4 = (bf16[64,1024]{1,0:T(8,128)(2,1)S(1)}, bf16[64,1024]{1,0:T(8,128)(2,1)S(1)}, u32[]{:S(2)}, u32[]{:S(2)}) collective-permute-start(bf16[64,1024]{1,0:T(8,128)(2,1)S(1)} %constant_dynamic-update-slice_fusion), channel_id=1, source_target_pairs={{0,0},{1,4},{2,32},{3,36},{4,1},{5,5},{6,33},{7,37},{8,8},{9,12},{... | collective-permute-start | bytes 393224 | tf_op jit(solution)/shard_map/ppermute | solution.py:255
  20.9 0.1 pad_add_fusion.5
  20.9 3.2 %collective-permute-start.5 = (bf16[64,1024]{1,0:T(8,128)(2,1)S(1)}, bf16[64,1024]{1,0:T(8,128)(2,1)S(1)}, u32[]{:S(2)}, u32[]{:S(2)}) collective-permute-start(bf16[64,1024]{1,0:T(8,128)(2,1)S(1)} %constant_dynamic-update-slice_fusion), channel_id=1, source_target_pairs={{0,32},{1,36},{2,0},{3,4},{4,33},{5,37},{6,1},{7,5},{8,40},{9,44},... | collective-permute-start | bytes 393224 | tf_op jit(solution)/shard_map/ppermute | solution.py:255
  24.2 0.0 collective-permute-done.8.rec2
  24.2 0.0 collective-permute-start.9
  24.2 0.1 pad_add_fusion.2.where_ref
  24.2 0.3 collective-permute-done.4
  24.6 3.0 %collective-permute-done.5 = bf16[64,1024]{1,0:T(8,128)(2,1)S(1)} collective-permute-done((bf16[64,1024]{1,0:T(8,128)(2,1)S(1)}, bf16[64,1024]{1,0:T(8,128)(2,1)S(1)}, u32[]{:S(2)}, u32[]{:S(2)}) %collective-permute-start.5) | collective-permute-done | bytes 131104 | tf_op jit(solution)/shard_map/ppermute | solution.py:255
  27.6 1.4 %collective-permute-start.16 = (bf16[128,1024]{1,0:T(8,128)(2,1)S(1)}, bf16[128,1024]{1,0:T(8,128)(2,1)S(1)}, u32[]{:S(2)}, u32[]{:S(2)}) collective-permute-start(bf16[128,1024]{1,0:T(8,128)(2,1)S(1)} %constant_dynamic-update-slice_fusion.5.src_ref), channel_id=1, source_target_pairs={{0,64},{4,68},{8,72},{12,76},{16,80},{20,84},{24,88},{28,92},{32,9... | collective-permute-start | bytes 786440 | tf_op jit(solution)/shard_map/ppermute | solution.py:245
  29.0 1.9 %collective-permute-start.13 = (bf16[128,1024]{1,0:T(8,128)(2,1)S(1)}, bf16[128,1024]{1,0:T(8,128)(2,1)S(1)}, u32[]{:S(2)}, u32[]{:S(2)}) collective-permute-start(bf16[128,1024]{1,0:T(8,128)(2,1)S(1)} %constant_dynamic-update-slice_fusion.5.src_ref), channel_id=1, source_target_pairs={{0,192},{4,196},{8,200},{12,204},{16,208},{20,212},{24,216},{28,22... | collective-permute-start | bytes 786440 | tf_op jit(solution)/shard_map/ppermute | solution.py:245
  30.9 0.7 %collective-permute-start.6 = (bf16[128,1024]{1,0:T(8,128)(2,1)S(1)}, bf16[128,1024]{1,0:T(8,128)(2,1)S(1)}, u32[]{:S(2)}, u32[]{:S(2)}) collective-permute-start(bf16[128,1024]{1,0:T(8,128)(2,1)S(1)} %constant_dynamic-update-slice_fusion.5.src_ref), channel_id=1, source_target_pairs={{0,128},{4,132},{8,136},{12,140},{16,144},{20,148},{24,152},{28,15... | collective-permute-start | bytes 786440 | tf_op jit(solution)/shard_map/ppermute | solution.py:245
  31.6 0.0 collective-permute-done.7.rec1
  31.6 0.0 collective-permute-done.9.rec3
  31.6 0.0 copy-done.1
  31.6 1.2 %widen_receivers.1 = (f32[16,2,16,1024]{3,2,1,0:T(8,128)S(1)}, f32[4,4,16,128]{3,2,1,0:T(8,128)S(1)}) custom-call(s32[4]{0:T(128)S(1)} %pad_add_fusion.2.where_ref, bf16[144,1024]{1,0:T(8,128)(2,1)S(1)} %fusion.1.rec0, bf16[144,1024]{1,0:T(8,128)(2,1)S(1)} %collective-permute-done.7.rec1, bf16[144,1024]{1,0:T(8,128)(2,1)S(1)} %collective-permute-done.8.rec2, ...), custom_call_target="tpu_custom_call" | custom-call | tf_op jit(solution)/shard_map/widen_receivers/pallas_call | solution.py:92
  32.8 0.0 copy-done.2
  32.8 2.9 %stack_group.4.refs_0_ = bf16[1,2,4,16,512]{4,3,2,1,0:T(8,128)(2,1)S(1)} custom-call(bf16[128,1024]{1,0:T(8,128)(2,1)S(1)} %constant_dynamic-update-slice_fusion.5.src_ref, f32[16,2,16,1024]{3,2,1,0:T(8,128)S(1)} %get-tuple-element.12.rec_ref, f32[4,16,128]{2,1,0:T(8,128)S(1)} %get-tuple-element.26.mask_ref, bf16[2,512,256]{2,1,0:T(8,128)(2,1)S(1)} %copy-done.2, ...), custom_call_target="tpu_custom_call" | custom-call | flops 2147483648 | bytes 3145728 | tf_op jit(solution)/shard_map/stack_group/pallas_call | solution.py:177
  35.7 2.7 %collective-permute-start.19 = (bf16[1,2,4,16,512]{4,3,2,1,0:T(8,128)(2,1)S(1)}, bf16[1,2,4,16,512]{4,3,2,1,0:T(8,128)(2,1)S(1)}, u32[]{:S(2)}, u32[]{:S(2)}) collective-permute-start(bf16[1,2,4,16,512]{4,3,2,1,0:T(8,128)(2,1)S(1)} %stack_group.4.refs_0_), channel_id=1, source_target_pairs={{0,2},{1,3},{2,0},{3,1},{4,6},{5,7},{6,4},{7,5},{8,10},{9,11},{10,... | collective-permute-start | bytes 393224 | tf_op jit(solution)/shard_map/ppermute | solution.py:241
  38.4 0.0 collective-permute-done.16.src_ref
  38.4 2.9 %stack_group.7 = bf16[1,2,4,16,512]{4,3,2,1,0:T(8,128)(2,1)S(1)} custom-call(bf16[128,1024]{1,0:T(8,128)(2,1)S(1)} %collective-permute-done.16.src_ref, f32[16,2,16,1024]{3,2,1,0:T(8,128)S(1)} %get-tuple-element.12.rec_ref, f32[4,16,128]{2,1,0:T(8,128)S(1)} %get-tuple-element.24.mask_ref, bf16[2,512,256]{2,1,0:T(8,128)(2,1)S(1)} %copy-done.2, ...), custom_call_target="tpu_custom_call" | custom-call | flops 2147483648 | bytes 3145728 | tf_op jit(solution)/shard_map/stack_group/pallas_call | solution.py:177
  41.3 0.1 collective-permute-start.17
  41.4 0.0 collective-permute-done.13.src_ref
  41.4 2.9 %stack_group.6 = bf16[1,2,4,16,512]{4,3,2,1,0:T(8,128)(2,1)S(1)} custom-call(bf16[128,1024]{1,0:T(8,128)(2,1)S(1)} %collective-permute-done.13.src_ref, f32[16,2,16,1024]{3,2,1,0:T(8,128)S(1)} %get-tuple-element.12.rec_ref, f32[4,16,128]{2,1,0:T(8,128)S(1)} %get-tuple-element.25.mask_ref, bf16[2,512,256]{2,1,0:T(8,128)(2,1)S(1)} %copy-done.2, ...), custom_call_target="tpu_custom_call" | custom-call | flops 2147483648 | bytes 3145728 | tf_op jit(solution)/shard_map/stack_group/pallas_call | solution.py:177
  44.4 1.5 %collective-permute-start.14 = (bf16[1,2,4,16,512]{4,3,2,1,0:T(8,128)(2,1)S(1)}, bf16[1,2,4,16,512]{4,3,2,1,0:T(8,128)(2,1)S(1)}, u32[]{:S(2)}, u32[]{:S(2)}) collective-permute-start(bf16[1,2,4,16,512]{4,3,2,1,0:T(8,128)(2,1)S(1)} %stack_group.6), channel_id=1, source_target_pairs={{0,2},{1,3},{2,0},{3,1},{4,6},{5,7},{6,4},{7,5},{8,10},{9,11},{10,... | collective-permute-start | bytes 393224 | tf_op jit(solution)/shard_map/ppermute | solution.py:241
  45.9 0.0 collective-permute-done.19
  45.9 2.9 %collective-permute-start.20 = (bf16[2,2,4,16,512]{4,3,2,1,0:T(8,128)(2,1)S(1)}, bf16[2,2,4,16,512]{4,3,2,1,0:T(8,128)(2,1)S(1)}, u32[]{:S(2)}, u32[]{:S(2)}) collective-permute-start(bf16[2,2,4,16,512]{4,3,2,1,0:T(8,128)(2,1)S(1)} %pad_maximum_fusion.2.refs_0_), channel_id=1, source_target_pairs={{0,1},{1,0},{2,3},{3,2},{4,5},{5,4},{6,7},{7,6},{8,9},{9,8},{10,11... | collective-permute-start | bytes 786440 | tf_op jit(solution)/shard_map/ppermute | solution.py:241
  48.8 0.0 collective-permute-done.6.src_ref
  48.8 2.9 %stack_group.5.refs_0_ = bf16[1,2,4,16,512]{4,3,2,1,0:T(8,128)(2,1)S(1)} custom-call(bf16[128,1024]{1,0:T(8,128)(2,1)S(1)} %collective-permute-done.6.src_ref, f32[16,2,16,1024]{3,2,1,0:T(8,128)S(1)} %get-tuple-element.12.rec_ref, f32[4,16,128]{2,1,0:T(8,128)S(1)} %get-tuple-element.27.mask_ref, bf16[2,512,256]{2,1,0:T(8,128)(2,1)S(1)} %copy-done.2, ...), custom_call_target="tpu_custom_call" | custom-call | flops 2147483648 | bytes 3145728 | tf_op jit(solution)/shard_map/stack_group/pallas_call | solution.py:177
  51.7 0.1 collective-permute-start.12
  51.8 1.4 %collective-permute-start.11 = (bf16[1,2,4,16,512]{4,3,2,1,0:T(8,128)(2,1)S(1)}, bf16[1,2,4,16,512]{4,3,2,1,0:T(8,128)(2,1)S(1)}, u32[]{:S(2)}, u32[]{:S(2)}) collective-permute-start(bf16[1,2,4,16,512]{4,3,2,1,0:T(8,128)(2,1)S(1)} %stack_group.5.refs_0_), channel_id=1, source_target_pairs={{0,2},{1,3},{2,0},{3,1},{4,6},{5,7},{6,4},{7,5},{8,10},{9,11},{10,... | collective-permute-start | bytes 393224 | tf_op jit(solution)/shard_map/ppermute | solution.py:241
  53.2 0.0 collective-permute-done.17
  53.2 0.8 %collective-permute-start.10 = (bf16[1,2,4,16,512]{4,3,2,1,0:T(8,128)(2,1)S(1)}, bf16[1,2,4,16,512]{4,3,2,1,0:T(8,128)(2,1)S(1)}, u32[]{:S(2)}, u32[]{:S(2)}) collective-permute-start(bf16[1,2,4,16,512]{4,3,2,1,0:T(8,128)(2,1)S(1)} %stack_group.5.refs_0_), channel_id=1, source_target_pairs={{0,1},{1,0},{2,3},{3,2},{4,5},{5,4},{6,7},{7,6},{8,9},{9,8},{10,11... | collective-permute-start | bytes 393224 | tf_op jit(solution)/shard_map/ppermute | solution.py:241
  54.0 0.0 collective-permute-done.14
  54.0 0.1 collective-permute-start.18
  54.1 0.0 collective-permute-done.20.refs_1_
  54.2 0.6 collective-permute-start.15
  54.7 0.1 pad_add_fusion.4
  54.8 0.0 copy-done
  54.8 1.9 %order_groups.4 = (f32[4,2,4,2,16,401]{5,4,3,2,1,0:T(8,128)}, f32[4,2,4,2,16,401]{5,4,3,2,1,0:T(8,128)}) custom-call(s32[3]{0:T(128)S(1)} %get-tuple-element.22.place_ref, bf16[512,512]{1,0:T(8,128)(2,1)S(1)} %copy-done, bf16[2,2,4,16,512]{4,3,2,1,0:T(8,128)(2,1)S(1)} %pad_maximum_fusion.2.refs_0_, ...), custom_call_target="tpu_custom_call" | custom-call | flops 268435456 | bytes 67108864 | tf_op jit(solution)/shard_map/order_groups/pallas_call | solution.py:224
  56.7 0.0 collective-permute-done.18.refs_1_
  56.7 1.9 %order_groups.5 = (f32[4,2,4,2,16,401]{5,4,3,2,1,0:T(8,128)}, f32[4,2,4,2,16,401]{5,4,3,2,1,0:T(8,128)}) custom-call(s32[3]{0:T(128)S(1)} %get-tuple-element.28.place_ref, bf16[512,512]{1,0:T(8,128)(2,1)S(1)} %copy-done, bf16[2,2,4,16,512]{4,3,2,1,0:T(8,128)(2,1)S(1)} %pad_maximum_fusion.1.refs_0_, ...), custom_call_target="tpu_custom_call", output_to_operand_aliasing={{0}: (4, {}), {1}: (5, {})} | custom-call | flops 268435456 | bytes 67108864 | tf_op jit(solution)/shard_map/order_groups/pallas_call | solution.py:224
  58.7 0.0 collective-permute-done.15.refs_1_
  58.7 1.9 %order_groups.6 = (f32[4,2,4,2,16,401]{5,4,3,2,1,0:T(8,128)}, f32[4,2,4,2,16,401]{5,4,3,2,1,0:T(8,128)}) custom-call(s32[3]{0:T(128)S(1)} %get-tuple-element.29.place_ref, bf16[512,512]{1,0:T(8,128)(2,1)S(1)} %copy-done, bf16[2,2,4,16,512]{4,3,2,1,0:T(8,128)(2,1)S(1)} %pad_maximum_fusion.refs_0_, ...), custom_call_target="tpu_custom_call", output_to_operand_aliasing={{0}: (4, {}), {1}: (5, {})} | custom-call | flops 268435456 | bytes 67108864 | tf_op jit(solution)/shard_map/order_groups/pallas_call | solution.py:224
  60.6 0.0 collective-permute-done.12.refs_3_
  60.6 0.0 collective-permute-done.11.refs_2_
  60.6 0.0 collective-permute-done.10.refs_1_
  60.6 1.9 %order_groups.7 = (f32[4,2,4,2,16,401]{5,4,3,2,1,0:T(8,128)}, f32[4,2,4,2,16,401]{5,4,3,2,1,0:T(8,128)}) custom-call(s32[3]{0:T(128)S(1)} %get-tuple-element.30.place_ref, bf16[512,512]{1,0:T(8,128)(2,1)S(1)} %copy-done, bf16[1,2,4,16,512]{4,3,2,1,0:T(8,128)(2,1)S(1)} %stack_group.5.refs_0_, ...), custom_call_target="tpu_custom_call", output_to_operand_aliasing={{0}: (6, {}), {1}: (7, {})} | custom-call | flops 268435456 | bytes 67108864 | tf_op jit(solution)/shard_map/order_groups/pallas_call | solution.py:224
  (14 shorter events, 0.2 us)
Async XLA Ops:
  0.6 31.0 %copy-start.1 = (bf16[512,512]{1,0:T(8,128)(2,1)S(1)}, bf16[512,512]{1,0:T(8,128)(2,1)}, u32[]{:S(2)}) copy-start(bf16[512,512]{1,0:T(8,128)(2,1)} %constant.27.clone.flip_ref) | copy-start | bytes 1572868
  1.4 14.0 %collective-permute-start.2 = (bf16[8,1024]{1,0:T(8,128)(2,1)S(1)}, bf16[8,1024]{1,0:T(8,128)(2,1)S(1)}, u32[]{:S(2)}, u32[]{:S(2)}) collective-permute-start(bf16[8,1024]{1,0:T(8,128)(2,1)S(1)} %reshape.18), channel_id=1, source_target_pairs={{0,24},{4,28},{8,16},{12,20},{16,8},{20,12},{24,0},{28,4},{32,56},... | collective-permute-start | bytes 49160 | tf_op jit(solution)/shard_map/ppermute | solution.py:245
  8.4 7.0 %collective-permute-start.1 = (bf16[8,1024]{1,0:T(8,128)(2,1)S(1)}, bf16[8,1024]{1,0:T(8,128)(2,1)S(1)}, u32[]{:S(2)}, u32[]{:S(2)}) collective-permute-start(bf16[8,1024]{1,0:T(8,128)(2,1)S(1)} %reshape.18), channel_id=1, source_target_pairs={{0,16},{4,20},{8,24},{12,28},{16,0},{20,4},{24,8},{28,12},{32,48},... | collective-permute-start | bytes 49160 | tf_op jit(solution)/shard_map/ppermute | solution.py:245
  9.4 6.1 %collective-permute-start = (bf16[8,1024]{1,0:T(8,128)(2,1)S(1)}, bf16[8,1024]{1,0:T(8,128)(2,1)S(1)}, u32[]{:S(2)}, u32[]{:S(2)}) collective-permute-start(bf16[8,1024]{1,0:T(8,128)(2,1)S(1)} %reshape.18), channel_id=1, source_target_pairs={{0,8},{4,12},{8,0},{12,4},{16,24},{20,28},{24,16},{28,20},{32,40},... | collective-permute-start | bytes 49160 | tf_op jit(solution)/shard_map/ppermute | solution.py:245
  11.3 21.5 %copy-start.2 = (bf16[2,512,256]{2,1,0:T(8,128)(2,1)S(1)}, bf16[2,512,256]{2,1,0:T(8,128)(2,1)}, u32[]{:S(2)}) copy-start(bf16[2,512,256]{2,1,0:T(8,128)(2,1)} %constant.26.clone.basis_ref) | copy-start | bytes 1572868
  12.6 11.6 %collective-permute-start.8 = (bf16[144,1024]{1,0:T(8,128)(2,1)S(1)}, bf16[144,1024]{1,0:T(8,128)(2,1)S(1)}, u32[]{:S(2)}, u32[]{:S(2)}) collective-permute-start(bf16[144,1024]{1,0:T(8,128)(2,1)S(1)} %fusion.1.rec0), channel_id=1, source_target_pairs={{0,2},{1,3},{2,0},{3,1},{4,6},{5,7},{6,4},{7,5},{8,10},{9,11},{10,... | collective-permute-start | bytes 884744 | tf_op jit(solution)/shard_map/ppermute | solution.py:241
  13.9 17.7 %collective-permute-start.7 = (bf16[144,1024]{1,0:T(8,128)(2,1)S(1)}, bf16[144,1024]{1,0:T(8,128)(2,1)S(1)}, u32[]{:S(2)}, u32[]{:S(2)}) collective-permute-start(bf16[144,1024]{1,0:T(8,128)(2,1)S(1)} %fusion.1.rec0), channel_id=1, source_target_pairs={{0,1},{1,0},{2,3},{3,2},{4,5},{5,4},{6,7},{7,6},{8,9},{9,8},{10,11... | collective-permute-start | bytes 884744 | tf_op jit(solution)/shard_map/ppermute | solution.py:241
  15.4 2.5 %collective-permute-start.3 = (bf16[32,1024]{1,0:T(8,128)(2,1)S(1)}, bf16[32,1024]{1,0:T(8,128)(2,1)S(1)}, u32[]{:S(2)}, u32[]{:S(2)}) collective-permute-start(bf16[32,1024]{1,0:T(8,128)(2,1)S(1)} %pad_maximum_fusion.3), channel_id=1, source_target_pairs={{0,1},{1,0},{2,3},{3,2},{4,5},{5,4},{6,7},{7,6},{8,9},{9,8},{10,11... | collective-permute-start | bytes 196616 | tf_op jit(solution)/shard_map/ppermute | solution.py:241
  18.0 6.6 %collective-permute-start.4 = (bf16[64,1024]{1,0:T(8,128)(2,1)S(1)}, bf16[64,1024]{1,0:T(8,128)(2,1)S(1)}, u32[]{:S(2)}, u32[]{:S(2)}) collective-permute-start(bf16[64,1024]{1,0:T(8,128)(2,1)S(1)} %constant_dynamic-update-slice_fusion), channel_id=1, source_target_pairs={{0,0},{1,4},{2,32},{3,36},{4,1},{5,5},{6,33},{7,37},{8,8},{9,12},{... | collective-permute-start | bytes 393224 | tf_op jit(solution)/shard_map/ppermute | solution.py:255
  20.9 6.6 %collective-permute-start.5 = (bf16[64,1024]{1,0:T(8,128)(2,1)S(1)}, bf16[64,1024]{1,0:T(8,128)(2,1)S(1)}, u32[]{:S(2)}, u32[]{:S(2)}) collective-permute-start(bf16[64,1024]{1,0:T(8,128)(2,1)S(1)} %constant_dynamic-update-slice_fusion), channel_id=1, source_target_pairs={{0,32},{1,36},{2,0},{3,4},{4,33},{5,37},{6,1},{7,5},{8,40},{9,44},... | collective-permute-start | bytes 393224 | tf_op jit(solution)/shard_map/ppermute | solution.py:255
  24.2 7.4 %collective-permute-start.9 = (bf16[144,1024]{1,0:T(8,128)(2,1)S(1)}, bf16[144,1024]{1,0:T(8,128)(2,1)S(1)}, u32[]{:S(2)}, u32[]{:S(2)}) collective-permute-start(bf16[144,1024]{1,0:T(8,128)(2,1)S(1)} %collective-permute-done.8.rec2), channel_id=1, source_target_pairs={{0,1},{1,0},{2,3},{3,2},{4,5},{5,4},{6,7},{7,6},{8,9},{9,8},{10,11... | collective-permute-start | bytes 884744 | tf_op jit(solution)/shard_map/ppermute | solution.py:241
  27.6 10.8 %collective-permute-start.16 = (bf16[128,1024]{1,0:T(8,128)(2,1)S(1)}, bf16[128,1024]{1,0:T(8,128)(2,1)S(1)}, u32[]{:S(2)}, u32[]{:S(2)}) collective-permute-start(bf16[128,1024]{1,0:T(8,128)(2,1)S(1)} %constant_dynamic-update-slice_fusion.5.src_ref), channel_id=1, source_target_pairs={{0,64},{4,68},{8,72},{12,76},{16,80},{20,84},{24,88},{28,92},{32,9... | collective-permute-start | bytes 786440 | tf_op jit(solution)/shard_map/ppermute | solution.py:245
  29.0 12.5 %collective-permute-start.13 = (bf16[128,1024]{1,0:T(8,128)(2,1)S(1)}, bf16[128,1024]{1,0:T(8,128)(2,1)S(1)}, u32[]{:S(2)}, u32[]{:S(2)}) collective-permute-start(bf16[128,1024]{1,0:T(8,128)(2,1)S(1)} %constant_dynamic-update-slice_fusion.5.src_ref), channel_id=1, source_target_pairs={{0,192},{4,196},{8,200},{12,204},{16,208},{20,212},{24,216},{28,22... | collective-permute-start | bytes 786440 | tf_op jit(solution)/shard_map/ppermute | solution.py:245
  30.9 18.0 %collective-permute-start.6 = (bf16[128,1024]{1,0:T(8,128)(2,1)S(1)}, bf16[128,1024]{1,0:T(8,128)(2,1)S(1)}, u32[]{:S(2)}, u32[]{:S(2)}) collective-permute-start(bf16[128,1024]{1,0:T(8,128)(2,1)S(1)} %constant_dynamic-update-slice_fusion.5.src_ref), channel_id=1, source_target_pairs={{0,128},{4,132},{8,136},{12,140},{16,144},{20,148},{24,152},{28,15... | collective-permute-start | bytes 786440 | tf_op jit(solution)/shard_map/ppermute | solution.py:245
  35.7 10.2 %collective-permute-start.19 = (bf16[1,2,4,16,512]{4,3,2,1,0:T(8,128)(2,1)S(1)}, bf16[1,2,4,16,512]{4,3,2,1,0:T(8,128)(2,1)S(1)}, u32[]{:S(2)}, u32[]{:S(2)}) collective-permute-start(bf16[1,2,4,16,512]{4,3,2,1,0:T(8,128)(2,1)S(1)} %stack_group.4.refs_0_), channel_id=1, source_target_pairs={{0,2},{1,3},{2,0},{3,1},{4,6},{5,7},{6,4},{7,5},{8,10},{9,11},{10,... | collective-permute-start | bytes 393224 | tf_op jit(solution)/shard_map/ppermute | solution.py:241
  41.3 11.9 %collective-permute-start.17 = (bf16[1,2,4,16,512]{4,3,2,1,0:T(8,128)(2,1)S(1)}, bf16[1,2,4,16,512]{4,3,2,1,0:T(8,128)(2,1)S(1)}, u32[]{:S(2)}, u32[]{:S(2)}) collective-permute-start(bf16[1,2,4,16,512]{4,3,2,1,0:T(8,128)(2,1)S(1)} %stack_group.7), channel_id=1, source_target_pairs={{0,2},{1,3},{2,0},{3,1},{4,6},{5,7},{6,4},{7,5},{8,10},{9,11},{10,... | collective-permute-start | bytes 393224 | tf_op jit(solution)/shard_map/ppermute | solution.py:241
  44.4 9.7 %collective-permute-start.14 = (bf16[1,2,4,16,512]{4,3,2,1,0:T(8,128)(2,1)S(1)}, bf16[1,2,4,16,512]{4,3,2,1,0:T(8,128)(2,1)S(1)}, u32[]{:S(2)}, u32[]{:S(2)}) collective-permute-start(bf16[1,2,4,16,512]{4,3,2,1,0:T(8,128)(2,1)S(1)} %stack_group.6), channel_id=1, source_target_pairs={{0,2},{1,3},{2,0},{3,1},{4,6},{5,7},{6,4},{7,5},{8,10},{9,11},{10,... | collective-permute-start | bytes 393224 | tf_op jit(solution)/shard_map/ppermute | solution.py:241
  45.9 8.2 %collective-permute-start.20 = (bf16[2,2,4,16,512]{4,3,2,1,0:T(8,128)(2,1)S(1)}, bf16[2,2,4,16,512]{4,3,2,1,0:T(8,128)(2,1)S(1)}, u32[]{:S(2)}, u32[]{:S(2)}) collective-permute-start(bf16[2,2,4,16,512]{4,3,2,1,0:T(8,128)(2,1)S(1)} %pad_maximum_fusion.2.refs_0_), channel_id=1, source_target_pairs={{0,1},{1,0},{2,3},{3,2},{4,5},{5,4},{6,7},{7,6},{8,9},{9,8},{10,11... | collective-permute-start | bytes 786440 | tf_op jit(solution)/shard_map/ppermute | solution.py:241
  48.8 6.0 %copy-start = (bf16[512,512]{1,0:T(8,128)(2,1)S(1)}, bf16[512,512]{1,0:T(8,128)(2,1)}, u32[]{:S(2)}) copy-start(bf16[512,512]{1,0:T(8,128)(2,1)} %constant.28.clone.order_ref) | copy-start | bytes 1572868
  51.7 8.9 %collective-permute-start.12 = (bf16[1,2,4,16,512]{4,3,2,1,0:T(8,128)(2,1)S(1)}, bf16[1,2,4,16,512]{4,3,2,1,0:T(8,128)(2,1)S(1)}, u32[]{:S(2)}, u32[]{:S(2)}) collective-permute-start(bf16[1,2,4,16,512]{4,3,2,1,0:T(8,128)(2,1)S(1)} %stack_group.5.refs_0_), channel_id=1, source_target_pairs={{0,3},{1,2},{2,1},{3,0},{4,7},{5,6},{6,5},{7,4},{8,11},{9,10},{10,... | collective-permute-start | bytes 393224 | tf_op jit(solution)/shard_map/ppermute | solution.py:241
  51.8 8.8 %collective-permute-start.11 = (bf16[1,2,4,16,512]{4,3,2,1,0:T(8,128)(2,1)S(1)}, bf16[1,2,4,16,512]{4,3,2,1,0:T(8,128)(2,1)S(1)}, u32[]{:S(2)}, u32[]{:S(2)}) collective-permute-start(bf16[1,2,4,16,512]{4,3,2,1,0:T(8,128)(2,1)S(1)} %stack_group.5.refs_0_), channel_id=1, source_target_pairs={{0,2},{1,3},{2,0},{3,1},{4,6},{5,7},{6,4},{7,5},{8,10},{9,11},{10,... | collective-permute-start | bytes 393224 | tf_op jit(solution)/shard_map/ppermute | solution.py:241
  53.2 7.4 %collective-permute-start.10 = (bf16[1,2,4,16,512]{4,3,2,1,0:T(8,128)(2,1)S(1)}, bf16[1,2,4,16,512]{4,3,2,1,0:T(8,128)(2,1)S(1)}, u32[]{:S(2)}, u32[]{:S(2)}) collective-permute-start(bf16[1,2,4,16,512]{4,3,2,1,0:T(8,128)(2,1)S(1)} %stack_group.5.refs_0_), channel_id=1, source_target_pairs={{0,1},{1,0},{2,3},{3,2},{4,5},{5,4},{6,7},{7,6},{8,9},{9,8},{10,11... | collective-permute-start | bytes 393224 | tf_op jit(solution)/shard_map/ppermute | solution.py:241
  54.0 2.7 %collective-permute-start.18 = (bf16[2,2,4,16,512]{4,3,2,1,0:T(8,128)(2,1)S(1)}, bf16[2,2,4,16,512]{4,3,2,1,0:T(8,128)(2,1)S(1)}, u32[]{:S(2)}, u32[]{:S(2)}) collective-permute-start(bf16[2,2,4,16,512]{4,3,2,1,0:T(8,128)(2,1)S(1)} %pad_maximum_fusion.1.refs_0_), channel_id=1, source_target_pairs={{0,1},{1,0},{2,3},{3,2},{4,5},{5,4},{6,7},{7,6},{8,9},{9,8},{10,11... | collective-permute-start | bytes 786440 | tf_op jit(solution)/shard_map/ppermute | solution.py:241
  54.2 4.5 %collective-permute-start.15 = (bf16[2,2,4,16,512]{4,3,2,1,0:T(8,128)(2,1)S(1)}, bf16[2,2,4,16,512]{4,3,2,1,0:T(8,128)(2,1)S(1)}, u32[]{:S(2)}, u32[]{:S(2)}) collective-permute-start(bf16[2,2,4,16,512]{4,3,2,1,0:T(8,128)(2,1)S(1)} %pad_maximum_fusion.refs_0_), channel_id=1, source_target_pairs={{0,1},{1,0},{2,3},{3,2},{4,5},{5,4},{6,7},{7,6},{8,9},{9,8},{10,11... | collective-permute-start | bytes 786440 | tf_op jit(solution)/shard_map/ppermute | solution.py:241
